TPU v7x, 128 devices: a whole 4x4x4 slice. The times are simulated.
128 devices in a mesh: dp: 8 (over y, z_lo), axial: 16 (over x, z_hi, core).
Axes of the slice: x: 4, y: 4, z: 4 (z_hi: 2, z_lo: 2; z = z_hi * 2 + z_lo), core: 2. Of those that a mesh axis runs over, the one named last changes fastest.
Arguments:
- single_state: bfloat16 [8, 256, 1024], P('dp', 'axial'), may hold values from -6 to 6
- pair_state: bfloat16 [8, 256, 256, 128], P('dp', 'axial'), may hold values from -6 to 6
- residue_mask: int32 [8, 256], P('dp'), may hold values from 0 to 1, as said below
- pair_cotangent: bfloat16 [8, 256, 256, 128], P('dp', 'axial'), may hold values from -6 to 6
- outer_norm_gain: float32 [1024], replicated, may hold values from 0.5 to 1.5
- outer_norm_bias: float32 [1024], replicated, may hold values from -1.5 to 1.5
- outer_left: bfloat16 [1024, 32], replicated, may hold values from -0.1875 to 0.1875
- outer_right: bfloat16 [1024, 32], replicated, may hold values from -0.1875 to 0.1875
- outer_proj: bfloat16 [1024, 128], replicated, may hold values from -0.1875 to 0.1875
- outer_bias: float32 [128], replicated, may hold values from -1.5 to 1.5
- triangle_norm_gain: float32 [2, 128], replicated, may hold values from 0.5 to 1.5
- triangle_norm_bias: float32 [2, 128], replicated, may hold values from -1.5 to 1.5
- triangle_proj: bfloat16 [2, 128, 512], replicated, may hold values from -0.5 to 0.5
- triangle_gate: bfloat16 [2, 128, 128], replicated, may hold values from -0.5 to 0.5
- triangle_out_gain: float32 [2, 128], replicated, may hold values from 0.5 to 1.5
- triangle_out_bias: float32 [2, 128], replicated, may hold values from -1.5 to 1.5
- triangle_out: bfloat16 [2, 128, 128], replicated, may hold values from -0.5 to 0.5
Outputs:
- single_gradient: bfloat16 [8, 256, 1024], P('dp', 'axial')
- pair_gradient: bfloat16 [8, 256, 256, 128], P('dp', 'axial')
- outer_norm_gain_gradient: float32 [1024], replicated
- outer_norm_bias_gradient: float32 [1024], replicated
- outer_left_gradient: float32 [1024, 32], replicated
- outer_right_gradient: float32 [1024, 32], replicated
- outer_proj_gradient: float32 [1024, 128], replicated
- outer_bias_gradient: float32 [128], replicated
- triangle_norm_gain_gradient: float32 [2, 128], replicated
- triangle_norm_bias_gradient: float32 [2, 128], replicated
- triangle_proj_gradient: float32 [2, 128, 512], replicated
- triangle_gate_gradient: float32 [2, 128, 128], replicated
- triangle_out_gain_gradient: float32 [2, 128], replicated
- triangle_out_bias_gradient: float32 [2, 128], replicated
- triangle_out_gradient: float32 [2, 128, 128], replicated
Inputs may be any that keep to these rules, and one draw needn't show every extreme that they name: `residue_mask`: in each protein the ones form a prefix of at least 128 residues, and at least the last residue is 0.
All inputs are finite; a program needn't handle non-finite values.
Results may differ from a plain program's by a relative error of at most 0.023.
Values may be sent and summed in bfloat16 or wider, within the bound.
A program may use at most 320 MiB of HBM per device.

v0:
```python
import jax
import jax.numpy as jnp
from jax import lax
from jax.sharding import PartitionSpec as P

EPSILON = 1e-05
HIGHEST = lax.Precision.HIGHEST


def norm_forward(values, weight_gain, weight_bias):
    average = jnp.mean(values, axis=-1, keepdims=True)
    centred = values - average
    variance = jnp.mean(centred * centred, axis=-1, keepdims=True)
    inverse = lax.rsqrt(variance + EPSILON)
    standard = centred * inverse
    return (standard * weight_gain + weight_bias, standard, inverse)


def norm_backward(cotangent, standard, inverse, weight_gain):
    scaled = cotangent * weight_gain
    centred = scaled - jnp.mean(scaled, axis=-1, keepdims=True)
    return inverse * (centred - standard * jnp.mean(scaled * standard, axis=-1, keepdims=True))


def project(inputs, matrix):
    return jnp.einsum("...c,cd->...d", inputs, matrix, preferred_element_type=jnp.float32)


def project_back(inputs, matrix):
    return jnp.einsum("...d,cd->...c", inputs, matrix, preferred_element_type=jnp.float32)


def cell_sum(first_factor, second_factor):
    return jnp.einsum(
        "ijc,ijd->cd", first_factor, second_factor, preferred_element_type=jnp.float32
    )


def row_sum(first_factor, second_factor):
    return jnp.einsum("ic,id->cd", first_factor, second_factor, preferred_element_type=jnp.float32)


def triangle_front(pair_in, pair_mask, weight_gain, weight_bias, proj_weight, gate_weight):
    normed, standard, inverse = norm_forward(pair_in.astype(jnp.float32), weight_gain, weight_bias)
    normed = normed.astype(jnp.bfloat16)
    projected = project(normed, proj_weight)
    hidden = projected.shape[-1] // 4
    left_side = (
        pair_mask * jax.nn.sigmoid(projected[..., :hidden]) * projected[..., hidden : 2 * hidden]
    ).astype(jnp.bfloat16)
    right_side = (
        pair_mask
        * jax.nn.sigmoid(projected[..., 2 * hidden : 3 * hidden])
        * projected[..., 3 * hidden :]
    ).astype(jnp.bfloat16)
    gate_value = jax.nn.sigmoid(project(normed, gate_weight))
    return (normed, standard, inverse, projected, gate_value, left_side, right_side)


def triangle_finish(product, out_gain, out_bias, out_weight):
    product_norm, product_standard, product_inverse = norm_forward(product, out_gain, out_bias)
    product_norm = product_norm.astype(jnp.bfloat16)
    linear_out = project(product_norm, out_weight)
    return (product_norm, product_standard, product_inverse, linear_out)


def triangle_grad_out(
    cotangent,
    gate_value,
    linear_out,
    product_norm,
    product_standard,
    product_inverse,
    out_gain,
    out_weight,
):
    linear_grad = (cotangent * gate_value).astype(jnp.bfloat16)
    gate_grad = (cotangent * linear_out * gate_value * (1.0 - gate_value)).astype(jnp.bfloat16)
    out_weight_sum = cell_sum(product_norm, linear_grad)
    norm_grad = project_back(linear_grad, out_weight)
    out_gain_sum = jnp.sum(norm_grad * product_standard, axis=(0, 1))
    out_bias_sum = jnp.sum(norm_grad, axis=(0, 1))
    product_grad = norm_backward(norm_grad, product_standard, product_inverse, out_gain).astype(
        jnp.bfloat16
    )
    return (gate_grad, product_grad, (out_gain_sum, out_bias_sum, out_weight_sum))


def triangle_grad_in(
    cotangent,
    gate_grad,
    left_grad,
    right_grad,
    projected,
    pair_mask,
    normed,
    standard,
    inverse,
    weight_gain,
    proj_weight,
    gate_weight,
):
    hidden = projected.shape[-1] // 4
    left_gate = jax.nn.sigmoid(projected[..., :hidden])
    right_gate = jax.nn.sigmoid(projected[..., 2 * hidden : 3 * hidden])
    left_masked = left_grad * pair_mask
    right_masked = right_grad * pair_mask
    proj_grad = jnp.concatenate(
        [
            left_masked * projected[..., hidden : 2 * hidden] * left_gate * (1.0 - left_gate),
            left_masked * left_gate,
            right_masked * projected[..., 3 * hidden :] * right_gate * (1.0 - right_gate),
            right_masked * right_gate,
        ],
        axis=-1,
    ).astype(jnp.bfloat16)
    proj_sum = cell_sum(normed, proj_grad)
    gate_sum = cell_sum(normed, gate_grad)
    normed_grad = project_back(proj_grad, proj_weight) + project_back(gate_grad, gate_weight)
    gain_sum = jnp.sum(normed_grad * standard, axis=(0, 1))
    bias_sum = jnp.sum(normed_grad, axis=(0, 1))
    input_grad = (cotangent + norm_backward(normed_grad, standard, inverse, weight_gain)).astype(
        jnp.bfloat16
    )
    return (input_grad, (gain_sum, bias_sum, proj_sum, gate_sum))


def core_forward(left_side, right_side, incoming):
    left_cells, right_cells = (
        lax.all_to_all(left_side, "axial", split_axis=2, concat_axis=0, tiled=True),
        lax.all_to_all(right_side, "axial", split_axis=2, concat_axis=0, tiled=True),
    )
    if incoming:
        partial_product = jnp.einsum(
            "kic,kjc->ijc", left_cells, right_cells, preferred_element_type=jnp.float32
        )
    else:
        partial_product = jnp.einsum(
            "ikc,jkc->ijc", left_cells, right_cells, preferred_element_type=jnp.float32
        )
    product = lax.all_to_all(
        partial_product.astype(jnp.bfloat16), "axial", split_axis=0, concat_axis=2, tiled=True
    ).astype(partial_product.dtype)
    return (product, (left_cells, right_cells))


def core_backward(product_grad, kept_core, incoming):
    first_kept, second_kept = kept_core
    grad_cells = lax.all_to_all(product_grad, "axial", split_axis=2, concat_axis=0, tiled=True)
    if incoming:
        left_part = jnp.einsum(
            "ijc,kjc->kic", grad_cells, second_kept, preferred_element_type=jnp.float32
        )
        right_part = jnp.einsum(
            "kic,ijc->kjc", first_kept, grad_cells, preferred_element_type=jnp.float32
        )
    else:
        left_part = jnp.einsum(
            "ijc,jkc->ikc", grad_cells, second_kept, preferred_element_type=jnp.float32
        )
        right_part = jnp.einsum(
            "ijc,ikc->jkc", grad_cells, first_kept, preferred_element_type=jnp.float32
        )
    left_grad, right_grad = (
        lax.all_to_all(
            left_part.astype(jnp.bfloat16), "axial", split_axis=0, concat_axis=2, tiled=True
        ).astype(left_part.dtype),
        lax.all_to_all(
            right_part.astype(jnp.bfloat16), "axial", split_axis=0, concat_axis=2, tiled=True
        ).astype(right_part.dtype),
    )
    return (left_grad, right_grad)


def triangle_forward(pair_in, pair_mask, params, incoming):
    weight_gain, weight_bias, proj_weight, gate_weight, out_gain, out_bias, out_weight = params
    normed, standard, inverse, projected, gate_value, left_side, right_side = triangle_front(
        pair_in, pair_mask, weight_gain, weight_bias, proj_weight, gate_weight
    )
    product, kept_core = core_forward(left_side, right_side, incoming)
    product_norm, product_standard, product_inverse, linear_out = triangle_finish(
        product, out_gain, out_bias, out_weight
    )
    pair_out = (pair_in.astype(jnp.float32) + gate_value * linear_out).astype(jnp.bfloat16)
    kept = (
        normed,
        standard,
        inverse,
        projected,
        gate_value,
        kept_core,
        product_norm,
        product_standard,
        product_inverse,
        linear_out,
    )
    return (pair_out, kept)


def triangle_backward(pair_grad, kept, pair_mask, params, incoming):
    weight_gain, weight_bias, proj_weight, gate_weight, out_gain, out_bias, out_weight = params
    (
        normed,
        standard,
        inverse,
        projected,
        gate_value,
        kept_core,
        product_norm,
        product_standard,
        product_inverse,
        linear_out,
    ) = kept
    cotangent = pair_grad.astype(jnp.float32)
    gate_grad, product_grad, out_sums = triangle_grad_out(
        cotangent,
        gate_value,
        linear_out,
        product_norm,
        product_standard,
        product_inverse,
        out_gain,
        out_weight,
    )
    left_grad, right_grad = core_backward(product_grad, kept_core, incoming)
    input_grad, in_sums = triangle_grad_in(
        cotangent,
        gate_grad,
        left_grad,
        right_grad,
        projected,
        pair_mask,
        normed,
        standard,
        inverse,
        weight_gain,
        proj_weight,
        gate_weight,
    )
    return (input_grad, in_sums + out_sums)


def local(
    single_state,
    pair_state,
    residue_mask,
    pair_cotangent,
    outer_norm_gain,
    outer_norm_bias,
    outer_left,
    outer_right,
    outer_proj,
    outer_bias,
    triangle_norm_gain,
    triangle_norm_bias,
    triangle_proj,
    triangle_gate,
    triangle_out_gain,
    triangle_out_bias,
    triangle_out,
):
    row_count = pair_state.shape[1]
    column_count = pair_state.shape[2]
    residue_weight = residue_mask[0].astype(jnp.float32)
    own_weight = lax.dynamic_slice_in_dim(
        residue_weight, lax.axis_index("axial") * row_count, row_count
    )
    pair_mask = (own_weight[:, None] * residue_weight[None, :])[:, :, None]
    single_norm, single_standard, single_inverse = norm_forward(
        single_state[0].astype(jnp.float32), outer_norm_gain, outer_norm_bias
    )
    single_norm = single_norm.astype(jnp.bfloat16)
    left_outer = (
        jnp.dot(single_norm, outer_left, preferred_element_type=jnp.float32) * own_weight[:, None]
    ).astype(jnp.bfloat16)
    right_outer = (
        jnp.dot(single_norm, outer_right, preferred_element_type=jnp.float32) * own_weight[:, None]
    ).astype(jnp.bfloat16)
    right_every = lax.all_gather(right_outer, "axial", axis=0, tiled=True)
    inner_width = outer_left.shape[1]
    outer_cube = outer_proj.reshape(inner_width, inner_width, -1)
    mixed = jnp.einsum(
        "jb,abc->jac", right_every, outer_cube, preferred_element_type=jnp.float32
    ).astype(jnp.bfloat16)
    outer_term = (
        jnp.einsum("ia,jac->ijc", left_outer, mixed, preferred_element_type=jnp.float32)
        + outer_bias
    )
    pair_first = (pair_state[0].astype(jnp.float32) + pair_mask * outer_term).astype(jnp.bfloat16)
    triangle_weights = (
        triangle_norm_gain,
        triangle_norm_bias,
        triangle_proj,
        triangle_gate,
        triangle_out_gain,
        triangle_out_bias,
        triangle_out,
    )
    params_out = tuple((member[0] for member in triangle_weights))
    params_in = tuple((member[1] for member in triangle_weights))
    pair_second, kept_out = triangle_forward(pair_first, pair_mask, params_out, False)
    unused_pair, kept_in = triangle_forward(pair_second, pair_mask, params_in, True)
    grad_second, sums_in = triangle_backward(pair_cotangent[0], kept_in, pair_mask, params_in, True)
    grad_first, sums_out = triangle_backward(grad_second, kept_out, pair_mask, params_out, False)
    outer_grad = (grad_first.astype(jnp.float32) * pair_mask).astype(jnp.bfloat16)
    outer_bias_sum = jnp.sum(outer_grad.astype(jnp.float32), axis=(0, 1))
    left_grad = (
        jnp.einsum("ijc,jac->ia", outer_grad, mixed, preferred_element_type=jnp.float32)
        * own_weight[:, None]
    ).astype(jnp.bfloat16)
    cube_values = outer_cube.astype(jnp.float32)
    mixed_own = lax.psum_scatter(
        jnp.einsum(
            "ia,ijc->jac", left_outer, outer_grad, preferred_element_type=jnp.float32
        ).astype(jnp.bfloat16),
        "axial",
        scatter_dimension=0,
        tiled=True,
    ).astype(jnp.float32)
    right_total = jnp.einsum("jac,abc->jb", mixed_own, cube_values, precision=HIGHEST)
    cube_sum = jnp.einsum(
        "jb,jac->abc", right_outer.astype(jnp.float32), mixed_own, precision=HIGHEST
    )
    right_grad = (right_total * own_weight[:, None]).astype(jnp.bfloat16)
    left_sum = row_sum(single_norm, left_grad)
    right_sum = row_sum(single_norm, right_grad)
    single_grad = project_back(left_grad, outer_left) + project_back(right_grad, outer_right)
    gain_sum = jnp.sum(single_grad * single_standard, axis=0)
    bias_sum = jnp.sum(single_grad, axis=0)
    single_gradient = norm_backward(
        single_grad, single_standard, single_inverse, outer_norm_gain
    ).astype(jnp.bfloat16)
    stacked = tuple(
        (jnp.stack([first_sum, second_sum]) for first_sum, second_sum in zip(sums_out, sums_in))
    )
    totals = lax.psum(
        (
            gain_sum,
            bias_sum,
            left_sum,
            right_sum,
            cube_sum.reshape(inner_width * inner_width, -1),
            outer_bias_sum,
            stacked[0],
            stacked[1],
            stacked[2],
            stacked[3],
            stacked[4],
            stacked[5],
            stacked[6],
        ),
        ("dp", "axial"),
    )
    divisor = 1.0 / float(lax.axis_size("dp") * column_count)
    return (
        single_gradient[None],
        grad_first[None],
        totals[0] * divisor,
        totals[1] * divisor,
        totals[2] * divisor,
        totals[3] * divisor,
        totals[4] * divisor,
        totals[5] * divisor,
        totals[6] * divisor,
        totals[7] * divisor,
        totals[8] * divisor,
        totals[9] * divisor,
        totals[10] * divisor,
        totals[11] * divisor,
        totals[12] * divisor,
    )


def solution(mesh):
    return jax.shard_map(
        local,
        mesh=mesh,
        in_specs=(
            P("dp", "axial", None),
            P("dp", "axial", None, None),
            P("dp", None),
            P("dp", "axial", None, None),
            P(),
            P(),
            P(),
            P(),
            P(),
            P(),
            P(),
            P(),
            P(),
            P(),
            P(),
            P(),
            P(),
        ),
        out_specs=(
            P("dp", "axial", None),
            P("dp", "axial", None, None),
            P(),
            P(),
            P(),
            P(),
            P(),
            P(),
            P(),
            P(),
            P(),
            P(),
            P(),
            P(),
            P(),
        ),
        check_vma=False,
    )
```

profile of v0, /device:TPU:1, one launch (start us, length us, event | category | flops | bytes accessed | tf_op | source)
XLA Modules:
  0.0 767.9 jit_solution(13440710947189199892)
XLA Ops:
  12.2 26.5 %all_gather.3 = bf16[256,32]{1,0:T(8,128)(2,1)S(1)} all-gather(bf16[16,32]{1,0:T(8,128)(2,1)S(1)} %fusion.75), channel_id=1, replica_groups=mesh['dp'=8,'axial'=16] {'axial'}, dimensions={0}, use_global_device_ids=true | all-gather | bytes 17408 | tf_op jit(solution)/shard_map/all_gather | solution.py:279
  39.5 7.1 convert_reduce_fusion
  61.8 15.2 %all-to-all-done = bf16[16,256,128]{1,0,2:T(8,128)(2,1)S(1)} async-done(((bf16[16,256,128]{1,0,2:T(8,128)(2,1)}), bf16[16,256,128]{1,0,2:T(8,128)(2,1)S(1)}, u32[]{:S(2)}, u32[]{:S(2)}) %all-to-all-start) | async-done | bytes 1048608 | tf_op jit(solution)/shard_map/all_to_all | solution.py:131
  77.0 4.9 all-to-all-start.1
  82.1 17.3 %all-to-all-done.1 = bf16[16,256,128]{1,0,2:T(8,128)(2,1)} async-done(((bf16[16,256,128]{1,0,2:T(8,128)(2,1)}), bf16[16,256,128]{1,0,2:T(8,128)(2,1)}, u32[]{:S(2)}, u32[]{:S(2)}) %all-to-all-start.1) | async-done | bytes 1048608 | tf_op jit(solution)/shard_map/all_to_all | solution.py:130
  104.0 4.7 all-to-all-start.2
  110.0 15.9 %all-to-all-done.2 = bf16[256,256,8]{1,2,0:T(8,128)(2,1)S(1)} async-done(((bf16[256,256,8]{1,2,0:T(8,128)(2,1)}), bf16[256,256,8]{1,2,0:T(8,128)(2,1)S(1)}, u32[]{:S(2)}, u32[]{:S(2)}) %all-to-all-start.2) | async-done | bytes 1048608 | tf_op jit(solution)/shard_map/all_to_all | solution.py:141
  156.9 4.3 all-to-all-start.3
  164.2 14.3 %all-to-all-done.3 = bf16[16,256,128]{1,0,2:T(8,128)(2,1)S(1)} async-done(((bf16[16,256,128]{1,0,2:T(8,128)(2,1)}), bf16[16,256,128]{1,0,2:T(8,128)(2,1)S(1)}, u32[]{:S(2)}, u32[]{:S(2)}) %all-to-all-start.3) | async-done | bytes 1048608 | tf_op jit(solution)/shard_map/all_to_all | solution.py:131
  178.5 4.9 all-to-all-start.4
  185.1 15.7 %all-to-all-done.4 = bf16[16,256,128]{1,0,2:T(8,128)(2,1)} async-done(((bf16[16,256,128]{1,0,2:T(8,128)(2,1)}), bf16[16,256,128]{1,0,2:T(8,128)(2,1)}, u32[]{:S(2)}, u32[]{:S(2)}) %all-to-all-start.4) | async-done | bytes 1048608 | tf_op jit(solution)/shard_map/all_to_all | solution.py:130
  207.3 4.3 all-to-all-start.5
  215.6 13.2 %all-to-all-done.5 = bf16[256,256,8]{1,2,0:T(8,128)(2,1)S(1)} async-done(((bf16[256,256,8]{1,2,0:T(8,128)(2,1)}), bf16[256,256,8]{1,2,0:T(8,128)(2,1)S(1)}, u32[]{:S(2)}, u32[]{:S(2)}) %all-to-all-start.5) | async-done | bytes 1048608 | tf_op jit(solution)/shard_map/all_to_all | solution.py:141
  235.1 4.6 multiply_reduce_fusion
  245.7 21.2 %all_to_all.162 = bf16[16,256,128]{1,0,2:T(8,128)(2,1)S(1)} all-to-all(bf16[16,256,128]{1,0,2:T(8,128)(2,1)} %copy.558), channel_id=1, replica_groups=mesh['dp'=8,'axial'=16] {'axial'}, dimensions={2} | all-to-all | bytes 2097152 | tf_op jit(solution)/shard_map/all_to_all | solution.py:149
  269.5 5.4 all-to-all-start.7
  283.3 9.1 %all-to-all-done.7 = bf16[256,256,8]{1,2,0:T(8,128)(2,1)} async-done(((bf16[256,256,8]{1,2,0:T(8,128)(2,1)}), bf16[256,256,8]{1,2,0:T(8,128)(2,1)}, u32[]{:S(2)}, u32[]{:S(2)}) %all-to-all-start.7) | async-done | bytes 1048608 | tf_op jit(solution)/shard_map/all_to_all | solution.py:165
  292.4 13.1 %all-to-all-start.8 = ((bf16[256,256,8]{1,2,0:T(8,128)(2,1)}), bf16[256,256,8]{1,2,0:T(8,128)(2,1)}, u32[]{:S(2)}, u32[]{:S(2)}) async-start(bf16[256,256,8]{1,2,0:T(8,128)(2,1)} %copy.566), calls=%async_computation.8 | async-start | bytes 2097152 | tf_op jit(solution)/shard_map/all_to_all | solution.py:168
  326.1 5.7 multiply_convert_fusion.9
  334.9 4.2 fusion.24
  347.9 8.4 %fusion.30 = (bf16[16,256,128]{2,0,1:T(8,128)(2,1)}, bf16[16,256,128]{2,0,1:T(8,128)(2,1)S(1)}) fusion(f32[16,256,128]{2,0,1:T(8,128)} %get-tuple-element.176, f32[16,256,128]{2,0,1:T(8,128)} %copy-done.18, f32[16,256]{0,1:T(8,128)} %copy.579, f32[16,256]{0,1:T(8,128)} %copy.537, bf16[16,256,128]{2,0,1:T(8,128)(2,1)S(1)} %copy-done.12, f32[16,256]{0,1:T(8,128)} %copy.577, ...), kind=kLoop, calls=%fused_computation.43 | loop fusion | flops 8912896 | bytes 10551808 | tf_op jit(solution)/shard_map/convert_element_type | solution.py:78
  365.9 22.1 %all_to_all.163 = bf16[16,256,128]{1,0,2:T(8,128)(2,1)S(1)} all-to-all(bf16[16,256,128]{1,0,2:T(8,128)(2,1)S(1)} %copy.584), channel_id=1, replica_groups=mesh['dp'=8,'axial'=16] {'axial'}, dimensions={2} | all-to-all | bytes 2097152 | tf_op jit(solution)/shard_map/all_to_all | solution.py:149
  392.2 5.4 all-to-all-start.10
  397.6 4.4 convolution_bitcast_fusion.2
  406.1 8.9 %all-to-all-done.10 = bf16[256,256,8]{1,2,0:T(8,128)(2,1)} async-done(((bf16[256,256,8]{1,2,0:T(8,128)(2,1)}), bf16[256,256,8]{1,2,0:T(8,128)(2,1)}, u32[]{:S(2)}, u32[]{:S(2)}) %all-to-all-start.10) | async-done | bytes 1048608 | tf_op jit(solution)/shard_map/all_to_all | solution.py:165
  415.0 4.3 all-to-all-start.11
  431.6 5.0 all-to-all-done.11
  441.2 5.7 multiply_convert_fusion.4
  455.2 6.4 convert_reduce_fusion.2
  480.1 50.8 %reduce-scatter.2.cloned.1.call-done = bf16[16,32,128]{2,1,0:T(8,128)(2,1)} async-done(((bf16[256,32,128]{2,1,0:T(8,128)(2,1)}), bf16[16,32,128]{2,1,0:T(8,128)(2,1)}) %reduce-scatter.2.cloned.1.call-update) | async-done | bytes 131088 | tf_op jit(solution)/shard_map/reduce_scatter | solution.py:312
  533.1 66.4 %all-reduce = (f32[1024]{0:T(1024)S(1)}, f32[1024]{0:T(1024)S(1)}, f32[128]{0:T(128)S(1)}, f32[2,128]{1,0:T(2,128)S(1)}, f32[2,128]{1,0:T(2,128)S(1)}, /*index=5*/f32[2,128]{1,0:T(2,128)S(1)}, f32[2,128]{1,0:T(2,128)S(1)}) all-reduce(f32[1024]{0:T(1024)S(1)} %get-tuple-element.121, ...), channel_id=1, replica_groups=mesh['dp'=8,'axial'=16] {'dp','axial'}, use_global_device_ids=true, to_apply=%region_22.0 | all-reduce | flops 3200 | bytes 25600 | tf_op jit(solution)/shard_map/psum | solution.py:336
  606.1 145.4 %all-reduce.4.cloned.1.call-done = (f32[1024,32]{0,1:T(8,128)}, f32[1024,32]{0,1:T(8,128)}, f32[1024,128]{1,0:T(8,128)}, f32[2,128,512]{2,1,0:T(8,128)}, f32[2,128,128]{2,1,0:T(8,128)}, /*index=5*/f32[2,128,128]{2,1,0:T(8,128)}) async-done(((f32[1024,32]{0,1:T(8,128)}, f32[1024,32]{0,1:T(8,128)}, f32[1024,128]{1,0:T(8,128)}, f32[2,128,512]{2,1,0:T(8,128)}, f32[2,128,128]{2,1,0:T(8,128)}, ...) | async-done | bytes 1572880 | tf_op jit(solution)/shard_map/psum | solution.py:336
  (380 shorter events, 207.0 us)
Async XLA Ops:
  7.2 31.6 %copy-start = (bf16[1024,128]{1,0:T(8,128)(2,1)S(1)}, bf16[1024,128]{1,0:T(8,128)(2,1)}, u32[]{:S(2)}) copy-start(bf16[1024,128]{1,0:T(8,128)(2,1)} %param.25) | copy-start | bytes 786436
  7.2 32.3 %copy-start.113 = (f32[128]{0:T(128)S(1)}, f32[128]{0:T(128)}, u32[]{:S(2)}) copy-start(f32[128]{0:T(128)} %param.26) | copy-start | bytes 1540
  7.2 32.3 %copy-start.108 = (bf16[1,16,256,128]{3,2,1,0:T(8,128)(2,1)S(1)}, bf16[1,16,256,128]{3,2,1,0:T(8,128)(2,1)}, u32[]{:S(2)}) copy-start(bf16[1,16,256,128]{3,2,1,0:T(8,128)(2,1)} %param.18) | copy-start | bytes 3145732
  9.9 28.8 %copy-start.100 = (f32[16]{0:T(128)}, f32[16]{0:T(128)S(1)}, u32[]{:S(2)}) copy-start(f32[16]{0:T(128)S(1)} %dynamic-slice_bitcast_fusion) | copy-start | bytes 196
  11.0 27.7 %copy-start.76 = (bf16[16,32]{1,0:T(8,128)(2,1)}, bf16[16,32]{1,0:T(8,128)(2,1)S(1)}, u32[]{:S(2)}) copy-start(bf16[16,32]{1,0:T(8,128)(2,1)S(1)} %fusion.75) | copy-start | bytes 3076
  12.1 34.5 %copy-start.85 = (bf16[16,32,1]{1,0,2:T(8,128)(2,1)}, bf16[16,32,1]{1,0,2:T(8,128)(2,1)S(1)}, u32[]{:S(2)}) copy-start(bf16[16,32,1]{1,0,2:T(8,128)(2,1)S(1)} %fusion.77) | copy-start | bytes 3076
  39.5 7.2 copy-start.28
  39.5 8.9 %copy-start.96 = (f32[2,128]{1,0:T(2,128)S(1)}, f32[2,128]{1,0:T(2,128)}, u32[]{:S(2)}) copy-start(f32[2,128]{1,0:T(2,128)} %param.28) | copy-start | bytes 3076
  39.5 8.9 %copy-start.97 = (f32[2,128]{1,0:T(2,128)S(1)}, f32[2,128]{1,0:T(2,128)}, u32[]{:S(2)}) copy-start(f32[2,128]{1,0:T(2,128)} %param.27) | copy-start | bytes 3076
  39.5 10.0 %copy-start.58 = (bf16[2,128,512]{2,1,0:T(8,128)(2,1)S(1)}, bf16[2,128,512]{2,1,0:T(8,128)(2,1)}, u32[]{:S(2)}) copy-start(bf16[2,128,512]{2,1,0:T(8,128)(2,1)} %param.29) | copy-start | bytes 786436
  56.1 20.9 %all-to-all-start = ((bf16[16,256,128]{1,0,2:T(8,128)(2,1)}), bf16[16,256,128]{1,0,2:T(8,128)(2,1)S(1)}, u32[]{:S(2)}, u32[]{:S(2)}) async-start(bf16[16,256,128]{1,0,2:T(8,128)(2,1)} %copy.523), calls=%async_computation | async-start | bytes 2097152 | tf_op jit(solution)/shard_map/all_to_all | solution.py:131
  77.0 22.3 %all-to-all-start.1 = ((bf16[16,256,128]{1,0,2:T(8,128)(2,1)}), bf16[16,256,128]{1,0,2:T(8,128)(2,1)}, u32[]{:S(2)}, u32[]{:S(2)}) async-start(bf16[16,256,128]{1,0,2:T(8,128)(2,1)} %copy.528), calls=%async_computation.1 | async-start | bytes 2097152 | tf_op jit(solution)/shard_map/all_to_all | solution.py:130
  82.0 20.1 %copy-start.5 = (bf16[16,16,256,8]{2,1,0,3:T(8,128)(2,1)}, bf16[16,16,256,8]{2,1,0,3:T(8,128)(2,1)S(1)}, u32[]{:S(2)}) copy-start(bf16[16,16,256,8]{2,1,0,3:T(8,128)(2,1)S(1)} %copy.525) | copy-start | bytes 3145732
  104.0 21.8 %all-to-all-start.2 = ((bf16[256,256,8]{1,2,0:T(8,128)(2,1)}), bf16[256,256,8]{1,2,0:T(8,128)(2,1)S(1)}, u32[]{:S(2)}, u32[]{:S(2)}) async-start(bf16[256,256,8]{1,2,0:T(8,128)(2,1)} %copy.531), calls=%async_computation.2 | async-start | bytes 2097152 | tf_op jit(solution)/shard_map/all_to_all | solution.py:141
  135.8 14.0 %copy-start.11 = (bf16[16,256,128]{2,0,1:T(8,128)(2,1)}, bf16[16,256,128]{2,0,1:T(8,128)(2,1)S(1)}, u32[]{:S(2)}) copy-start(bf16[16,256,128]{2,0,1:T(8,128)(2,1)S(1)} %get-tuple-element.147) | copy-start | bytes 3145732
  156.9 21.6 %all-to-all-start.3 = ((bf16[16,256,128]{1,0,2:T(8,128)(2,1)}), bf16[16,256,128]{1,0,2:T(8,128)(2,1)S(1)}, u32[]{:S(2)}, u32[]{:S(2)}) async-start(bf16[16,256,128]{1,0,2:T(8,128)(2,1)} %copy.543), calls=%async_computation.3 | async-start | bytes 2097152 | tf_op jit(solution)/shard_map/all_to_all | solution.py:131
  178.5 22.3 %all-to-all-start.4 = ((bf16[16,256,128]{1,0,2:T(8,128)(2,1)}), bf16[16,256,128]{1,0,2:T(8,128)(2,1)}, u32[]{:S(2)}, u32[]{:S(2)}) async-start(bf16[16,256,128]{1,0,2:T(8,128)(2,1)} %copy.548), calls=%async_computation.4 | async-start | bytes 2097152 | tf_op jit(solution)/shard_map/all_to_all | solution.py:130
  185.1 19.5 %copy-start.8 = (bf16[16,16,256,8]{2,3,1,0:T(8,128)(2,1)}, bf16[16,16,256,8]{2,3,1,0:T(8,128)(2,1)S(1)}, u32[]{:S(2)}) copy-start(bf16[16,16,256,8]{2,3,1,0:T(8,128)(2,1)S(1)} %copy.545) | copy-start | bytes 3145732
  207.3 21.6 %all-to-all-start.5 = ((bf16[256,256,8]{1,2,0:T(8,128)(2,1)}), bf16[256,256,8]{1,2,0:T(8,128)(2,1)S(1)}, u32[]{:S(2)}, u32[]{:S(2)}) async-start(bf16[256,256,8]{1,2,0:T(8,128)(2,1)} %copy.552), calls=%async_computation.5 | async-start | bytes 2097152 | tf_op jit(solution)/shard_map/all_to_all | solution.py:141
  245.7 21.3 %copy-start.9 = (bf16[16,16,256,8]{2,3,1,0:T(8,128)(2,1)S(1)}, bf16[16,16,256,8]{2,3,1,0:T(8,128)(2,1)}, u32[]{:S(2)}) copy-start(bf16[16,16,256,8]{2,3,1,0:T(8,128)(2,1)} %copy-done.8) | copy-start | bytes 3145732
  269.5 22.8 %all-to-all-start.7 = ((bf16[256,256,8]{1,2,0:T(8,128)(2,1)}), bf16[256,256,8]{1,2,0:T(8,128)(2,1)}, u32[]{:S(2)}, u32[]{:S(2)}) async-start(bf16[256,256,8]{1,2,0:T(8,128)(2,1)} %copy.562), calls=%async_computation.7 | async-start | bytes 2097152 | tf_op jit(solution)/shard_map/all_to_all | solution.py:165
  292.4 30.3 %all-to-all-start.8 = ((bf16[256,256,8]{1,2,0:T(8,128)(2,1)}), bf16[256,256,8]{1,2,0:T(8,128)(2,1)}, u32[]{:S(2)}, u32[]{:S(2)}) async-start(bf16[256,256,8]{1,2,0:T(8,128)(2,1)} %copy.566), calls=%async_computation.8 | async-start | bytes 2097152 | tf_op jit(solution)/shard_map/all_to_all | solution.py:168
  334.9 13.0 %copy-start.21 = (bf16[1,16,256,128]{3,2,1,0:T(8,128)(2,1)S(1)}, bf16[1,16,256,128]{3,2,1,0:T(8,128)(2,1)}, u32[]{:S(2)}) copy-start(bf16[1,16,256,128]{3,2,1,0:T(8,128)(2,1)} %param.20) | copy-start | bytes 3145732
  347.9 8.4 %copy-start.17 = (f32[16,256,128]{2,0,1:T(8,128)S(1)}, f32[16,256,128]{2,0,1:T(8,128)}, u32[]{:S(2)}) copy-start(f32[16,256,128]{2,0,1:T(8,128)} %get-tuple-element.176) | copy-start | bytes 6291460
  365.9 22.2 %copy-start.6 = (bf16[16,16,256,8]{2,1,0,3:T(8,128)(2,1)S(1)}, bf16[16,16,256,8]{2,1,0,3:T(8,128)(2,1)}, u32[]{:S(2)}) copy-start(bf16[16,16,256,8]{2,1,0,3:T(8,128)(2,1)} %copy-done.5) | copy-start | bytes 3145732
  392.2 22.8 %all-to-all-start.10 = ((bf16[256,256,8]{1,2,0:T(8,128)(2,1)}), bf16[256,256,8]{1,2,0:T(8,128)(2,1)}, u32[]{:S(2)}, u32[]{:S(2)}) async-start(bf16[256,256,8]{1,2,0:T(8,128)(2,1)} %copy.588), calls=%async_computation.10 | async-start | bytes 2097152 | tf_op jit(solution)/shard_map/all_to_all | solution.py:165
  415.0 21.6 %all-to-all-start.11 = ((bf16[256,256,8]{1,2,0:T(8,128)(2,1)}), bf16[256,256,8]{1,2,0:T(8,128)(2,1)S(1)}, u32[]{:S(2)}, u32[]{:S(2)}) async-start(bf16[256,256,8]{1,2,0:T(8,128)(2,1)} %copy.592), calls=%async_computation.11 | async-start | bytes 2097152 | tf_op jit(solution)/shard_map/all_to_all | solution.py:168
  419.3 111.5 %reduce-scatter.2.cloned.1.call-start = ((), (), s32[]{:S(2)}) async-start(), calls=%async_computation.13 | async-start | bytes 2228224 | tf_op jit(solution)/shard_map/reduce_scatter | solution.py:312
  463.7 287.9 %all-reduce.4.cloned.1.call-start = ((), (), s32[]{:S(2)}) async-start(), calls=%async_computation.14 | async-start | bytes 3145728 | tf_op jit(solution)/shard_map/psum | solution.py:336
  477.3 55.5 %copy-start.71 = (bf16[1024,32]{0,1:T(8,128)(2,1)S(1)}, bf16[1024,32]{0,1:T(8,128)(2,1)}, u32[]{:S(2)}) copy-start(bf16[1024,32]{0,1:T(8,128)(2,1)} %param.24) | copy-start | bytes 196612
  477.4 124.8 %copy-start.77 = (bf16[16,32]{1,0:T(8,128)(2,1)S(1)}, bf16[16,32]{1,0:T(8,128)(2,1)}, u32[]{:S(2)}) copy-start(bf16[16,32]{1,0:T(8,128)(2,1)} %copy-done.76) | copy-start | bytes 3076
  751.5 8.2 %copy-start.56 = (f32[2,128,512]{2,1,0:T(8,128)S(1)}, f32[2,128,512]{2,1,0:T(8,128)}, u32[]{:S(2)}) copy-start(f32[2,128,512]{2,1,0:T(8,128)} %get-tuple-element.139) | copy-start | bytes 1572868
  (94 other events, 249.5 us)
Sparse Core Ops, SparseCore 0:
  463.8 66.9 reduce-scatter.1
  604.3 147.1 all-reduce.3
where the time goes:
time: 779 us; the launch traced here: 768 us
  waiting for transfers between devices  313 us (40%)
  blocking collectives  136 us (17%)
  local copies, waits for them, and re-layouts  86 us (11%)
  other arithmetic  82.1 us (11%)
  matrix products  79.4 us (10%)
  starting transfers between devices  55.3 us (7%)
  between operations  16 us (2%)
    psum x1, waiting for transfers between devices, local(): lax.psum((gain_sum, bias_sum, left_sum, right_sum, cube_sum.reshape(inner...  145 us
    psum x1, blocking collectives, local(): lax.psum((gain_sum, bias_sum, left_sum, right_sum, cube_sum.reshape(inner...  66.4 us
    reduce_scatter x1, waiting for transfers between devices, local(): lax.psum_scatter(jnp.einsum('ia,ijc->jac', left_outer, outer_grad, prefer...  50.8 us
    all_to_all x2, blocking collectives, core_backward(): lax.all_to_all(product_grad, 'axial', split_axis=2, concat_axis=0, tiled=...  43.3 us
    all_to_all x2, waiting for transfers between devices, core_forward(): lax.all_to_all(left_side, 'axial', split_axis=2, concat_axis=0, tiled=True)  33 us
    all_to_all x2, waiting for transfers between devices, core_forward(): lax.all_to_all(right_side, 'axial', split_axis=2, concat_axis=0, tiled=True)  29.5 us
    all_to_all x2, waiting for transfers between devices, core_forward(): lax.all_to_all(partial_product.astype(jnp.bfloat16), 'axial', split_axis=...  29.1 us
    all_gather x1, blocking collectives, local(): right_every = lax.all_gather(right_outer, 'axial', axis=0, tiled=True)  26.5 us
  transfers between devices with their start and end apart: 12, of which 12 were waited for; matrix products, arithmetic and copies ran while one was open for 10% of the time, Pallas kernels for 0%

commit v1 on v0

v1 whole, which is shorter than its diff:
```python
import functools

import jax
import jax.numpy as jnp
from jax import lax
from jax.experimental import pallas as pl
from jax.experimental.pallas import tpu as pltpu
from jax.sharding import PartitionSpec as P

EPSILON = 1e-05
F32 = jnp.float32
BF16 = jnp.bfloat16
MESH = pl.DeviceIdType.MESH
C = 128
I = 16
J = 256
B = 32
Q = 4
CQ = 4
PART = 208
VMEM_LIMIT = 56 * 2**20


def nn(a, b):
    return lax.dot_general(a, b, (((1,), (0,)), ((), ())), preferred_element_type=F32)


def nt(a, b):
    return lax.dot_general(a, b, (((1,), (1,)), ((), ())), preferred_element_type=F32)


def tn(a, b):
    return lax.dot_general(a, b, (((0,), (0,)), ((), ())), preferred_element_type=F32)


def sigmoid(x):
    return 0.5 * jnp.tanh(0.5 * x) + 0.5


def norm(x, axis=0):
    centred = x - jnp.mean(x, axis=axis, keepdims=True)
    variance = jnp.mean(centred * centred, axis=axis, keepdims=True)
    inverse = lax.rsqrt(variance + EPSILON)
    return centred * inverse, inverse


def norm_back(scaled, standard, inverse, axis=0):
    first = jnp.mean(scaled, axis=axis, keepdims=True)
    second = jnp.mean(scaled * standard, axis=axis, keepdims=True)
    return inverse * (scaled - first - standard * second)


def put_row(cells, i, value):
    cells[0, pl.ds(i, C, stride=I), :] = value[:, :C]
    cells[1, pl.ds(i, C, stride=I), :] = value[:, C:]


def get_row(cells, i):
    return jnp.concatenate(
        [cells[0, pl.ds(i, C, stride=I), :], cells[1, pl.ds(i, C, stride=I), :]], axis=1
    )


def cells_out(cells, out_ref):
    def step(n, _):
        for half in range(2):
            part = cells[half, pl.ds(pl.multiple_of(n * 256, 256), 256), :]
            out_ref[pl.ds(n * 16, 16), :, half * C : (half + 1) * C] = part.reshape(
                16, I, C
            ).astype(BF16)
        return 0

    lax.fori_loop(0, 8, step, 0)


def cells_in(in_ref, cells):
    def step(n, _):
        for half in range(2):
            part = in_ref[pl.ds(n * 16, 16), :, half * C : (half + 1) * C]
            cells[half, pl.ds(pl.multiple_of(n * 256, 256), 256), :] = part.astype(F32).reshape(
                256, C
            )
        return 0

    lax.fori_loop(0, 8, step, 0)


def wide(ref):
    return jnp.broadcast_to(ref[...], (C, J))


def send_factors(pair_in, mask_row, gain, bias, front_weight, left_cells, right_cells, i):
    standard, _ = norm(pair_in)
    normed = (standard * gain + bias).astype(BF16)
    projected = nn(front_weight[: 4 * C, :], normed)
    put_row(left_cells, i, mask_row * sigmoid(projected[:C]) * projected[C : 2 * C])
    put_row(right_cells, i, mask_row * sigmoid(projected[2 * C : 3 * C]) * projected[3 * C :])


def head_kernel(single_ref, gain_ref, bias_ref, weight_ref, own_ref, every_ref, send_sem, recv_sem):
    me = lax.axis_index("axial")
    dp = lax.axis_index("dp")
    barrier = pltpu.get_barrier_semaphore()

    def greet(t, _):
        pl.semaphore_signal(
            barrier, inc=1, device_id=(dp, lax.rem(me + t, 16)), device_id_type=MESH
        )
        return 0

    lax.fori_loop(1, 16, greet, 0)
    standard, _ = norm(single_ref[...].astype(F32), axis=1)
    normed = (standard * gain_ref[...] + bias_ref[...]).astype(BF16)
    both = nn(normed, weight_ref[...]) * own_ref[...]
    mine = pl.ds(pl.multiple_of(me * I, I), I)
    every_ref[mine, :] = both.astype(BF16)
    pl.semaphore_wait(barrier, 15)

    def copy(t):
        return pltpu.make_async_remote_copy(
            src_ref=every_ref.at[mine],
            dst_ref=every_ref.at[mine],
            send_sem=send_sem.at[t],
            recv_sem=recv_sem.at[t],
            device_id=(dp, lax.rem(me + t, 16)),
            device_id_type=MESH,
        )

    def begin(t, _):
        copy(t).start()
        return 0

    def finish(t, _):
        copy(t).wait()
        return 0

    lax.fori_loop(1, 16, begin, 0)
    lax.fori_loop(1, 16, finish, 0)


def mixed_rows(own_left, cube_ref, mixed_cells):
    for b in range(B):
        mixed_cells[b * I : (b + 1) * I, :] = nn(own_left, cube_ref[:, b * C : (b + 1) * C])


def front_first_kernel(
    pair_ref,
    every_ref,
    own_both_ref,
    cube_ref,
    mask_ref,
    outer_bias_ref,
    gain_ref,
    bias_ref,
    front_ref,
    first_ref,
    left_ref,
    right_ref,
    left_cells,
    right_cells,
    mixed_cells,
):
    right_rows = every_ref[...].astype(F32).T[B : 2 * B].astype(BF16)
    mixed_rows(own_both_ref[:, :B], cube_ref, mixed_cells)
    gain, bias, outer_bias = wide(gain_ref), wide(bias_ref), wide(outer_bias_ref)

    def step(i, _):
        mask_row = mask_ref[pl.ds(i, 1), :]
        mixed_left = mixed_cells[pl.ds(i, B, stride=I), :].astype(BF16)
        term = tn(mixed_left, right_rows) + outer_bias
        first = (pair_ref[i].astype(F32).T + mask_row * term).astype(BF16)
        first_ref[i] = first
        send_factors(
            first.astype(F32), mask_row, gain, bias, front_ref, left_cells, right_cells, i
        )
        return 0

    lax.fori_loop(0, I, step, 0)
    cells_out(left_cells, left_ref)
    cells_out(right_cells, right_ref)


def middle_kernel(
    product_ref,
    first_ref,
    mask_ref,
    gain0_ref,
    bias0_ref,
    front0_ref,
    out_gain0_ref,
    out_bias0_ref,
    out0_ref,
    gain1_ref,
    bias1_ref,
    front1_ref,
    second_ref,
    left_ref,
    right_ref,
    product_cells,
    left_cells,
    right_cells,
):
    cells_in(product_ref, product_cells)
    gain0, bias0, gain1, bias1 = wide(gain0_ref), wide(bias0_ref), wide(gain1_ref), wide(bias1_ref)
    out_gain0, out_bias0 = wide(out_gain0_ref), wide(out_bias0_ref)

    def step(i, _):
        mask_row = mask_ref[pl.ds(i, 1), :]
        product_standard, _ = norm(get_row(product_cells, i))
        product_norm = (product_standard * out_gain0 + out_bias0).astype(BF16)
        linear = tn(out0_ref[...], product_norm)
        first = first_ref[i].astype(F32)
        standard, _ = norm(first)
        normed = (standard * gain0 + bias0).astype(BF16)
        gate = sigmoid(nn(front0_ref[4 * C :, :], normed))
        second = (first + gate * linear).astype(BF16)
        second_ref[i] = second
        send_factors(
            second.astype(F32), mask_row, gain1, bias1, front1_ref, left_cells, right_cells, i
        )
        return 0

    lax.fori_loop(0, I, step, 0)
    cells_out(left_cells, left_ref)
    cells_out(right_cells, right_ref)


def back_out(cotangent, product, pair_in, gain, bias, front_ref, out_gain, out_bias, out_ref, sums):
    out_sum, out_gain_sum, out_bias_sum = sums
    product_standard, product_inverse = norm(product)
    product_norm = (product_standard * out_gain + out_bias).astype(BF16)
    linear = tn(out_ref[...], product_norm)
    standard, _ = norm(pair_in)
    normed = (standard * gain + bias).astype(BF16)
    gate = sigmoid(nn(front_ref[4 * C :, :], normed))
    linear_grad = (cotangent * gate).astype(BF16)
    gate_grad = (cotangent * linear * gate * (1.0 - gate)).astype(BF16)
    out_sum[...] += nt(product_norm, linear_grad)
    norm_grad = nn(out_ref[...], linear_grad)
    out_gain_sum[...] += norm_grad * product_standard
    out_bias_sum[...] += norm_grad
    return gate_grad, norm_back(norm_grad * out_gain, product_standard, product_inverse)


def back_in(
    cotangent,
    gate_grad,
    left_grad,
    right_grad,
    pair_in,
    mask_row,
    gain,
    bias,
    front_ref,
    back_ref,
    sums,
):
    front_sum, gain_sum, bias_sum = sums
    standard, inverse = norm(pair_in)
    normed = (standard * gain + bias).astype(BF16)
    projected = nn(front_ref[: 4 * C, :], normed)
    grads = []
    for at, side in ((0, left_grad), (2 * C, right_grad)):
        gate = sigmoid(projected[at : at + C])
        masked = side * mask_row * gate
        grads.append((masked * projected[at + C : at + 2 * C] * (1.0 - gate)).astype(BF16))
        grads.append(masked.astype(BF16))
    grads = jnp.concatenate(grads + [gate_grad], axis=0)
    front_sum[...] += nt(normed, grads)
    normed_grad = nn(back_ref[...], grads)
    gain_sum[...] += normed_grad * standard
    bias_sum[...] += normed_grad
    return (cotangent + norm_back(normed_grad * gain, standard, inverse)).astype(BF16)


def clear(*refs):
    for ref in refs:
        ref[...] = jnp.zeros(ref.shape, ref.dtype)


def columns(*refs):
    made = [jnp.sum(ref[...], axis=1, keepdims=True) for ref in refs]
    lane = lax.broadcasted_iota(jnp.int32, (C, C), 1)
    total = jnp.zeros((C, C), F32)
    for n, column in enumerate(made):
        total = jnp.where(lane == n, column, total)
    return total


def back_second_kernel(
    product_ref,
    second_ref,
    cotangent_ref,
    gain_ref,
    bias_ref,
    front_ref,
    out_gain_ref,
    out_bias_ref,
    out_ref,
    grad_ref,
    gate_grad_ref,
    out_sum,
    small_ref,
    product_cells,
    grad_cells,
    out_gain_sum,
    out_bias_sum,
):
    cells_in(product_ref, product_cells)
    gain, bias = wide(gain_ref), wide(bias_ref)
    out_gain, out_bias = wide(out_gain_ref), wide(out_bias_ref)
    clear(out_sum, out_gain_sum, out_bias_sum)

    def step(i, _):
        gate_grad, product_grad = back_out(
            cotangent_ref[i].astype(F32).T,
            get_row(product_cells, i),
            second_ref[i].astype(F32),
            gain,
            bias,
            front_ref,
            out_gain,
            out_bias,
            out_ref,
            (out_sum, out_gain_sum, out_bias_sum),
        )
        gate_grad_ref[i] = gate_grad
        put_row(grad_cells, i, product_grad)
        return 0

    lax.fori_loop(0, I, step, 0)
    cells_out(grad_cells, grad_ref)
    small_ref[...] = columns(out_gain_sum, out_bias_sum)


def back_middle_kernel(
    left_ref,
    right_ref,
    second_ref,
    cotangent_ref,
    gate_grad1_ref,
    product_ref,
    first_ref,
    mask_ref,
    gain1_ref,
    bias1_ref,
    front1_ref,
    back1_ref,
    gain0_ref,
    bias0_ref,
    front0_ref,
    out_gain0_ref,
    out_bias0_ref,
    out0_ref,
    grad_second_ref,
    grad_ref,
    gate_grad0_ref,
    front_sum,
    out_sum,
    small_ref,
    left_cells,
    right_cells,
    product_cells,
    grad_cells,
    gain_sum,
    bias_sum,
    out_gain_sum,
    out_bias_sum,
):
    cells_in(left_ref, left_cells)
    cells_in(right_ref, right_cells)
    cells_in(product_ref, product_cells)
    gain1, bias1, gain0, bias0 = wide(gain1_ref), wide(bias1_ref), wide(gain0_ref), wide(bias0_ref)
    out_gain0, out_bias0 = wide(out_gain0_ref), wide(out_bias0_ref)
    clear(front_sum, out_sum, gain_sum, bias_sum, out_gain_sum, out_bias_sum)

    def step(i, _):
        grad_second = back_in(
            cotangent_ref[i].astype(F32).T,
            gate_grad1_ref[i],
            get_row(left_cells, i),
            get_row(right_cells, i),
            second_ref[i].astype(F32),
            mask_ref[pl.ds(i, 1), :],
            gain1,
            bias1,
            front1_ref,
            back1_ref,
            (front_sum, gain_sum, bias_sum),
        )
        grad_second_ref[i] = grad_second
        gate_grad, product_grad = back_out(
            grad_second.astype(F32),
            get_row(product_cells, i),
            first_ref[i].astype(F32),
            gain0,
            bias0,
            front0_ref,
            out_gain0,
            out_bias0,
            out0_ref,
            (out_sum, out_gain_sum, out_bias_sum),
        )
        gate_grad0_ref[i] = gate_grad
        put_row(grad_cells, i, product_grad)
        return 0

    lax.fori_loop(0, I, step, 0)
    cells_out(grad_cells, grad_ref)
    small_ref[...] = columns(gain_sum, bias_sum, out_gain_sum, out_bias_sum)


def back_first_kernel(
    left_ref,
    right_ref,
    first_ref,
    grad_second_ref,
    gate_grad_ref,
    mask_ref,
    every_ref,
    own_both_ref,
    cube_ref,
    gain_ref,
    bias_ref,
    front_ref,
    back_ref,
    pair_grad_ref,
    front_sum,
    small_ref,
    cube_sum_ref,
    left_single_ref,
    right_total_ref,
    left_cells,
    right_cells,
    mixed_cells,
    outer_cells,
    gain_sum,
    bias_sum,
    outer_bias_sum,
    right_total,
):
    cells_in(left_ref, left_cells)
    cells_in(right_ref, right_cells)
    right_rows = every_ref[...].astype(F32).T[B : 2 * B].astype(BF16)
    own_left = own_both_ref[:, :B]
    mixed_rows(own_left, cube_ref, mixed_cells)
    gain, bias = wide(gain_ref), wide(bias_ref)
    clear(front_sum, gain_sum, bias_sum, outer_bias_sum, right_total)

    def step(i, _):
        mask_row = mask_ref[pl.ds(i, 1), :]
        grad_first = back_in(
            grad_second_ref[i].astype(F32),
            gate_grad_ref[i],
            get_row(left_cells, i),
            get_row(right_cells, i),
            first_ref[i].astype(F32),
            mask_row,
            gain,
            bias,
            front_ref,
            back_ref,
            (front_sum, gain_sum, bias_sum),
        ).astype(F32)
        pair_grad_ref[i] = grad_first.T.astype(BF16)
        outer_grad = grad_first * mask_row
        outer_bias_sum[...] += outer_grad
        outer_grad = outer_grad.astype(BF16)
        outer_cells[pl.ds(i, B, stride=I), :] = nt(right_rows, outer_grad)
        mixed_left = mixed_cells[pl.ds(i, B, stride=I), :].astype(BF16)
        right_total[:B, :] += nn(mixed_left, outer_grad)
        return 0

    lax.fori_loop(0, I, step, 0)
    small_ref[...] = columns(gain_sum, bias_sum, outer_bias_sum)
    left_single = jnp.zeros((I, B), F32)
    for b in range(B):
        rows = outer_cells[b * I : (b + 1) * I, :].astype(BF16)
        cube_sum_ref[b * B : (b + 1) * B, :] = tn(own_left, rows)
        left_single += nt(rows, cube_ref[:, b * C : (b + 1) * C])
    left_single_ref[...] = jnp.concatenate([left_single, jnp.zeros((I, C - B), F32)], axis=1)
    right_total_ref[...] = right_total[...].T


class Place:
    def __init__(self):
        self.me = lax.axis_index("axial")
        self.dp = lax.axis_index("dp")
        self.half = lax.rem(self.me // 2, 2)
        self.group = (self.me // 4) * 2 + lax.rem(self.me, 2)
        self.other = self.me + 2 - 4 * self.half

    def axial(self, group):
        return (group // 2) * 4 + self.half * 2 + lax.rem(group, 2)

    def peer(self, t):
        return lax.rem(self.group + t, 8)

    def greet(self):
        barrier = pltpu.get_barrier_semaphore()

        def signal(t, _):
            pl.semaphore_signal(
                barrier,
                inc=1,
                device_id=(self.dp, self.axial(self.peer(t))),
                device_id_type=MESH,
            )
            return 0

        lax.fori_loop(1, 8, signal, 0)
        pl.semaphore_signal(barrier, inc=1, device_id=(self.dp, self.other), device_id_type=MESH)
        pl.semaphore_wait(barrier, 8)

    def to_group(self, source, target, send_sem, recv_sem, t):
        group = self.peer(t)
        return pltpu.make_async_remote_copy(
            src_ref=source(group),
            dst_ref=target,
            send_sem=send_sem.at[t],
            recv_sem=recv_sem.at[t],
            device_id=(self.dp, self.axial(group)),
            device_id_type=MESH,
        )

    def to_half(self, source, target, send_sem, recv_sem):
        return pltpu.make_async_remote_copy(
            src_ref=source,
            dst_ref=target,
            send_sem=send_sem,
            recv_sem=recv_sem,
            device_id=(self.dp, self.other),
            device_id_type=MESH,
        )


def each_peer(do):
    def step(t, _):
        do(t)
        return 0

    lax.fori_loop(1, 8, step, 0)


def each_piece(do):
    def step(q, _):
        do(q)
        return 0

    lax.fori_loop(0, Q, step, 0)


def each_channel(q, do):
    def step(n, _):
        do(q * CQ + n)
        return 0

    lax.fori_loop(0, CQ, step, 0)


def rows_of(at, count=I):
    return pl.ds(pl.multiple_of(at, 16), count)


class Spread:
    def __init__(self, place, source, target, row, sems, at):
        self.place, self.source, self.target, self.row = place, source, target, row
        self.send_sem, self.recv_sem, self.local_sem = sems
        self.at = at

    def copy(self, q, t):
        return self.place.to_group(
            lambda group: self.source.at[pl.ds(group * 16 + q * CQ, CQ)],
            self.target.at[pl.ds(q * CQ, CQ), rows_of(self.row)],
            self.send_sem.at[self.at, q],
            self.recv_sem.at[self.at, q],
            t,
        )

    def local(self):
        return pltpu.make_async_copy(
            self.source.at[pl.ds(self.place.group * 16, 16)],
            self.target.at[:, rows_of(self.row)],
            self.local_sem.at[self.at],
        )

    def send(self, q):
        each_peer(lambda t: self.copy(q, t).start())

    def arrive(self, q):
        each_peer(lambda t: self.copy(q, t).wait_recv())

    def sent(self):
        each_piece(lambda q: each_peer(lambda t: self.copy(q, t).wait_send()))


class Collect:
    def __init__(self, place, source, target, sems, at):
        self.place, self.source, self.target = place, source, target
        self.send_sem, self.recv_sem, self.local_sem = sems
        self.at = at

    def copy(self, q, t):
        return self.place.to_group(
            lambda group: self.source.at[pl.ds(q * CQ, CQ), rows_of(group * I)],
            self.target.at[pl.ds(self.place.group * 16 + q * CQ, CQ)],
            self.send_sem.at[self.at, q],
            self.recv_sem.at[self.at, q],
            t,
        )

    def local(self):
        return pltpu.make_async_copy(
            self.source.at[:, rows_of(self.place.group * I)],
            self.target.at[pl.ds(self.place.group * 16, 16)],
            self.local_sem.at[self.at],
        )

    def send(self, q):
        each_peer(lambda t: self.copy(q, t).start())

    def finish(self):
        each_piece(lambda q: each_peer(lambda t: self.copy(q, t).wait()))


def swap_rows(place, target, send_sem, recv_sem, q, x):
    rows = rows_of(x * 64 + place.half * 32, 32)
    block = target.at[pl.ds(q * CQ, CQ), rows]
    return place.to_half(block, block, send_sem.at[q, x], recv_sem.at[q, x])


def each_x(do):
    def step(x, _):
        do(x)
        return 0

    lax.fori_loop(0, 4, step, 0)


def split_halves(place, whole, kept, sent, channel):
    for x in range(4):
        kept[channel, x * 32 : (x + 1) * 32, :] = whole[
            pl.ds(pl.multiple_of(x * 64 + place.half * 32, 32), 32), :
        ]
        sent[channel, x * 32 : (x + 1) * 32, :] = whole[
            pl.ds(pl.multiple_of(x * 64 + 32 - place.half * 32, 32), 32), :
        ].astype(BF16)


def swap_sums(place, sent, received, send_sem, recv_sem, q):
    piece = pl.ds(q * CQ, CQ)
    return place.to_half(
        sent.at[piece], received.at[piece], send_sem.at[q, 0], recv_sem.at[q, 0]
    )


def outgoing_kernel(
    left_ref,
    right_ref,
    left_kept,
    right_kept,
    product_ref,
    staged,
    send_sem,
    recv_sem,
    local_sem,
    half_send,
    half_recv,
):
    place = Place()
    sems = (send_sem, recv_sem, local_sem)
    right = Spread(place, right_ref, right_kept, place.me * I, sems, 0)
    left = Spread(place, left_ref, left_kept, place.group * I, sems, 1)
    product = Collect(place, staged, product_ref, sems, 2)
    right.local().start()
    left.local().start()
    place.greet()
    each_piece(right.send)
    each_piece(left.send)
    right.local().wait()
    left.local().wait()

    def forward(q):
        right.arrive(q)
        each_x(lambda x: swap_rows(place, right_kept, half_send, half_recv, q, x).start())

    each_piece(forward)

    def multiply(q):
        left.arrive(q)
        each_x(lambda x: swap_rows(place, right_kept, half_send, half_recv, q, x).wait_recv())

        def one(c):
            staged[c] = nt(left_kept[c], right_kept[c]).astype(BF16)

        each_channel(q, one)
        product.send(q)

    each_piece(multiply)
    product.local().start()
    right.sent()
    left.sent()
    each_piece(
        lambda q: each_x(
            lambda x: swap_rows(place, right_kept, half_send, half_recv, q, x).wait_send()
        )
    )
    product.local().wait()
    product.finish()


def incoming_kernel(
    left_ref,
    right_ref,
    left_kept,
    right_kept,
    product_ref,
    staged,
    whole,
    kept_sum,
    sent_sum,
    received_sum,
    send_sem,
    recv_sem,
    local_sem,
    half_send,
    half_recv,
):
    place = Place()
    sems = (send_sem, recv_sem, local_sem)
    right = Spread(place, right_ref, right_kept, place.group * I, sems, 0)
    left = Spread(place, left_ref, left_kept, place.group * I, sems, 1)
    product = Collect(place, staged, product_ref, sems, 2)
    right.local().start()
    left.local().start()
    place.greet()

    def begin(q):
        left.send(q)
        right.send(q)

    each_piece(begin)
    right.local().wait()
    left.local().wait()

    def multiply(q):
        left.arrive(q)
        right.arrive(q)

        def one(c):
            whole[...] = tn(left_kept[c], right_kept[c])
            split_halves(place, whole, kept_sum, sent_sum, c)

        each_channel(q, one)
        swap_sums(place, sent_sum, received_sum, half_send, half_recv, q).start()

    each_piece(multiply)

    def add(q):
        swap_sums(place, sent_sum, received_sum, half_send, half_recv, q).wait_recv()

        def one(c):
            staged[c] = (kept_sum[c] + received_sum[c].astype(F32)).astype(BF16)

        each_channel(q, one)
        product.send(q)

    each_piece(add)
    product.local().start()
    right.sent()
    left.sent()
    each_piece(
        lambda q: swap_sums(place, sent_sum, received_sum, half_send, half_recv, q).wait_send()
    )
    product.local().wait()
    product.finish()


def incoming_back_kernel(
    grad_ref,
    left_kept,
    right_kept,
    left_ref,
    right_ref,
    grad_every,
    left_staged,
    right_staged,
    send_sem,
    recv_sem,
    local_sem,
    half_send,
    half_recv,
):
    place = Place()
    sems = (send_sem, recv_sem, local_sem)
    grad = Spread(place, grad_ref, grad_every, place.me * I, sems, 0)
    left = Collect(place, left_staged, left_ref, sems, 1)
    right = Collect(place, right_staged, right_ref, sems, 2)
    grad.local().start()
    place.greet()
    each_piece(grad.send)
    grad.local().wait()

    def forward(q):
        grad.arrive(q)
        each_x(lambda x: swap_rows(place, grad_every, half_send, half_recv, q, x).start())

    each_piece(forward)

    def multiply(q):
        each_x(lambda x: swap_rows(place, grad_every, half_send, half_recv, q, x).wait_recv())

        def one(c):
            left_staged[c] = nt(right_kept[c], grad_every[c]).astype(BF16)
            right_staged[c] = nn(left_kept[c], grad_every[c]).astype(BF16)

        each_channel(q, one)
        left.send(q)
        right.send(q)

    each_piece(multiply)
    left.local().start()
    right.local().start()
    grad.sent()
    each_piece(
        lambda q: each_x(
            lambda x: swap_rows(place, grad_every, half_send, half_recv, q, x).wait_send()
        )
    )
    left.local().wait()
    right.local().wait()
    left.finish()
    right.finish()


def outgoing_back_kernel(
    grad_ref,
    left_kept,
    right_kept,
    left_ref,
    right_ref,
    grad_half,
    left_staged,
    right_staged,
    whole,
    kept_sum,
    sent_sum,
    received_sum,
    send_sem,
    recv_sem,
    local_sem,
    half_send,
    half_recv,
):
    place = Place()
    sems = (send_sem, recv_sem, local_sem)
    grad = Spread(place, grad_ref, grad_half, place.group * I, sems, 0)
    left = Collect(place, left_staged, left_ref, sems, 1)
    right = Collect(place, right_staged, right_ref, sems, 2)
    grad.local().start()
    place.greet()
    each_piece(grad.send)
    grad.local().wait()

    def multiply(q):
        grad.arrive(q)

        def one(c):
            whole[...] = tn(grad_half[c], left_kept[c])
            split_halves(place, whole, kept_sum, sent_sum, c)
            left_staged[c] = nn(grad_half[c], right_kept[c]).astype(BF16)

        each_channel(q, one)
        swap_sums(place, sent_sum, received_sum, half_send, half_recv, q).start()
        left.send(q)

    each_piece(multiply)

    def add(q):
        swap_sums(place, sent_sum, received_sum, half_send, half_recv, q).wait_recv()

        def one(c):
            right_staged[c] = (kept_sum[c] + received_sum[c].astype(F32)).astype(BF16)

        each_channel(q, one)
        right.send(q)

    each_piece(add)
    left.local().start()
    right.local().start()
    grad.sent()
    each_piece(
        lambda q: swap_sums(place, sent_sum, received_sum, half_send, half_recv, q).wait_send()
    )
    left.local().wait()
    right.local().wait()
    left.finish()
    right.finish()


def total_kernel(
    scale,
    right_total_ref,
    left_single_ref,
    single_ref,
    gain_ref,
    bias_ref,
    weight_ref,
    own_ref,
    front0_sum,
    front1_sum,
    out0_sum,
    out1_sum,
    cube_sum,
    small_ref,
    single_grad_ref,
    total_ref,
    packed,
    right_parts,
    pair_part,
    chip_sum,
    chip_parts,
    dp_parts,
    right_send,
    right_recv,
    core_sem,
    chip_send,
    chip_recv,
    dp_send,
    dp_recv,
    back_send,
    back_recv,
    last_send,
    last_recv,
):
    me = lax.axis_index("axial")
    dp = lax.axis_index("dp")
    core = lax.rem(me, 2)
    chip = me // 2
    sibling = me + 1 - 2 * core
    barrier = pltpu.get_barrier_semaphore()

    def greet(t, _):
        pl.semaphore_signal(
            barrier, inc=1, device_id=(dp, lax.rem(me + t, 16)), device_id_type=MESH
        )
        return 0

    def greet_dp(t, _):
        pl.semaphore_signal(
            barrier, inc=1, device_id=(lax.rem(dp + t, 8), me), device_id_type=MESH
        )
        return 0

    lax.fori_loop(1, 16, greet, 0)
    lax.fori_loop(1, 8, greet_dp, 0)

    def put(at, value):
        count = value.shape[0]
        while count:
            room = min(count, PART - at % PART)
            packed[at // PART, at % PART : at % PART + room, :] = value[:room].astype(BF16)
            at, value, count = at + room, value[room:], count - room

    for n in range(5):
        put(n * C, front0_sum[:, n * C : (n + 1) * C])
        put((5 + n) * C, front1_sum[:, n * C : (n + 1) * C])
    put(10 * C, out0_sum[...])
    put(11 * C, out1_sum[...])
    put(12 * C, cube_sum[...])
    put(24 * C, small_ref[...])
    standard, inverse = norm(single_ref[...].astype(F32), axis=1)
    normed = (standard * gain_ref[...] + bias_ref[...]).astype(BF16)
    pl.semaphore_wait(barrier, 22)

    def right_copy(t):
        target = lax.rem(me + t, 16)
        return pltpu.make_async_remote_copy(
            src_ref=right_total_ref.at[rows_of(target * I)],
            dst_ref=right_parts.at[t],
            send_sem=right_send.at[t],
            recv_sem=right_recv.at[t],
            device_id=(dp, target),
            device_id_type=MESH,
        )

    def loop(first, last, do):
        def step(t, _):
            do(t)
            return 0

        lax.fori_loop(first, last, step, 0)

    loop(1, 16, lambda t: right_copy(t).start())
    loop(1, 16, lambda t: right_copy(t).wait_recv())
    right_single = right_total_ref[rows_of(me * I), :]
    for t in range(1, 16):
        right_single += right_parts[t]
    both = jnp.concatenate(
        [left_single_ref[:, :B], right_single[:, :B], jnp.zeros((I, C - 2 * B), F32)], axis=1
    )
    both = (both * own_ref[...]).astype(BF16)
    single_grad = nt(both, weight_ref[...])
    gain_sum = jnp.sum(single_grad * standard, axis=0, keepdims=True)
    bias_sum = jnp.sum(single_grad, axis=0, keepdims=True)
    single_grad_ref[...] = norm_back(
        single_grad * gain_ref[...], standard, inverse, axis=1
    ).astype(BF16)
    factor_sums = tn(both, normed)
    for n in range(8):
        put(20 * C + n * 64, factor_sums[:64, n * C : (n + 1) * C])
    tail = [gain_sum[:, n * C : (n + 1) * C] for n in range(8)]
    tail += [bias_sum[:, n * C : (n + 1) * C] for n in range(8)]
    put(25 * C, jnp.concatenate(tail + [jnp.zeros((C - 16, C), F32)], axis=0))

    pair_copy = pltpu.make_async_remote_copy(
        src_ref=packed.at[pl.ds(8 - 8 * core, 8)],
        dst_ref=pair_part,
        send_sem=core_sem.at[0],
        recv_sem=core_sem.at[1],
        device_id=(dp, sibling),
        device_id_type=MESH,
    )
    pair_copy.start()
    pair_copy.wait()

    def chip_copy(t):
        target = lax.rem(chip + t, 8)
        return pltpu.make_async_remote_copy(
            src_ref=chip_sum.at[target],
            dst_ref=chip_parts.at[t],
            send_sem=chip_send.at[t],
            recv_sem=chip_recv.at[t],
            device_id=(dp, target * 2 + core),
            device_id_type=MESH,
        )

    def add_pair(t):
        n = lax.rem(chip + t, 8)
        chip_sum[n] = (packed[core * 8 + n].astype(F32) + pair_part[n].astype(F32)).astype(BF16)

    def add_and_send(t):
        add_pair(t)
        chip_copy(t).start()

    loop(1, 8, add_and_send)
    add_pair(0)
    loop(1, 8, lambda t: chip_copy(t).wait_recv())
    total = chip_sum[chip].astype(F32)
    for t in range(1, 8):
        total += chip_parts[t].astype(F32)
    dp_parts[dp] = total.astype(BF16)

    def dp_copy(t):
        return pltpu.make_async_remote_copy(
            src_ref=dp_parts.at[dp],
            dst_ref=dp_parts.at[dp],
            send_sem=dp_send.at[t],
            recv_sem=dp_recv.at[t],
            device_id=(lax.rem(dp + t, 8), me),
            device_id_type=MESH,
        )

    loop(1, 8, lambda t: dp_copy(t).start())
    loop(1, 8, lambda t: dp_copy(t).wait_recv())
    total = dp_parts[0].astype(F32)
    for n in range(1, 8):
        total += dp_parts[n].astype(F32)
    total_ref[core * 8 + chip] = (total * scale).astype(BF16)

    def back_copy(t):
        block = total_ref.at[core * 8 + chip]
        return pltpu.make_async_remote_copy(
            src_ref=block,
            dst_ref=block,
            send_sem=back_send.at[t],
            recv_sem=back_recv.at[t],
            device_id=(dp, lax.rem(chip + t, 8) * 2 + core),
            device_id_type=MESH,
        )

    def last_copy(t):
        block = total_ref.at[core * 8 + lax.rem(chip + 8 - t, 8)]
        return pltpu.make_async_remote_copy(
            src_ref=block,
            dst_ref=block,
            send_sem=last_send.at[t],
            recv_sem=last_recv.at[t],
            device_id=(dp, sibling),
            device_id_type=MESH,
        )

    loop(1, 8, lambda t: back_copy(t).start())
    last_copy(0).start()

    def pass_on(t):
        back_copy(t).wait_recv()
        last_copy(t).start()

    loop(1, 8, pass_on)
    loop(0, 8, lambda t: last_copy(t).wait())
    loop(1, 8, lambda t: back_copy(t).wait_send())
    loop(1, 8, lambda t: dp_copy(t).wait_send())
    loop(1, 8, lambda t: chip_copy(t).wait_send())
    loop(1, 16, lambda t: right_copy(t).wait_send())


def unpack_kernel(
    total_ref,
    outer_gain_ref,
    outer_bias_ref,
    outer_left_ref,
    outer_right_ref,
    cube_ref,
    pair_bias_ref,
    norm_gain_ref,
    norm_bias_ref,
    proj_ref,
    gate_ref,
    out_gain_ref,
    out_bias_ref,
    out_ref,
):
    for t in range(2):
        for n in range(4):
            at = (5 * t + n) * C
            proj_ref[t, :, n * C : (n + 1) * C] = total_ref[at : at + C, :].astype(F32)
        at = (5 * t + 4) * C
        gate_ref[t] = total_ref[at : at + C, :].astype(F32)
        out_ref[t] = total_ref[(10 + t) * C : (11 + t) * C, :].astype(F32)
    cube = total_ref[12 * C : 20 * C, :].astype(F32).reshape(B, B, C)
    cube_ref[...] = jnp.swapaxes(cube, 0, 1).reshape(B * B, C)
    for n in range(8):
        at = 20 * C + n * 64
        block = jnp.concatenate(
            [total_ref[at : at + 64, :].astype(F32), jnp.zeros((64, C), F32)], axis=0
        ).T
        outer_left_ref[n * C : (n + 1) * C, :] = block[:, :B]
        outer_right_ref[n * C : (n + 1) * C, :] = block[:, B : 2 * B]
    small = total_ref[24 * C : 25 * C, :].astype(F32).T
    for t in range(2):
        norm_gain_ref[t : t + 1, :] = small[4 * t : 4 * t + 1]
        norm_bias_ref[t : t + 1, :] = small[4 * t + 1 : 4 * t + 2]
        out_gain_ref[t : t + 1, :] = small[4 * t + 2 : 4 * t + 3]
        out_bias_ref[t : t + 1, :] = small[4 * t + 3 : 4 * t + 4]
    pair_bias_ref[...] = small[8:9]
    rows = total_ref[25 * C : 25 * C + 16, :].astype(F32)
    outer_gain_ref[...] = rows[:8]
    outer_bias_ref[...] = rows[8:16]


def call(kernel, outs, scratch, args, name, collective=None, flops=0):
    return pl.pallas_call(
        kernel,
        out_shape=[jax.ShapeDtypeStruct(shape, dtype) for shape, dtype in outs],
        in_specs=[pl.BlockSpec(memory_space=pltpu.VMEM)] * len(args),
        out_specs=[pl.BlockSpec(memory_space=pltpu.VMEM)] * len(outs),
        scratch_shapes=scratch,
        name=name,
        compiler_params=pltpu.CompilerParams(
            collective_id=collective,
            has_side_effects=collective is not None,
            vmem_limit_bytes=VMEM_LIMIT,
        ),
    )(*args)


CELLS = pltpu.VMEM((2, C * I, C), F32)
SUMS = pltpu.VMEM((C, J), F32)
DMA = pltpu.SemaphoreType.DMA
EXCHANGE_SEMS = [DMA((3, Q, 8)), DMA((3, Q, 8)), DMA((3,)), DMA((Q, 4)), DMA((Q, 4))]
BY_CHANNEL = ((C, I, J), BF16)
BY_ROW = ((I, C, J), BF16)
HALF = (16, C, J)
EVERY = (16, J, J)


def local(
    single_state,
    pair_state,
    residue_mask,
    pair_cotangent,
    outer_norm_gain,
    outer_norm_bias,
    outer_left,
    outer_right,
    outer_proj,
    outer_bias,
    triangle_norm_gain,
    triangle_norm_bias,
    triangle_proj,
    triangle_gate,
    triangle_out_gain,
    triangle_out_bias,
    triangle_out,
):
    me = lax.axis_index("axial")
    weight = residue_mask[0].astype(F32)
    own = lax.dynamic_slice_in_dim(weight, me * I, I)[:, None]
    mask = own * weight[None, :]
    own_wide = jnp.broadcast_to(own, (I, C))
    factor_weight = jnp.concatenate(
        [outer_left, outer_right, jnp.zeros((outer_left.shape[0], C - 2 * B), BF16)], axis=1
    )
    single = single_state[0]
    single_gain, single_bias = outer_norm_gain[None, :], outer_norm_bias[None, :]
    cube = outer_proj.reshape(B, B * C)
    back_weight = jnp.concatenate([triangle_proj, triangle_gate], axis=2)
    front_weight = jnp.swapaxes(back_weight, 1, 2)
    gains = [triangle_norm_gain[t][:, None] for t in range(2)]
    biases = [triangle_norm_bias[t][:, None] for t in range(2)]
    out_gains = [triangle_out_gain[t][:, None] for t in range(2)]
    out_biases = [triangle_out_bias[t][:, None] for t in range(2)]
    fronts = [front_weight[t] for t in range(2)]
    backs = [back_weight[t] for t in range(2)]
    outs = [triangle_out[t] for t in range(2)]

    (every,) = call(
        head_kernel,
        [((J, C), BF16)],
        [DMA((16,)), DMA((16,))],
        (single, single_gain, single_bias, factor_weight, own_wide),
        "head",
        collective=0,
    )
    own_both = lax.dynamic_slice_in_dim(every, me * I, I)
    mixed_scratch = pltpu.VMEM((B * I, C), F32)
    first, left0, right0 = call(
        front_first_kernel,
        [BY_ROW, BY_CHANNEL, BY_CHANNEL],
        [CELLS, CELLS, mixed_scratch],
        (
            pair_state[0],
            every,
            own_both,
            cube,
            mask,
            outer_bias[:, None],
            gains[0],
            biases[0],
            fronts[0],
        ),
        "front_first",
    )
    left0_kept, right0_kept, product0 = call(
        outgoing_kernel,
        [(HALF, BF16), (EVERY, BF16), BY_CHANNEL],
        [pltpu.VMEM(HALF, BF16)] + EXCHANGE_SEMS,
        (left0, right0),
        "outgoing",
        collective=1,
    )
    second, left1, right1 = call(
        middle_kernel,
        [BY_ROW, BY_CHANNEL, BY_CHANNEL],
        [CELLS, CELLS, CELLS],
        (
            product0,
            first,
            mask,
            gains[0],
            biases[0],
            fronts[0],
            out_gains[0],
            out_biases[0],
            outs[0],
            gains[1],
            biases[1],
            fronts[1],
        ),
        "middle",
    )
    sum_scratch = [
        pltpu.VMEM((J, J), F32),
        pltpu.VMEM(HALF, F32),
        pltpu.VMEM(HALF, BF16),
        pltpu.VMEM(HALF, BF16),
    ]
    left1_kept, right1_kept, product1 = call(
        incoming_kernel,
        [(HALF, BF16), (HALF, BF16), BY_CHANNEL],
        [pltpu.VMEM(HALF, BF16)] + sum_scratch + EXCHANGE_SEMS,
        (left1, right1),
        "incoming",
        collective=2,
    )
    cotangent = pair_cotangent[0]
    product_grad1, gate_grad1, out1_sum, small1 = call(
        back_second_kernel,
        [BY_CHANNEL, BY_ROW, ((C, C), F32), ((C, C), F32)],
        [CELLS, CELLS, SUMS, SUMS],
        (
            product1,
            second,
            cotangent,
            gains[1],
            biases[1],
            fronts[1],
            out_gains[1],
            out_biases[1],
            outs[1],
        ),
        "back_second",
    )
    left_grad1, right_grad1 = call(
        incoming_back_kernel,
        [BY_CHANNEL, BY_CHANNEL],
        [pltpu.VMEM(EVERY, BF16), pltpu.VMEM(HALF, BF16), pltpu.VMEM(HALF, BF16)] + EXCHANGE_SEMS,
        (product_grad1, left1_kept, right1_kept),
        "incoming_back",
        collective=3,
    )
    grad_second, product_grad0, gate_grad0, front1_sum, out0_sum, small_middle = call(
        back_middle_kernel,
        [
            BY_ROW,
            BY_CHANNEL,
            BY_ROW,
            ((C, 5 * C), F32),
            ((C, C), F32),
            ((C, C), F32),
        ],
        [CELLS, CELLS, CELLS, CELLS, SUMS, SUMS, SUMS, SUMS],
        (
            left_grad1,
            right_grad1,
            second,
            cotangent,
            gate_grad1,
            product0,
            first,
            mask,
            gains[1],
            biases[1],
            fronts[1],
            backs[1],
            gains[0],
            biases[0],
            fronts[0],
            out_gains[0],
            out_biases[0],
            outs[0],
        ),
        "back_middle",
    )
    left_grad0, right_grad0 = call(
        outgoing_back_kernel,
        [BY_CHANNEL, BY_CHANNEL],
        [pltpu.VMEM(HALF, BF16), pltpu.VMEM(HALF, BF16), pltpu.VMEM(HALF, BF16)]
        + sum_scratch
        + EXCHANGE_SEMS,
        (product_grad0, left0_kept, right0_kept),
        "outgoing_back",
        collective=4,
    )
    pair_gradient, front0_sum, small0, cube_sum, left_single, right_total = call(
        back_first_kernel,
        [
            ((I, J, C), BF16),
            ((C, 5 * C), F32),
            ((C, C), F32),
            ((B * B, C), F32),
            ((I, C), F32),
            ((J, C), F32),
        ],
        [
            CELLS,
            CELLS,
            mixed_scratch,
            mixed_scratch,
            SUMS,
            SUMS,
            SUMS,
            pltpu.VMEM((C, J), F32),
        ],
        (
            left_grad0,
            right_grad0,
            first,
            grad_second,
            gate_grad0,
            mask,
            every,
            own_both,
            cube,
            gains[0],
            biases[0],
            fronts[0],
            backs[0],
        ),
        "back_first",
    )
    small = jnp.concatenate(
        [
            small0[:, :2],
            small_middle[:, 2:4],
            small_middle[:, :2],
            small1[:, :2],
            small0[:, 2:3],
            jnp.zeros((C, C - 9), F32),
        ],
        axis=1,
    )
    scale = 1.0 / float(lax.axis_size("dp") * J)
    part = (PART, C)
    single_gradient, total = call(
        functools.partial(total_kernel, scale),
        [((I, single.shape[1]), BF16), ((16,) + part, BF16)],
        [
            pltpu.VMEM((16,) + part, BF16),
            pltpu.VMEM((16, I, C), F32),
            pltpu.VMEM((8,) + part, BF16),
            pltpu.VMEM((8,) + part, BF16),
            pltpu.VMEM((8,) + part, BF16),
            pltpu.VMEM((8,) + part, BF16),
            DMA((16,)),
            DMA((16,)),
            DMA((2,)),
        ]
        + [DMA((8,))] * 8,
        (
            right_total,
            left_single,
            single,
            single_gain,
            single_bias,
            factor_weight,
            own_wide,
            front0_sum,
            front1_sum,
            out0_sum,
            out1_sum,
            cube_sum,
            small,
        ),
        "total",
        collective=5,
    )
    unpacked = call(
        unpack_kernel,
        [
            ((8, C), F32),
            ((8, C), F32),
            (outer_left.shape, F32),
            (outer_right.shape, F32),
            (outer_proj.shape, F32),
            ((1, C), F32),
            ((2, C), F32),
            ((2, C), F32),
            (triangle_proj.shape, F32),
            (triangle_gate.shape, F32),
            ((2, C), F32),
            ((2, C), F32),
            (triangle_out.shape, F32),
        ],
        [],
        (total.reshape(16 * PART, C),),
        "unpack",
    )
    unpacked = list(unpacked)
    unpacked[0] = unpacked[0].reshape(-1)
    unpacked[1] = unpacked[1].reshape(-1)
    unpacked[5] = unpacked[5].reshape(-1)
    return (single_gradient[None], pair_gradient[None]) + tuple(unpacked)


def solution(mesh):
    whole = P()
    rows = P("dp", "axial", None)
    cells = P("dp", "axial", None, None)
    return jax.shard_map(
        local,
        mesh=mesh,
        in_specs=(rows, cells, P("dp", None), cells) + (whole,) * 13,
        out_specs=(rows, cells) + (whole,) * 13,
        check_vma=False,
    )
```

time: 779 us -> 346 us (0.44); the launches traced: 768 us -> 345 us
  Pallas kernels: 0 us -> 319 us
  waiting for transfers between devices: 313 us -> 0 us
  blocking collectives: 136 us -> 0 us
  other arithmetic: 82.1 us -> 2.27 us
  matrix products: 79.4 us -> 0 us
  local copies, waits for them, and re-layouts: 86 us -> 22.6 us
  starting transfers between devices: 55.3 us -> 0 us
  between operations: 16 us -> 0.86 us
    pallas_call x0 -> x12, Pallas kernels: none -> 319 us  [call(): pl.pallas_call(kernel, out_shape=[jax.ShapeDtypeStruct(shape, dtype) for...]
    psum x1 -> x0, waiting for transfers between devices: 145 us -> none  [local(): lax.psum((gain_sum, bias_sum, left_sum, right_sum, cube_sum.reshape(inner...]
    all_to_all x10 -> x0, waiting for transfers between devices: 117 us -> none  [the longest x2 33 us: core_forward(): lax.all_to_all(left_side, 'axial', split_axis=2, concat_axis=0, tiled=True)]
    dot_general x36 -> x0, matrix products: 79.4 us -> none  [the longest x8 18.1 us: project_back(): jnp.einsum('...d,cd->...c', inputs, matrix, preferred_element_type=jnp.fl...]
    psum x1 -> x0, blocking collectives: 66.4 us -> none  [local(): lax.psum((gain_sum, bias_sum, left_sum, right_sum, cube_sum.reshape(inner...]
    all_to_all x10 -> x0, starting transfers between devices: 55 us -> none  [the longest x2 17.4 us: core_backward(): lax.all_to_all(right_part.astype(jnp.bfloat16), 'axial', split_axis=0, co...]
    reduce_scatter x1 -> x0, waiting for transfers between devices: 50.8 us -> none  [local(): lax.psum_scatter(jnp.einsum('ia,ijc->jac', left_outer, outer_grad, prefer...]
    convert_element_type x20 -> x0, local copies, waits for them, and re-layouts: 48.5 us -> none  [the longest x4 10.1 us: core_backward(): left_grad, right_grad = (lax.all_to_all(left_part.astype(jnp.bfloat16), '...]
  transfers between devices with their start and end apart: 12 -> 0, of which waited for: 12 -> 0; matrix products, arithmetic and copies ran while one was open for 10% -> 0% of each run, Pallas kernels for 0% -> 0%
where the time goes in v1:
time: 346 us; the launch traced here: 345 us
  Pallas kernels  319 us (92%)
  local copies, waits for them, and re-layouts  22.6 us (7%)
    pallas_call x12, Pallas kernels, call(): pl.pallas_call(kernel, out_shape=[jax.ShapeDtypeStruct(shape, dtype) for...  319 us
    unnamed x28, local copies, waits for them, and re-layouts  7.39 us

profile of v1, /device:TPU:1, one launch (start us, length us, event | category | flops | bytes accessed | tf_op | source)
XLA Modules:
  0.0 345.1 jit_solution(1093856982207525699)
XLA Ops:
  2.2 1.0 copy.32
  3.2 1.0 copy.33
  4.3 0.9 maximum_maximum_fusion.weight_ref
  5.2 12.3 %head.1.every_ref = bf16[256,128]{1,0:T(8,128)(2,1)} custom-call(bf16[16,1024]{1,0:T(8,128)(2,1)} %bitcast.52, f32[1,1024]{1,0:T(1,128)} %bitcast.56, f32[1,1024]{1,0:T(1,128)} %bitcast.58, bf16[1024,128]{1,0:T(8,128)(2,1)} %maximum_maximum_fusion.weight_ref, f32[16,128]{1,0:T(8,128)} %broadcast_in_dim.31.own_ref), custom_call_target="tpu_custom_call" | custom-call | tf_op jit(solution)/shard_map/head/pallas_call | solution.py:1153
  17.5 1.3 constant_dynamic-slice_fusion.own_both_ref
  19.4 1.0 constant_dynamic-update-slice_fusion.1
  20.5 0.8 copy.37.front_ref.front0_ref
  21.3 0.7 copy.35.gain_ref.gain0_ref
  22.0 0.7 copy.36.bias_ref.bias0_ref
  22.8 0.8 reshape.48.cube_ref
  23.6 0.7 copy.34.outer_bias_ref
  24.3 13.1 %front_first.1 = (bf16[16,128,256]{2,1,0:T(8,128)(2,1)}, bf16[128,16,256]{2,1,0:T(8,128)(2,1)}, bf16[128,16,256]{2,1,0:T(8,128)(2,1)}) custom-call(bf16[16,256,128]{2,1,0:T(8,128)(2,1)} %bitcast.49, bf16[256,128]{1,0:T(8,128)(2,1)} %head.1.every_ref, bf16[16,128]{1,0:T(8,128)(2,1)} %constant_dynamic-slice_fusion.own_both_ref, ...), custom_call_target="tpu_custom_call" | custom-call | tf_op jit(solution)/shard_map/front_first/pallas_call | solution.py:1153
  37.5 46.2 %outgoing.1 = (bf16[16,128,256]{2,1,0:T(8,128)(2,1)}, bf16[16,256,256]{2,1,0:T(8,128)(2,1)}, bf16[128,16,256]{2,1,0:T(8,128)(2,1)}) custom-call(bf16[128,16,256]{2,1,0:T(8,128)(2,1)} %get-tuple-element.62.left_ref, bf16[128,16,256]{2,1,0:T(8,128)(2,1)} %get-tuple-element.63.right_ref), custom_call_target="tpu_custom_call" | custom-call | tf_op jit(solution)/shard_map/outgoing/pallas_call | solution.py:1153
  83.7 0.8 copy.45.front1_ref.front_ref
  86.0 0.7 copy.41.out_gain0_ref
  86.7 0.7 copy.42.out_bias0_ref
  88.1 14.8 %middle.1 = (bf16[16,128,256]{2,1,0:T(8,128)(2,1)}, bf16[128,16,256]{2,1,0:T(8,128)(2,1)}, bf16[128,16,256]{2,1,0:T(8,128)(2,1)}) custom-call(bf16[128,16,256]{2,1,0:T(8,128)(2,1)} %get-tuple-element.64.product_ref, bf16[16,128,256]{2,1,0:T(8,128)(2,1)} %get-tuple-element.65.first_ref, f32[16,256]{1,0:T(8,128)} %broadcast_multiply_fusion.mask_ref, ...), custom_call_target="tpu_custom_call" | custom-call | tf_op jit(solution)/shard_map/middle/pallas_call | solution.py:1153
  102.9 47.7 %incoming.1 = (bf16[16,128,256]{2,1,0:T(8,128)(2,1)}, bf16[16,128,256]{2,1,0:T(8,128)(2,1)}, bf16[128,16,256]{2,1,0:T(8,128)(2,1)}) custom-call(bf16[128,16,256]{2,1,0:T(8,128)(2,1)} %get-tuple-element.66.left_ref, bf16[128,16,256]{2,1,0:T(8,128)(2,1)} %get-tuple-element.67.right_ref), custom_call_target="tpu_custom_call" | custom-call | tf_op jit(solution)/shard_map/incoming/pallas_call | solution.py:1153
  150.5 0.7 copy.49.out_gain_ref
  151.3 0.7 copy.50.out_bias_ref
  152.0 12.0 %back_second.1 = (bf16[128,16,256]{2,1,0:T(8,128)(2,1)}, bf16[16,128,256]{2,1,0:T(8,128)(2,1)}, f32[128,128]{1,0:T(8,128)}, f32[128,128]{1,0:T(8,128)}) custom-call(bf16[128,16,256]{2,1,0:T(8,128)(2,1)} %get-tuple-element.68.product_ref, bf16[16,128,256]{2,1,0:T(8,128)(2,1)} %get-tuple-element.69.second_ref, bf16[16,256,128]{2,1,0:T(8,128)(2,1)} %bitcast.46, ...), custom_call_target="tpu_custom_call" | custom-call | tf_op jit(solution)/shard_map/back_second/pallas_call | solution.py:1153
  164.0 46.9 %incoming_back.1 = (bf16[128,16,256]{2,1,0:T(8,128)(2,1)}, bf16[128,16,256]{2,1,0:T(8,128)(2,1)}) custom-call(bf16[128,16,256]{2,1,0:T(8,128)(2,1)} %get-tuple-element.70.grad_ref, bf16[16,128,256]{2,1,0:T(8,128)(2,1)} %get-tuple-element.71.left_kept, bf16[16,128,256]{2,1,0:T(8,128)(2,1)} %get-tuple-element.72.right_kept), custom_call_target="tpu_custom_call" | custom-call | tf_op jit(solution)/shard_map/incoming_back/pallas_call | solution.py:1153
  210.9 0.8 slice_bitcast_fusion
  211.6 22.5 %back_middle.1 = (bf16[16,128,256]{2,1,0:T(8,128)(2,1)}, bf16[128,16,256]{2,1,0:T(8,128)(2,1)}, bf16[16,128,256]{2,1,0:T(8,128)(2,1)}, f32[128,640]{1,0:T(8,128)...) custom-call(bf16[128,16,256]{2,1,0:T(8,128)(2,1)} %get-tuple-element.73.left_ref, ...), custom_call_target="tpu_custom_call" | custom-call | tf_op jit(solution)/shard_map/back_middle/pallas_call | solution.py:1153
  234.1 45.0 %outgoing_back.1 = (bf16[128,16,256]{2,1,0:T(8,128)(2,1)}, bf16[128,16,256]{2,1,0:T(8,128)(2,1)}) custom-call(bf16[128,16,256]{2,1,0:T(8,128)(2,1)} %get-tuple-element.76.grad_ref, bf16[16,128,256]{2,1,0:T(8,128)(2,1)} %get-tuple-element.77.left_kept, bf16[16,256,256]{2,1,0:T(8,128)(2,1)} %get-tuple-element.78.right_kept), custom_call_target="tpu_custom_call" | custom-call | tf_op jit(solution)/shard_map/outgoing_back/pallas_call | solution.py:1153
  279.1 17.4 %back_first.1 = (bf16[16,256,128]{2,1,0:T(8,128)(2,1)}, f32[128,640]{1,0:T(8,128)}, f32[128,128]{1,0:T(8,128)}, f32[1024,128]{1,0:T(8,128)}, f32[16,128]{1,0:T(8,128)}, /*index=5*/f32[256,128]{1,0:T(8,128)}) custom-call(bf16[128,16,256]{2,1,0:T(8,128)(2,1)} %get-tuple-element.79.left_ref, bf16[128,16,256]{2,1,0:T(8,128)(2,1)} %get-tuple-element.80.right_ref, ...), custom_call_target="tpu_custom_call" | custom-call | tf_op jit(solution)/shard_map/back_first/pallas_call | solution.py:1153
  296.5 0.9 slice.75
  297.5 1.6 concatenate.11.small_ref
  299.1 38.8 %total.1 = (bf16[16,1024]{1,0:T(8,128)(2,1)}, bf16[16,208,128]{2,1,0:T(8,128)(2,1)}) custom-call(f32[256,128]{1,0:T(8,128)} %get-tuple-element.83.right_total_ref, f32[16,128]{1,0:T(8,128)} %get-tuple-element.84.left_single_ref, bf16[16,1024]{1,0:T(8,128)(2,1)} %bitcast.53, f32[1,1024]{1,0:T(1,128)} %bitcast.57, f32[1,1024]{1,0:T(1,128)} %bitcast.59, ...), custom_call_target="tpu_custom_call" | custom-call | tf_op jit(solution)/shard_map/total/pallas_call | solution.py:1153
  337.9 2.8 unpack.1
  340.7 1.9 copy.62
  342.6 1.9 copy.63
  (40 shorter events, 5.1 us)
Async XLA Ops:
  0.6 19.7 %copy-start.3 = (bf16[2,128,128]{2,1,0:T(8,128)(2,1)S(1)}, bf16[2,128,128]{2,1,0:T(8,128)(2,1)}, u32[]{:S(2)}) copy-start(bf16[2,128,128]{2,1,0:T(8,128)(2,1)} %param.30) | copy-start | bytes 196612
  0.7 20.6 %copy-start.6 = (f32[2,128]{1,0:T(2,128)S(1)}, f32[2,128]{1,0:T(2,128)}, u32[]{:S(2)}) copy-start(f32[2,128]{1,0:T(2,128)} %param.27) | copy-start | bytes 3076
  0.7 21.4 %copy-start.7 = (f32[2,128]{1,0:T(2,128)S(1)}, f32[2,128]{1,0:T(2,128)}, u32[]{:S(2)}) copy-start(f32[2,128]{1,0:T(2,128)} %param.28) | copy-start | bytes 3076
  0.7 22.1 %copy-start = (bf16[1024,128]{1,0:T(8,128)(2,1)S(1)}, bf16[1024,128]{1,0:T(8,128)(2,1)}, u32[]{:S(2)}) copy-start(bf16[1024,128]{1,0:T(8,128)(2,1)} %param.25) | copy-start | bytes 786436
  0.7 22.9 %copy-start.10 = (f32[128]{0:T(128)S(1)}, f32[128]{0:T(128)}, u32[]{:S(2)}) copy-start(f32[128]{0:T(128)} %param.26) | copy-start | bytes 1540
  24.3 61.6 %copy-start.8 = (f32[2,128]{1,0:T(2,128)S(1)}, f32[2,128]{1,0:T(2,128)}, u32[]{:S(2)}) copy-start(f32[2,128]{1,0:T(2,128)} %param.31) | copy-start | bytes 3076
  24.3 62.4 %copy-start.9 = (f32[2,128]{1,0:T(2,128)S(1)}, f32[2,128]{1,0:T(2,128)}, u32[]{:S(2)}) copy-start(f32[2,128]{1,0:T(2,128)} %param.32) | copy-start | bytes 3076
  24.3 63.1 %copy-start.4 = (bf16[2,128,128]{2,1,0:T(8,128)(2,1)S(1)}, bf16[2,128,128]{2,1,0:T(8,128)(2,1)}, u32[]{:S(2)}) copy-start(bf16[2,128,128]{2,1,0:T(8,128)(2,1)} %param.33) | copy-start | bytes 196612
  279.1 18.3 %copy-start.1 = (f32[128,128]{1,0:T(8,128)S(1)}, f32[128,128]{1,0:T(8,128)}, u32[]{:S(2)}) copy-start(f32[128,128]{1,0:T(8,128)} %get-tuple-element.91) | copy-start | bytes 196612
  279.1 18.4 %copy-start.2 = (f32[128,128]{1,0:T(8,128)S(1)}, f32[128,128]{1,0:T(8,128)}, u32[]{:S(2)}) copy-start(f32[128,128]{1,0:T(8,128)} %get-tuple-element.92) | copy-start | bytes 196612
  337.9 6.5 %copy-start.5 = (bf16[16,1024]{1,0:T(8,128)(2,1)S(1)}, bf16[16,1024]{1,0:T(8,128)(2,1)}, u32[]{:S(2)}) copy-start(bf16[16,1024]{1,0:T(8,128)(2,1)} %get-tuple-element.93) | copy-start | bytes 98308

commit v2 on v1

v2 whole, which is shorter than its diff:
```python
import functools

import jax
import jax.numpy as jnp
from jax import lax
from jax.experimental import pallas as pl
from jax.experimental.pallas import tpu as pltpu
from jax.sharding import PartitionSpec as P

EPSILON = 1e-05
F32 = jnp.float32
BF16 = jnp.bfloat16
MESH = pl.DeviceIdType.MESH
C = 128
I = 16
J = 256
B = 32
Q = 2
CQ = 8
PART = 208
VMEM_LIMIT = 60 * 2**20


def nn(a, b):
    return lax.dot_general(a, b, (((1,), (0,)), ((), ())), preferred_element_type=F32)


def nt(a, b):
    return lax.dot_general(a, b, (((1,), (1,)), ((), ())), preferred_element_type=F32)


def tn(a, b):
    return lax.dot_general(a, b, (((0,), (0,)), ((), ())), preferred_element_type=F32)


def sigmoid(x):
    return 0.5 * jnp.tanh(0.5 * x) + 0.5


def norm(x, axis=0):
    centred = x - jnp.mean(x, axis=axis, keepdims=True)
    variance = jnp.mean(centred * centred, axis=axis, keepdims=True)
    inverse = lax.rsqrt(variance + EPSILON)
    return centred * inverse, inverse


def norm_back(scaled, standard, inverse, axis=0):
    first = jnp.mean(scaled, axis=axis, keepdims=True)
    second = jnp.mean(scaled * standard, axis=axis, keepdims=True)
    return inverse * (scaled - first - standard * second)


def put_pair(cells, p, value):
    cells[pl.ds(2 * p, C, stride=I), :] = value[:, :C]
    cells[pl.ds(2 * p + 1, C, stride=I), :] = value[:, C:]


def get_pair(cells, p):
    return side_by_side(cells[pl.ds(2 * p, C, stride=I), :], cells[pl.ds(2 * p + 1, C, stride=I), :])


def side_by_side(a, b):
    return jnp.concatenate([a, b], axis=1)


def lanes(h):
    return slice(h * C, (h + 1) * C)


def cells_out(cells, out_ref, h):
    def step(n, _):
        part = cells[pl.ds(pl.multiple_of(n * 256, 256), 256), :]
        out_ref[pl.ds(n * 16, 16), :, lanes(h)] = part.reshape(16, I, C).astype(BF16)
        return 0

    lax.fori_loop(0, 8, step, 0)


def cells_in(in_ref, cells, h):
    def step(n, _):
        part = in_ref[pl.ds(n * 16, 16), :, lanes(h)]
        cells[pl.ds(pl.multiple_of(n * 256, 256), 256), :] = part.astype(F32).reshape(256, C)
        return 0

    lax.fori_loop(0, 8, step, 0)


def rows_in(ref, p, h):
    return side_by_side(
        ref[2 * p, lanes(h), :].astype(F32).T, ref[2 * p + 1, lanes(h), :].astype(F32).T
    )


def mask_pair(mask_ref, p, h):
    return side_by_side(
        mask_ref[h, pl.ds(2 * p, 1), :], mask_ref[h, pl.ds(2 * p + 1, 1), :]
    )


def wide(ref):
    return side_by_side(ref[...], ref[...])


def send_factors(pair_in, mask_row, gain, bias, front_ref, left_cells, right_cells, p):
    standard, _ = norm(pair_in)
    normed = (standard * gain + bias).astype(BF16)
    projected = nn(front_ref[: 4 * C, :], normed)
    put_pair(left_cells, p, mask_row * sigmoid(projected[:C]) * projected[C : 2 * C])
    put_pair(right_cells, p, mask_row * sigmoid(projected[2 * C : 3 * C]) * projected[3 * C :])


def over_pairs(body, hook=None, at=4):
    def step(p, _):
        if hook is not None:
            pl.when(p == at)(hook)
        body(p)
        return 0

    lax.fori_loop(0, I // 2, step, 0)


def head_kernel(single_ref, gain_ref, bias_ref, weight_ref, own_ref, every_ref, send_sem, recv_sem):
    me = lax.axis_index("axial")
    dp = lax.axis_index("dp")
    barrier = pltpu.get_barrier_semaphore()

    def greet(t, _):
        pl.semaphore_signal(
            barrier, inc=1, device_id=(dp, lax.rem(me + t, 16)), device_id_type=MESH
        )
        return 0

    lax.fori_loop(1, 16, greet, 0)
    standard, _ = norm(single_ref[...].astype(F32), axis=1)
    normed = (standard * gain_ref[...] + bias_ref[...]).astype(BF16)
    both = nn(normed, weight_ref[...]) * own_ref[...]
    mine = pl.ds(pl.multiple_of(me * I, I), I)
    every_ref[mine, :] = both.astype(BF16)
    pl.semaphore_wait(barrier, 15)

    def copy(t):
        return pltpu.make_async_remote_copy(
            src_ref=every_ref.at[mine],
            dst_ref=every_ref.at[mine],
            send_sem=send_sem.at[t],
            recv_sem=recv_sem.at[t],
            device_id=(dp, lax.rem(me + t, 16)),
            device_id_type=MESH,
        )

    def begin(t, _):
        copy(t).start()
        return 0

    def finish(t, _):
        copy(t).wait()
        return 0

    lax.fori_loop(1, 16, begin, 0)
    lax.fori_loop(1, 16, finish, 0)


def mixed_rows(own_left, cube_ref, mixed_cells):
    for b in range(B):
        mixed_cells[b * I : (b + 1) * I, :] = nn(own_left, cube_ref[:, b * C : (b + 1) * C])


def back_out(cotangent, product, pair_in, gain, bias, front_ref, out_gain, out_bias, out_ref, sums):
    out_sum, out_gain_sum, out_bias_sum = sums
    product_standard, product_inverse = norm(product)
    product_norm = (product_standard * out_gain + out_bias).astype(BF16)
    linear = tn(out_ref[...], product_norm)
    standard, _ = norm(pair_in)
    normed = (standard * gain + bias).astype(BF16)
    gate = sigmoid(nn(front_ref[4 * C :, :], normed))
    linear_grad = (cotangent * gate).astype(BF16)
    gate_grad = (cotangent * linear * gate * (1.0 - gate)).astype(BF16)
    out_sum[...] += nt(product_norm, linear_grad)
    norm_grad = nn(out_ref[...], linear_grad)
    out_gain_sum[...] += norm_grad * product_standard
    out_bias_sum[...] += norm_grad
    return gate_grad, norm_back(norm_grad * out_gain, product_standard, product_inverse)


def back_in(
    cotangent,
    gate_grad,
    left_grad,
    right_grad,
    pair_in,
    mask_row,
    gain,
    bias,
    front_ref,
    back_ref,
    sums,
):
    front_sum, gain_sum, bias_sum = sums
    standard, inverse = norm(pair_in)
    normed = (standard * gain + bias).astype(BF16)
    projected = nn(front_ref[: 4 * C, :], normed)
    grads = []
    for at, side in ((0, left_grad), (2 * C, right_grad)):
        gate = sigmoid(projected[at : at + C])
        masked = side * mask_row * gate
        grads.append((masked * projected[at + C : at + 2 * C] * (1.0 - gate)).astype(BF16))
        grads.append(masked.astype(BF16))
    grads = jnp.concatenate(grads + [gate_grad], axis=0)
    front_sum[...] += nt(normed, grads)
    normed_grad = nn(back_ref[...], grads)
    gain_sum[...] += normed_grad * standard
    bias_sum[...] += normed_grad
    return (cotangent + norm_back(normed_grad * gain, standard, inverse)).astype(BF16)


def clear(*refs):
    for ref in refs:
        ref[...] = jnp.zeros(ref.shape, ref.dtype)


def columns(*refs):
    made = [jnp.sum(ref[...], axis=1, keepdims=True) for ref in refs]
    lane = lax.broadcasted_iota(jnp.int32, (C, C), 1)
    total = jnp.zeros((C, C), F32)
    for n, column in enumerate(made):
        total = jnp.where(lane == n, column, total)
    return total


class Place:
    def __init__(self):
        self.me = lax.axis_index("axial")
        self.dp = lax.axis_index("dp")
        self.half = lax.rem(self.me // 2, 2)
        self.group = (self.me // 4) * 2 + lax.rem(self.me, 2)
        self.other = self.me + 2 - 4 * self.half

    def axial(self, group):
        return (group // 2) * 4 + self.half * 2 + lax.rem(group, 2)

    def peer(self, t):
        return lax.rem(self.group + t, 8)

    def greet(self):
        barrier = pltpu.get_barrier_semaphore()

        def signal(t, _):
            pl.semaphore_signal(
                barrier,
                inc=1,
                device_id=(self.dp, self.axial(self.peer(t))),
                device_id_type=MESH,
            )
            return 0

        lax.fori_loop(1, 8, signal, 0)
        pl.semaphore_signal(barrier, inc=1, device_id=(self.dp, self.other), device_id_type=MESH)
        pl.semaphore_wait(barrier, 8)

    def copy(self, source, target, send_sem, recv_sem, axial):
        return pltpu.make_async_remote_copy(
            src_ref=source,
            dst_ref=target,
            send_sem=send_sem,
            recv_sem=recv_sem,
            device_id=(self.dp, axial),
            device_id_type=MESH,
        )


def loop(first, last, do):
    def step(n, _):
        do(n)
        return 0

    lax.fori_loop(first, last, step, 0)


def rows_of(at, count=I):
    return pl.ds(pl.multiple_of(at, 16), count)


def piece(q):
    return pl.ds(q * CQ, CQ)


def wait_bytes(ref, sem):
    pltpu.make_async_copy(ref, ref, sem).wait()


class Travel:
    def __init__(self, place, source, target, sems, at):
        self.place, self.source, self.target = place, source, target
        self.send_sem, self.recv_sem, self.local_sem = (sem.at[at] for sem in sems)

    def send(self, h):
        pltpu.make_async_copy(*self.ends(h, self.place.group, slice(None)), self.local_sem.at[h]).start()
        for q in range(Q):
            self.send_piece(h, q)

    def send_piece(self, h, q):
        def start(t):
            group = self.place.peer(t)
            self.place.copy(
                *self.ends(h, group, q),
                self.send_sem,
                self.recv_sem.at[h, q],
                self.place.axial(group),
            ).start()

        loop(1, 8, start)

    def local(self, h):
        pltpu.make_async_copy(*self.ends(h, self.place.group, slice(None)), self.local_sem.at[h]).start()

    def here(self, h):
        pltpu.make_async_copy(*self.ends(h, self.place.group, slice(None)), self.local_sem.at[h]).wait()

    def arrive(self, h, q):
        wait_bytes(self.by_channel().at[: 7 * CQ, :, lanes(h)], self.recv_sem.at[h, q])

    def arrive_half(self, h):
        self.here(h)
        for q in range(Q):
            self.arrive(h, q)

    def sent(self):
        wait_bytes(self.by_channel().at[: 7 * 16], self.send_sem)


class Spread(Travel):
    def __init__(self, place, source, target, row, sems, at):
        super().__init__(place, source, target, sems, at)
        self.row = row

    def by_channel(self):
        return self.source

    def ends(self, h, group, q):
        if isinstance(q, slice):
            channels, kept = pl.ds(group * 16, 16), q
        else:
            channels, kept = pl.ds(group * 16 + q * CQ, CQ), piece(q)
        return (
            self.source.at[channels, :, lanes(h)],
            self.target.at[kept, rows_of(self.row), lanes(h)],
        )


class Collect(Travel):
    def by_channel(self):
        return self.target

    def ends(self, h, group, q):
        mine = self.place.group * 16
        if isinstance(q, slice):
            channels, kept = pl.ds(mine, 16), q
        else:
            channels, kept = pl.ds(mine + q * CQ, CQ), piece(q)
        return (
            self.source.at[kept, rows_of(group * I), lanes(h)],
            self.target.at[channels, :, lanes(h)],
        )


class Swap:
    def __init__(self, place, sems, at):
        self.place = place
        self.send_sem, self.recv_sem = (sem.at[at] for sem in sems)

    def rows(self, ref, h, q, r):
        for x in (2 * r, 2 * r + 1):
            block = ref.at[piece(q), rows_of(x * 64 + self.place.half * 32, 32), lanes(h)]
            self.place.copy(
                block, block, self.send_sem, self.recv_sem.at[h, q, r], self.place.other
            ).start()

    def sums(self, sent, received, h, q, r):
        where = (piece(q), slice(64 * r, 64 * r + 64), lanes(h))
        self.place.copy(
            sent.at[where],
            received.at[where],
            self.send_sem,
            self.recv_sem.at[h, q, r],
            self.place.other,
        ).start()

    def arrive(self, ref, h, q, r):
        wait_bytes(ref.at[piece(q), :64, lanes(h)], self.recv_sem.at[h, q, r])

    def sent(self, ref):
        wait_bytes(ref, self.send_sem)


def split_rows(place, whole, kept, sent, channel, r):
    for n in range(2):
        to = slice(64 * r + 32 * n, 64 * r + 32 * n + 32)
        kept[channel, to, :] = whole[rows_of(n * 64 + place.half * 32, 32), :]
        sent[channel, to, :] = whole[rows_of(n * 64 + 32 - place.half * 32, 32), :].astype(BF16)


def trunk_kernel(
    pair_ref,
    cotangent_ref,
    every_ref,
    cube_ref,
    mask_ref,
    outer_bias_ref,
    norm_gain_ref,
    norm_bias_ref,
    out_gain_ref,
    out_bias_ref,
    front_ref,
    back_ref,
    out_ref,
    pair_grad_ref,
    front0_sum,
    front1_sum,
    out0_sum,
    out1_sum,
    small_ref,
    cube_sum_ref,
    left_single_ref,
    right_total_ref,
    first,
    second,
    gate_grad0,
    gate_grad1,
    grad_second,
    sends,
    arrived,
    staged,
    left0,
    right0,
    left1,
    right1,
    grad1,
    grad0,
    kept_sum,
    sent_sum,
    received_sum,
    cells,
    mixed_cells,
    outer_cells,
    wides,
    sums,
    right_total,
    whole,
    send_sem,
    recv_sem,
    local_sem,
    half_send,
    half_recv,
):
    place = Place()
    place.greet()
    for t in range(2):
        for n, ref in enumerate((norm_gain_ref, norm_bias_ref, out_gain_ref, out_bias_ref)):
            wides[4 * t + n] = jnp.broadcast_to(ref[t : t + 1, :], (C, C)).T
    wides[8] = jnp.broadcast_to(outer_bias_ref[...], (C, C)).T
    clear(sums, front0_sum, front1_sum, out0_sum, out1_sum, right_total, outer_cells)
    right_rows = every_ref[...].astype(F32).T[B : 2 * B].astype(BF16)
    own_left = every_ref[rows_of(place.me * I), :][:, :B]
    mixed_rows(own_left, cube_ref, mixed_cells)

    sems = (send_sem, recv_sem, local_sem)
    swap_sems = (half_send, half_recv)
    me_row, group_row = place.me * I, place.group * I
    travel = [
        Spread(place, sends.at[0], left0, group_row, sems, 0),
        Spread(place, sends.at[1], right0, me_row, sems, 1),
        Collect(place, staged.at[0], arrived.at[0], sems, 2),
        Spread(place, sends.at[2], left1, group_row, sems, 3),
        Spread(place, sends.at[3], right1, group_row, sems, 4),
        Collect(place, staged.at[1], arrived.at[1], sems, 5),
        Spread(place, sends.at[4], grad1, me_row, sems, 6),
        Collect(place, staged.at[2], arrived.at[2], sems, 7),
        Collect(place, staged.at[3], arrived.at[3], sems, 8),
        Spread(place, sends.at[5], grad0, group_row, sems, 9),
        Collect(place, staged.at[4], arrived.at[4], sems, 10),
        Collect(place, staged.at[5], arrived.at[5], sems, 11),
    ]
    (
        send_left0,
        send_right0,
        send_product0,
        send_left1,
        send_right1,
        send_product1,
        send_grad1,
        send_left_grad1,
        send_right_grad1,
        send_grad0,
        send_left_grad0,
        send_right_grad0,
    ) = travel
    swaps = [Swap(place, swap_sems, n) for n in range(4)]

    def over_channels(q, do):
        loop(q * CQ, (q + 1) * CQ, do)

    def front_first(h, hook=None):
        gain, bias, outer_bias = wide(wides.at[0]), wide(wides.at[1]), wide(wides.at[8])

        def body(p):
            mask_row = mask_pair(mask_ref, p, h)
            mixed = [mixed_cells[pl.ds(2 * p + n, B, stride=I), :].astype(BF16) for n in range(2)]
            term = side_by_side(*[tn(m, right_rows[:, lanes(h)]) for m in mixed]) + outer_bias
            value = (rows_in(pair_ref, p, h) + mask_row * term).astype(BF16)
            first[h, p] = value
            send_factors(
                value.astype(F32), mask_row, gain, bias, front_ref.at[0], cells.at[0], cells.at[1], p
            )

        over_pairs(body, hook)
        cells_out(cells.at[1], sends.at[1], h)
        send_right0.send(h)
        cells_out(cells.at[0], sends.at[0], h)
        send_left0.send(h)

    def forward(travelling, ref, swap, h):
        travelling.here(h)
        if h == 0:
            for q in range(Q):
                travelling.arrive(h, q)
                for r in range(2):
                    swap.rows(ref, h, q, r)
        else:
            for q in range(Q):
                travelling.arrive(h, q)
                swap.rows(ref, h, q, 0)
            for q in range(Q):
                swap.rows(ref, h, q, 1)

    front_first(0)
    front_first(1, lambda: forward(send_right0, right0, swaps[0], 0))
    forward(send_right0, right0, swaps[0], 1)
    send_left0.arrive_half(0)
    send_left0.arrive_half(1)
    for h in range(2):
        for q in range(Q):
            for n in range(2):
                swaps[0].arrive(right0, n, q, h)

            def multiply(c):
                staged[0, c, :, lanes(h)] = nt(left0[c], right0[c, lanes(h), :]).astype(BF16)

            over_channels(q, multiply)
            send_product0.send_piece(h, q)
        send_product0.local(h)

    def middle(h):
        send_product0.arrive_half(h)
        cells_in(arrived.at[0], cells.at[2], h)
        gain0, bias0 = wide(wides.at[0]), wide(wides.at[1])
        out_gain0, out_bias0 = wide(wides.at[2]), wide(wides.at[3])
        gain1, bias1 = wide(wides.at[4]), wide(wides.at[5])

        def body(p):
            product_standard, _ = norm(get_pair(cells.at[2], p))
            product_norm = (product_standard * out_gain0 + out_bias0).astype(BF16)
            linear = tn(out_ref[0], product_norm)
            value = first[h, p].astype(F32)
            standard, _ = norm(value)
            normed = (standard * gain0 + bias0).astype(BF16)
            gate = sigmoid(nn(front_ref[0, 4 * C :, :], normed))
            value = (value + gate * linear).astype(BF16)
            second[h, p] = value
            send_factors(
                value.astype(F32),
                mask_pair(mask_ref, p, h),
                gain1,
                bias1,
                front_ref.at[1],
                cells.at[0],
                cells.at[1],
                p,
            )

        over_pairs(body)
        for n, way in ((0, send_left1), (1, send_right1)):
            cells_out(cells.at[n], sends.at[2 + n], h)
            way.local(h)
        for q in range(Q):
            send_left1.send_piece(h, q)
            send_right1.send_piece(h, q)

    middle(0)
    middle(1)
    for way in (send_left1, send_right1):
        way.here(0)
        way.here(1)
    for q in range(Q):
        for way in (send_left1, send_right1):
            for h in range(2):
                way.arrive(h, q)

        def multiply_sums(c):
            for r in range(2):
                whole[...] = tn(left1[c, :, lanes(r)], right1[c])
                split_rows(place, whole, kept_sum, sent_sum.at[0], c, r)

        over_channels(q, multiply_sums)
        for r in range(2):
            swaps[1].sums(sent_sum.at[0], received_sum.at[0], 0, q, r)
    for q in range(Q):
        for r in range(2):
            swaps[1].sums(sent_sum.at[0], received_sum.at[0], 1, q, r)

    def add_halves(swap, received, target, way, h):
        for q in range(Q):
            for r in range(2):
                swap.arrive(received, h, q, r)

            def add(c):
                target[c, :, lanes(h)] = (
                    kept_sum[c, :, lanes(h)] + received[c, :, lanes(h)].astype(F32)
                ).astype(BF16)

            over_channels(q, add)
            way.send_piece(h, q)
        way.local(h)

    def back_second(h, hook=None):
        send_product1.arrive_half(h)
        cells_in(arrived.at[1], cells.at[2], h)
        gain, bias = wide(wides.at[4]), wide(wides.at[5])
        out_gain, out_bias = wide(wides.at[6]), wide(wides.at[7])

        def body(p):
            gate_grad, product_grad = back_out(
                rows_in(cotangent_ref, p, h),
                get_pair(cells.at[2], p),
                second[h, p].astype(F32),
                gain,
                bias,
                front_ref.at[1],
                out_gain,
                out_bias,
                out_ref.at[1],
                (out1_sum, sums.at[6], sums.at[7]),
            )
            gate_grad1[h, p] = gate_grad
            put_pair(cells.at[3], p, product_grad)

        over_pairs(body, hook)
        cells_out(cells.at[3], sends.at[4], h)
        send_grad1.send(h)

    add_halves(swaps[1], received_sum.at[0], staged.at[1], send_product1, 0)
    back_second(0)
    add_halves(swaps[1], received_sum.at[0], staged.at[1], send_product1, 1)
    forward(send_grad1, grad1, swaps[2], 0)
    back_second(1)
    forward(send_grad1, grad1, swaps[2], 1)
    for h in range(2):
        for q in range(Q):
            for r in range(2):
                if h == 0 or r == 1:
                    swaps[2].arrive(grad1, h, q, r)

            def right_back(c):
                staged[3, c, :, lanes(h)] = nn(left1[c], grad1[c, :, lanes(h)]).astype(BF16)

            over_channels(q, right_back)
            send_right_grad1.send_piece(h, q)
        send_right_grad1.local(h)
        for q in range(Q):
            if h == 0:
                swaps[2].arrive(grad1, 1, q, 0)

            def left_back(c):
                staged[2, c, :, lanes(h)] = nt(right1[c], grad1[c, lanes(h), :]).astype(BF16)

            over_channels(q, left_back)
            send_left_grad1.send_piece(h, q)
        send_left_grad1.local(h)

    def back_middle(h, hook=None):
        send_left_grad1.arrive_half(h)
        send_right_grad1.arrive_half(h)
        cells_in(arrived.at[2], cells.at[0], h)
        cells_in(arrived.at[3], cells.at[1], h)
        cells_in(arrived.at[0], cells.at[2], h)
        gain1, bias1, gain0, bias0 = (wide(wides.at[n]) for n in (4, 5, 0, 1))
        out_gain0, out_bias0 = wide(wides.at[2]), wide(wides.at[3])

        def body(p):
            value = back_in(
                rows_in(cotangent_ref, p, h),
                gate_grad1[h, p],
                get_pair(cells.at[0], p),
                get_pair(cells.at[1], p),
                second[h, p].astype(F32),
                mask_pair(mask_ref, p, h),
                gain1,
                bias1,
                front_ref.at[1],
                back_ref.at[1],
                (front1_sum, sums.at[4], sums.at[5]),
            )
            grad_second[h, p] = value
            gate_grad, product_grad = back_out(
                value.astype(F32),
                get_pair(cells.at[2], p),
                first[h, p].astype(F32),
                gain0,
                bias0,
                front_ref.at[0],
                out_gain0,
                out_bias0,
                out_ref.at[0],
                (out0_sum, sums.at[2], sums.at[3]),
            )
            gate_grad0[h, p] = gate_grad
            put_pair(cells.at[3], p, product_grad)

        over_pairs(body, hook)
        cells_out(cells.at[3], sends.at[5], h)
        send_grad0.send(h)

    def right_sums(r):
        send_grad0.here(r)
        for q in range(Q):
            send_grad0.arrive(r, q)

            def multiply_back(c):
                whole[...] = tn(grad0[c, :, lanes(r)], left0[c])
                split_rows(place, whole, kept_sum, sent_sum.at[1], c, r)

            over_channels(q, multiply_back)
            swaps[3].sums(sent_sum.at[1], received_sum.at[1], 0, q, r)
            if r == 0:
                swaps[3].sums(sent_sum.at[1], received_sum.at[1], 1, q, r)
        if r == 1:
            for q in range(Q):
                swaps[3].sums(sent_sum.at[1], received_sum.at[1], 1, q, r)

    back_middle(0)
    back_middle(1, lambda: right_sums(0))
    right_sums(1)
    for h in range(2):
        for q in range(Q):

            def left_back_out(c):
                staged[4, c, :, lanes(h)] = nn(grad0[c], right0[c, :, lanes(h)]).astype(BF16)

            over_channels(q, left_back_out)
            send_left_grad0.send_piece(h, q)
        send_left_grad0.local(h)

    def back_first(h):
        send_left_grad0.arrive_half(h)
        send_right_grad0.arrive_half(h)
        cells_in(arrived.at[4], cells.at[0], h)
        cells_in(arrived.at[5], cells.at[1], h)
        gain, bias = wide(wides.at[0]), wide(wides.at[1])

        def body(p):
            mask_row = mask_pair(mask_ref, p, h)
            value = back_in(
                grad_second[h, p].astype(F32),
                gate_grad0[h, p],
                get_pair(cells.at[0], p),
                get_pair(cells.at[1], p),
                first[h, p].astype(F32),
                mask_row,
                gain,
                bias,
                front_ref.at[0],
                back_ref.at[0],
                (front0_sum, sums.at[0], sums.at[1]),
            ).astype(F32)
            outer_grad = value * mask_row
            sums[8] += outer_grad
            outer_grad = outer_grad.astype(BF16)
            for n in range(2):
                pair_grad_ref[2 * p + n, lanes(h), :] = value[:, lanes(n)].T.astype(BF16)
                grad_row = outer_grad[:, lanes(n)]
                rows = pl.ds(2 * p + n, B, stride=I)
                outer_cells[rows, :] += nt(right_rows[:, lanes(h)], grad_row)
                mixed_left = mixed_cells[rows, :].astype(BF16)
                right_total[:B, lanes(h)] += nn(mixed_left, grad_row)

        over_pairs(body)

    add_halves(swaps[3], received_sum.at[1], staged.at[5], send_right_grad0, 0)
    back_first(0)
    add_halves(swaps[3], received_sum.at[1], staged.at[5], send_right_grad0, 1)
    back_first(1)

    small_ref[...] = columns(*[sums.at[n] for n in range(9)])
    left_single = jnp.zeros((I, B), F32)
    for b in range(B):
        rows = outer_cells[b * I : (b + 1) * I, :].astype(BF16)
        cube_sum_ref[b * B : (b + 1) * B, :] = tn(own_left, rows)
        left_single += nt(rows, cube_ref[:, b * C : (b + 1) * C])
    left_single_ref[...] = side_by_side(left_single, jnp.zeros((I, C - B), F32))
    right_total_ref[...] = right_total[...].T
    for way in travel:
        way.sent()
    swaps[0].sent(left0)
    swaps[1].sent(left0)
    swaps[2].sent(left0)
    swaps[3].sent(left0)


def total_kernel(
    scale,
    right_total_ref,
    left_single_ref,
    single_ref,
    gain_ref,
    bias_ref,
    weight_ref,
    own_ref,
    front0_sum,
    front1_sum,
    out0_sum,
    out1_sum,
    cube_sum,
    small_ref,
    single_grad_ref,
    total_ref,
    packed,
    right_parts,
    pair_part,
    chip_sum,
    chip_parts,
    dp_parts,
    right_send,
    right_recv,
    core_sem,
    chip_send,
    chip_recv,
    dp_send,
    dp_recv,
    back_send,
    back_recv,
    last_send,
    last_recv,
):
    me = lax.axis_index("axial")
    dp = lax.axis_index("dp")
    core = lax.rem(me, 2)
    chip = me // 2
    sibling = me + 1 - 2 * core
    barrier = pltpu.get_barrier_semaphore()

    def greet(t, _):
        pl.semaphore_signal(
            barrier, inc=1, device_id=(dp, lax.rem(me + t, 16)), device_id_type=MESH
        )
        return 0

    def greet_dp(t, _):
        pl.semaphore_signal(
            barrier, inc=1, device_id=(lax.rem(dp + t, 8), me), device_id_type=MESH
        )
        return 0

    lax.fori_loop(1, 16, greet, 0)
    lax.fori_loop(1, 8, greet_dp, 0)

    def put(at, value):
        count = value.shape[0]
        while count:
            room = min(count, PART - at % PART)
            packed[at // PART, at % PART : at % PART + room, :] = value[:room].astype(BF16)
            at, value, count = at + room, value[room:], count - room

    for n in range(5):
        put(n * C, front0_sum[:, n * C : (n + 1) * C])
        put((5 + n) * C, front1_sum[:, n * C : (n + 1) * C])
    put(10 * C, out0_sum[...])
    put(11 * C, out1_sum[...])
    put(12 * C, cube_sum[...])
    put(24 * C, small_ref[...])
    standard, inverse = norm(single_ref[...].astype(F32), axis=1)
    normed = (standard * gain_ref[...] + bias_ref[...]).astype(BF16)
    pl.semaphore_wait(barrier, 22)

    def right_copy(t):
        target = lax.rem(me + t, 16)
        return pltpu.make_async_remote_copy(
            src_ref=right_total_ref.at[rows_of(target * I)],
            dst_ref=right_parts.at[t],
            send_sem=right_send.at[t],
            recv_sem=right_recv.at[t],
            device_id=(dp, target),
            device_id_type=MESH,
        )

    loop(1, 16, lambda t: right_copy(t).start())
    loop(1, 16, lambda t: right_copy(t).wait_recv())
    right_single = right_total_ref[rows_of(me * I), :]
    for t in range(1, 16):
        right_single += right_parts[t]
    both = jnp.concatenate(
        [left_single_ref[:, :B], right_single[:, :B], jnp.zeros((I, C - 2 * B), F32)], axis=1
    )
    both = (both * own_ref[...]).astype(BF16)
    single_grad = nt(both, weight_ref[...])
    gain_sum = jnp.sum(single_grad * standard, axis=0, keepdims=True)
    bias_sum = jnp.sum(single_grad, axis=0, keepdims=True)
    single_grad_ref[...] = norm_back(
        single_grad * gain_ref[...], standard, inverse, axis=1
    ).astype(BF16)
    factor_sums = tn(both, normed)
    for n in range(8):
        put(20 * C + n * 64, factor_sums[:64, n * C : (n + 1) * C])
    tail = [gain_sum[:, n * C : (n + 1) * C] for n in range(8)]
    tail += [bias_sum[:, n * C : (n + 1) * C] for n in range(8)]
    put(25 * C, jnp.concatenate(tail + [jnp.zeros((C - 16, C), F32)], axis=0))

    pair_copy = pltpu.make_async_remote_copy(
        src_ref=packed.at[pl.ds(8 - 8 * core, 8)],
        dst_ref=pair_part,
        send_sem=core_sem.at[0],
        recv_sem=core_sem.at[1],
        device_id=(dp, sibling),
        device_id_type=MESH,
    )
    pair_copy.start()
    pair_copy.wait()

    def chip_copy(t):
        target = lax.rem(chip + t, 8)
        return pltpu.make_async_remote_copy(
            src_ref=chip_sum.at[target],
            dst_ref=chip_parts.at[t],
            send_sem=chip_send.at[t],
            recv_sem=chip_recv.at[t],
            device_id=(dp, target * 2 + core),
            device_id_type=MESH,
        )

    def add_pair(t):
        n = lax.rem(chip + t, 8)
        chip_sum[n] = (packed[core * 8 + n].astype(F32) + pair_part[n].astype(F32)).astype(BF16)

    def add_and_send(t):
        add_pair(t)
        chip_copy(t).start()

    loop(1, 8, add_and_send)
    add_pair(0)
    loop(1, 8, lambda t: chip_copy(t).wait_recv())
    total = chip_sum[chip].astype(F32)
    for t in range(1, 8):
        total += chip_parts[t].astype(F32)
    dp_parts[dp] = total.astype(BF16)

    def dp_copy(t):
        return pltpu.make_async_remote_copy(
            src_ref=dp_parts.at[dp],
            dst_ref=dp_parts.at[dp],
            send_sem=dp_send.at[t],
            recv_sem=dp_recv.at[t],
            device_id=(lax.rem(dp + t, 8), me),
            device_id_type=MESH,
        )

    loop(1, 8, lambda t: dp_copy(t).start())
    loop(1, 8, lambda t: dp_copy(t).wait_recv())
    total = dp_parts[0].astype(F32)
    for n in range(1, 8):
        total += dp_parts[n].astype(F32)
    total_ref[core * 8 + chip] = (total * scale).astype(BF16)

    def back_copy(t):
        block = total_ref.at[core * 8 + chip]
        return pltpu.make_async_remote_copy(
            src_ref=block,
            dst_ref=block,
            send_sem=back_send.at[t],
            recv_sem=back_recv.at[t],
            device_id=(dp, lax.rem(chip + t, 8) * 2 + core),
            device_id_type=MESH,
        )

    def last_copy(t):
        block = total_ref.at[core * 8 + lax.rem(chip + 8 - t, 8)]
        return pltpu.make_async_remote_copy(
            src_ref=block,
            dst_ref=block,
            send_sem=last_send.at[t],
            recv_sem=last_recv.at[t],
            device_id=(dp, sibling),
            device_id_type=MESH,
        )

    loop(1, 8, lambda t: back_copy(t).start())
    last_copy(0).start()

    def pass_on(t):
        back_copy(t).wait_recv()
        last_copy(t).start()

    loop(1, 8, pass_on)
    loop(0, 8, lambda t: last_copy(t).wait())
    loop(1, 8, lambda t: back_copy(t).wait_send())
    loop(1, 8, lambda t: dp_copy(t).wait_send())
    loop(1, 8, lambda t: chip_copy(t).wait_send())
    loop(1, 16, lambda t: right_copy(t).wait_send())


def unpack_kernel(
    total_ref,
    outer_gain_ref,
    outer_bias_ref,
    outer_left_ref,
    outer_right_ref,
    cube_ref,
    pair_bias_ref,
    norm_gain_ref,
    norm_bias_ref,
    proj_ref,
    gate_ref,
    out_gain_ref,
    out_bias_ref,
    out_ref,
):
    for t in range(2):
        for n in range(4):
            at = (5 * t + n) * C
            proj_ref[t, :, n * C : (n + 1) * C] = total_ref[at : at + C, :].astype(F32)
        at = (5 * t + 4) * C
        gate_ref[t] = total_ref[at : at + C, :].astype(F32)
        out_ref[t] = total_ref[(10 + t) * C : (11 + t) * C, :].astype(F32)
    cube = total_ref[12 * C : 20 * C, :].astype(F32).reshape(B, B, C)
    cube_ref[...] = jnp.swapaxes(cube, 0, 1).reshape(B * B, C)
    for n in range(8):
        at = 20 * C + n * 64
        block = jnp.concatenate(
            [total_ref[at : at + 64, :].astype(F32), jnp.zeros((64, C), F32)], axis=0
        ).T
        outer_left_ref[n * C : (n + 1) * C, :] = block[:, :B]
        outer_right_ref[n * C : (n + 1) * C, :] = block[:, B : 2 * B]
    small = total_ref[24 * C : 25 * C, :].astype(F32).T
    for t in range(2):
        norm_gain_ref[t : t + 1, :] = small[4 * t : 4 * t + 1]
        norm_bias_ref[t : t + 1, :] = small[4 * t + 1 : 4 * t + 2]
        out_gain_ref[t : t + 1, :] = small[4 * t + 2 : 4 * t + 3]
        out_bias_ref[t : t + 1, :] = small[4 * t + 3 : 4 * t + 4]
    pair_bias_ref[...] = small[8:9]
    rows = total_ref[25 * C : 25 * C + 16, :].astype(F32)
    outer_gain_ref[...] = rows[:8]
    outer_bias_ref[...] = rows[8:16]


def call(kernel, outs, scratch, args, name, collective=None, flops=0):
    return pl.pallas_call(
        kernel,
        out_shape=[jax.ShapeDtypeStruct(shape, dtype) for shape, dtype in outs],
        in_specs=[pl.BlockSpec(memory_space=pltpu.VMEM)] * len(args),
        out_specs=[pl.BlockSpec(memory_space=pltpu.VMEM)] * len(outs),
        scratch_shapes=scratch,
        name=name,
        compiler_params=pltpu.CompilerParams(
            collective_id=collective,
            has_side_effects=collective is not None,
            vmem_limit_bytes=VMEM_LIMIT,
        ),
    )(*args)


DMA = pltpu.SemaphoreType.DMA
BY_CHANNEL = (C, I, J)
BY_PAIR = (2, I // 2, C, J)
HALF = (16, C, J)
EVERY = (16, J, J)


def local(
    single_state,
    pair_state,
    residue_mask,
    pair_cotangent,
    outer_norm_gain,
    outer_norm_bias,
    outer_left,
    outer_right,
    outer_proj,
    outer_bias,
    triangle_norm_gain,
    triangle_norm_bias,
    triangle_proj,
    triangle_gate,
    triangle_out_gain,
    triangle_out_bias,
    triangle_out,
):
    me = lax.axis_index("axial")
    weight = residue_mask[0].astype(F32)
    own = lax.dynamic_slice_in_dim(weight, me * I, I)[:, None]
    mask = own[None] * weight.reshape(2, 1, C)
    own_wide = jnp.broadcast_to(own, (I, C))
    factor_weight = jnp.concatenate(
        [outer_left, outer_right, jnp.zeros((outer_left.shape[0], C - 2 * B), BF16)], axis=1
    )
    single = single_state[0]
    single_gain, single_bias = outer_norm_gain[None, :], outer_norm_bias[None, :]
    cube = outer_proj.reshape(B, B * C)
    back_weight = jnp.concatenate([triangle_proj, triangle_gate], axis=2)
    front_weight = jnp.swapaxes(back_weight, 1, 2)

    (every,) = call(
        head_kernel,
        [((J, C), BF16)],
        [DMA((16,)), DMA((16,))],
        (single, single_gain, single_bias, factor_weight, own_wide),
        "head",
        collective=0,
    )
    (
        pair_gradient,
        front0_sum,
        front1_sum,
        out0_sum,
        out1_sum,
        small,
        cube_sum,
        left_single,
        right_total,
    ) = call(
        trunk_kernel,
        [
            ((I, J, C), BF16),
            ((C, 5 * C), F32),
            ((C, 5 * C), F32),
            ((C, C), F32),
            ((C, C), F32),
            ((C, C), F32),
            ((B * B, C), F32),
            ((I, C), F32),
            ((J, C), F32),
        ],
        [pltpu.VMEM(BY_PAIR, BF16)] * 5
        + [pltpu.VMEM((6,) + BY_CHANNEL, BF16)] * 2
        + [pltpu.VMEM((6,) + HALF, BF16)]
        + [pltpu.VMEM(shape, BF16) for shape in (HALF, EVERY, HALF, HALF, EVERY, HALF)]
        + [
            pltpu.VMEM(HALF, F32),
            pltpu.VMEM((2,) + HALF, BF16),
            pltpu.VMEM((2,) + HALF, BF16),
            pltpu.VMEM((4, C * I, C), F32),
            pltpu.VMEM((B * I, C), F32),
            pltpu.VMEM((B * I, C), F32),
            pltpu.VMEM((9, C, C), F32),
            pltpu.VMEM((9, C, J), F32),
            pltpu.VMEM((C, J), F32),
            pltpu.VMEM((C, J), F32),
            DMA((12,)),
            DMA((12, 2, Q)),
            DMA((12, 2)),
            DMA((4,)),
            DMA((4, 2, Q, 2)),
        ],
        (
            pair_state[0],
            pair_cotangent[0],
            every,
            cube,
            mask,
            outer_bias[None, :],
            triangle_norm_gain,
            triangle_norm_bias,
            triangle_out_gain,
            triangle_out_bias,
            front_weight,
            back_weight,
            triangle_out,
        ),
        "trunk",
        collective=1,
    )
    scale = 1.0 / float(lax.axis_size("dp") * J)
    part = (PART, C)
    single_gradient, total = call(
        functools.partial(total_kernel, scale),
        [((I, single.shape[1]), BF16), ((16,) + part, BF16)],
        [
            pltpu.VMEM((16,) + part, BF16),
            pltpu.VMEM((16, I, C), F32),
            pltpu.VMEM((8,) + part, BF16),
            pltpu.VMEM((8,) + part, BF16),
            pltpu.VMEM((8,) + part, BF16),
            pltpu.VMEM((8,) + part, BF16),
            DMA((16,)),
            DMA((16,)),
            DMA((2,)),
        ]
        + [DMA((8,))] * 8,
        (
            right_total,
            left_single,
            single,
            single_gain,
            single_bias,
            factor_weight,
            own_wide,
            front0_sum,
            front1_sum,
            out0_sum,
            out1_sum,
            cube_sum,
            small,
        ),
        "total",
        collective=2,
    )
    unpacked = call(
        unpack_kernel,
        [
            ((8, C), F32),
            ((8, C), F32),
            (outer_left.shape, F32),
            (outer_right.shape, F32),
            (outer_proj.shape, F32),
            ((1, C), F32),
            ((2, C), F32),
            ((2, C), F32),
            (triangle_proj.shape, F32),
            (triangle_gate.shape, F32),
            ((2, C), F32),
            ((2, C), F32),
            (triangle_out.shape, F32),
        ],
        [],
        (total.reshape(16 * PART, C),),
        "unpack",
    )
    unpacked = list(unpacked)
    unpacked[0] = unpacked[0].reshape(-1)
    unpacked[1] = unpacked[1].reshape(-1)
    unpacked[5] = unpacked[5].reshape(-1)
    return (single_gradient[None], pair_gradient[None]) + tuple(unpacked)


def solution(mesh):
    whole = P()
    rows = P("dp", "axial", None)
    cells = P("dp", "axial", None, None)
    return jax.shard_map(
        local,
        mesh=mesh,
        in_specs=(rows, cells, P("dp", None), cells) + (whole,) * 13,
        out_specs=(rows, cells) + (whole,) * 13,
        check_vma=False,
    )
```

time: 346 us -> 285 us (0.82)
  Pallas kernels: 319 us -> 271 us
  local copies, waits for them, and re-layouts: 22.6 us -> 10.7 us
    pallas_call x12 -> x4, Pallas kernels: 319 us -> 271 us  [call(): pl.pallas_call(kernel, out_shape=[jax.ShapeDtypeStruct(shape, dtype) for...]
    another operation x12 -> x0, local copies, waits for them, and re-layouts: 5.91 us -> none  [the longest x3 1.49 us: local(): out_gains = [triangle_out_gain[t][:, None] for t in range(2)]]
    unnamed x28 -> x23, local copies, waits for them, and re-layouts: 7.39 us -> 8.12 us
where the time goes in v2:
time: 285 us; the launch traced here: 284 us
  Pallas kernels  271 us (95%)
  local copies, waits for them, and re-layouts  10.7 us (4%)
    pallas_call x4, Pallas kernels, call(): pl.pallas_call(kernel, out_shape=[jax.ShapeDtypeStruct(shape, dtype) for...  271 us
    unnamed x23, local copies, waits for them, and re-layouts  8.12 us

profile of v2, /device:TPU:1, one launch (start us, length us, event | category | flops | bytes accessed | tf_op | source)
XLA Modules:
  0.0 284.1 jit_solution(16083751896625769410)
XLA Ops:
  0.7 0.0 copy-start.7
  0.7 0.1 pad.2.clone
  0.7 0.6 copy-done.7
  1.3 0.1 dynamic-slice_bitcast_fusion
  1.4 0.7 broadcast_in_dim.27.own_ref
  2.1 0.7 broadcast_multiply_fusion.mask_ref
  2.8 0.0 copy-start.4
  2.8 1.0 copy.32
  3.8 0.0 copy-done.4
  3.8 0.2 copy.33
  4.0 0.9 maximum_maximum_fusion.weight_ref
  4.9 0.0 copy-start.2
  4.9 12.4 %head.1.every_ref = bf16[256,128]{1,0:T(8,128)(2,1)} custom-call(bf16[16,1024]{1,0:T(8,128)(2,1)} %bitcast.21, f32[1,1024]{1,0:T(1,128)} %bitcast.24, f32[1,1024]{1,0:T(1,128)} %bitcast.26, bf16[1024,128]{1,0:T(8,128)(2,1)} %maximum_maximum_fusion.weight_ref, f32[16,128]{1,0:T(8,128)} %broadcast_in_dim.27.own_ref), custom_call_target="tpu_custom_call" | custom-call | tf_op jit(solution)/shard_map/head/pallas_call | solution.py:1053
  17.2 0.0 copy-done.2
  17.3 0.0 copy-start.3
  17.3 0.8 reshape.56.cube_ref
  18.1 0.1 copy-done.3
  18.2 0.0 copy-start.5
  18.2 0.8 copy-done.5
  19.1 0.0 copy-start
  19.1 0.9 copy.34.front_ref
  20.0 0.0 copy-done
  20.0 217.4 %trunk.1 = (bf16[16,256,128]{2,1,0:T(8,128)(2,1)}, f32[128,640]{1,0:T(8,128)}, f32[128,640]{1,0:T(8,128)}, f32[128,128]{1,0:T(8,128)}, f32[128,128]{1,0:T(8,128)...) custom-call(bf16[16,256,128]{2,1,0:T(8,128)(2,1)} %bitcast.18, ...), custom_call_target="tpu_custom_call" | custom-call | tf_op jit(solution)/shard_map/trunk/pallas_call | solution.py:1053
  237.4 38.5 %total.1 = (bf16[16,1024]{1,0:T(8,128)(2,1)}, bf16[16,208,128]{2,1,0:T(8,128)(2,1)}) custom-call(f32[256,128]{1,0:T(8,128)} %get-tuple-element.39.right_total_ref, f32[16,128]{1,0:T(8,128)} %get-tuple-element.40.left_single_ref, bf16[16,1024]{1,0:T(8,128)(2,1)} %bitcast.22, f32[1,1024]{1,0:T(1,128)} %bitcast.25, f32[1,1024]{1,0:T(1,128)} %bitcast.27, ...), custom_call_target="tpu_custom_call" | custom-call | tf_op jit(solution)/shard_map/total/pallas_call | solution.py:1053
  275.9 0.0 copy-start.1
  275.9 2.8 unpack.1
  278.8 1.9 copy.35
  280.7 1.9 copy.36
  282.5 0.0 copy-done.6
  282.5 0.6 copy.40
  283.1 0.0 copy-done.1
  283.2 1.0 copy.41
  (5 shorter events, 0.0 us)
Async XLA Ops:
  0.7 0.7 copy-start.7
  2.8 1.0 copy-start.4
  4.9 12.4 %copy-start.2 = (bf16[1024,128]{1,0:T(8,128)(2,1)S(1)}, bf16[1024,128]{1,0:T(8,128)(2,1)}, u32[]{:S(2)}) copy-start(bf16[1024,128]{1,0:T(8,128)(2,1)} %param.25) | copy-start | bytes 786436
  17.3 1.0 copy-start.3
  18.2 0.8 copy-start.5
  19.1 0.9 copy-start
  275.9 7.2 %copy-start.1 = (bf16[16,256,128]{2,1,0:T(8,128)(2,1)S(1)}, bf16[16,256,128]{2,1,0:T(8,128)(2,1)}, u32[]{:S(2)}) copy-start(bf16[16,256,128]{2,1,0:T(8,128)(2,1)} %get-tuple-element.48) | copy-start | bytes 3145732
  280.6 1.9 copy-start.6

commit v3 on v2

--- a/solution.py
+++ b/solution.py
@@ -17,7 +17,7 @@
 B = 32
 Q = 2
 CQ = 8
-PART = 208
+UNROLL = 4
 VMEM_LIMIT = 60 * 2**20
 
 
@@ -89,6 +89,18 @@
     return side_by_side(
         ref[2 * p, lanes(h), :].astype(F32).T, ref[2 * p + 1, lanes(h), :].astype(F32).T
     )
+
+
+def weight_rows(residue_ref):
+    return residue_ref[...].astype(F32)
+
+
+def own_weights(residue_ref, me):
+    weights = weight_rows(residue_ref)
+    flat = side_by_side(weights[0:1], weights[1:2])
+    lane = lax.broadcasted_iota(jnp.int32, (I, J), 1)
+    row = lax.broadcasted_iota(jnp.int32, (I, J), 0) + me * I
+    return jnp.sum(jnp.where(lane == row, flat, 0.0), axis=1, keepdims=True)
 
 
 def mask_pair(mask_ref, p, h):
@@ -110,54 +122,19 @@
 
 
 def over_pairs(body, hook=None, at=4):
-    def step(p, _):
+    def step(n, _):
         if hook is not None:
-            pl.when(p == at)(hook)
-        body(p)
+            pl.when(2 * n == at)(hook)
+        body(2 * n)
+        body(2 * n + 1)
         return 0
 
-    lax.fori_loop(0, I // 2, step, 0)
-
-
-def head_kernel(single_ref, gain_ref, bias_ref, weight_ref, own_ref, every_ref, send_sem, recv_sem):
-    me = lax.axis_index("axial")
-    dp = lax.axis_index("dp")
-    barrier = pltpu.get_barrier_semaphore()
-
-    def greet(t, _):
-        pl.semaphore_signal(
-            barrier, inc=1, device_id=(dp, lax.rem(me + t, 16)), device_id_type=MESH
-        )
-        return 0
-
-    lax.fori_loop(1, 16, greet, 0)
-    standard, _ = norm(single_ref[...].astype(F32), axis=1)
-    normed = (standard * gain_ref[...] + bias_ref[...]).astype(BF16)
-    both = nn(normed, weight_ref[...]) * own_ref[...]
-    mine = pl.ds(pl.multiple_of(me * I, I), I)
-    every_ref[mine, :] = both.astype(BF16)
-    pl.semaphore_wait(barrier, 15)
-
-    def copy(t):
-        return pltpu.make_async_remote_copy(
-            src_ref=every_ref.at[mine],
-            dst_ref=every_ref.at[mine],
-            send_sem=send_sem.at[t],
-            recv_sem=recv_sem.at[t],
-            device_id=(dp, lax.rem(me + t, 16)),
-            device_id_type=MESH,
-        )
-
-    def begin(t, _):
-        copy(t).start()
-        return 0
-
-    def finish(t, _):
-        copy(t).wait()
-        return 0
-
-    lax.fori_loop(1, 16, begin, 0)
-    lax.fori_loop(1, 16, finish, 0)
+    lax.fori_loop(0, I // 4, step, 0)
+
+
+def factor_weights(left_ref, right_ref):
+    empty = jnp.zeros((C - 2 * B, left_ref.shape[1]), BF16)
+    return jnp.concatenate([left_ref[...], right_ref[...], empty], axis=0)
 
 
 def mixed_rows(own_left, cube_ref, mixed_cells):
@@ -244,18 +221,27 @@
     def greet(self):
         barrier = pltpu.get_barrier_semaphore()
 
-        def signal(t, _):
+        def signal(t):
             pl.semaphore_signal(
                 barrier,
                 inc=1,
-                device_id=(self.dp, self.axial(self.peer(t))),
+                device_id=(self.dp, lax.rem(self.me + t, 16)),
                 device_id_type=MESH,
             )
-            return 0
-
-        lax.fori_loop(1, 8, signal, 0)
-        pl.semaphore_signal(barrier, inc=1, device_id=(self.dp, self.other), device_id_type=MESH)
-        pl.semaphore_wait(barrier, 8)
+
+        def signal_dp(t):
+            pl.semaphore_signal(
+                barrier,
+                inc=1,
+                device_id=(lax.rem(self.dp + t, 8), self.me),
+                device_id_type=MESH,
+            )
+
+        loop(1, 16, signal)
+        loop(1, 8, signal_dp)
+
+    def met(self):
+        pl.semaphore_wait(pltpu.get_barrier_semaphore(), 22)
 
     def copy(self, source, target, send_sem, recv_sem, axial):
         return pltpu.make_async_remote_copy(
@@ -264,6 +250,16 @@
             send_sem=send_sem,
             recv_sem=recv_sem,
             device_id=(self.dp, axial),
+            device_id_type=MESH,
+        )
+
+    def copy_dp(self, block, send_sem, recv_sem, t):
+        return pltpu.make_async_remote_copy(
+            src_ref=block,
+            dst_ref=block,
+            send_sem=send_sem,
+            recv_sem=recv_sem,
+            device_id=(lax.rem(self.dp + t, 8), self.me),
             device_id_type=MESH,
         )
 
@@ -392,19 +388,135 @@
         wait_bytes(ref, self.send_sem)
 
 
-def split_rows(place, whole, kept, sent, channel, r):
+def split_rows(place, whole, kept, sent, channel, r, to_lanes, of_lanes):
     for n in range(2):
         to = slice(64 * r + 32 * n, 64 * r + 32 * n + 32)
-        kept[channel, to, :] = whole[rows_of(n * 64 + place.half * 32, 32), :]
-        sent[channel, to, :] = whole[rows_of(n * 64 + 32 - place.half * 32, 32), :].astype(BF16)
+        kept[channel, to, to_lanes] = whole[rows_of(n * 64 + place.half * 32, 32), of_lanes]
+        sent[channel, to, to_lanes] = whole[
+            rows_of(n * 64 + 32 - place.half * 32, 32), of_lanes
+        ].astype(BF16)
+
+
+class Total:
+    def __init__(self, place, scale, total, first_part, refs, sems):
+        self.place, self.scale, self.total, self.first = place, scale, total, first_part
+        self.packed, self.pair_part, self.chip_sum, self.chip_parts, self.dp_parts = refs
+        self.sem, self.back_recv = sems
+        self.part = self.packed.shape[1]
+        self.core = lax.rem(place.me, 2)
+        self.chip = place.me // 2
+        self.sibling = place.me + 1 - 2 * self.core
+
+    def put(self, at, value):
+        count, part = value.shape[0], self.part
+        while count:
+            room = min(count, part - at % part)
+            self.packed[at // part, at % part : at % part + room, :] = value[:room].astype(BF16)
+            at, value, count = at + room, value[room:], count - room
+
+    def pair_copy(self):
+        return self.place.copy(
+            self.packed.at[pl.ds(8 - 8 * self.core, 8)],
+            self.pair_part,
+            self.sem.at[0],
+            self.sem.at[1],
+            self.sibling,
+        )
+
+    def start(self):
+        self.pair_copy().start()
+
+    def to_chips(self):
+        self.pair_copy().wait()
+
+        def add(t):
+            n = lax.rem(self.chip + t, 8)
+            self.chip_sum[n] = (
+                self.packed[self.core * 8 + n].astype(F32) + self.pair_part[n].astype(F32)
+            ).astype(BF16)
+
+        def add_and_send(t):
+            add(t)
+            n = lax.rem(self.chip + t, 8)
+            self.place.copy(
+                self.chip_sum.at[n],
+                self.chip_parts.at[t],
+                self.sem.at[2],
+                self.sem.at[3],
+                n * 2 + self.core,
+            ).start()
+
+        loop(1, 8, add_and_send)
+        add(0)
+
+    def to_dp(self):
+        wait_bytes(self.chip_parts.at[1:8], self.sem.at[3])
+        total = self.chip_sum[self.chip].astype(F32)
+        for t in range(1, 8):
+            total += self.chip_parts[t].astype(F32)
+        dp = self.place.dp
+        self.dp_parts[dp] = total.astype(BF16)
+        loop(
+            1,
+            8,
+            lambda t: self.place.copy_dp(
+                self.dp_parts.at[dp], self.sem.at[4], self.sem.at[5], t
+            ).start(),
+        )
+
+    def block(self, chip):
+        at = self.first + (self.core * 8 + chip) * self.part
+        return self.total.at[rows_of(at, self.part)]
+
+    def back_copy(self, t):
+        block = self.block(self.chip)
+        return self.place.copy(
+            block,
+            block,
+            self.sem.at[6],
+            self.back_recv.at[t],
+            lax.rem(self.chip + t, 8) * 2 + self.core,
+        )
+
+    def pass_copy(self, t):
+        block = self.block(lax.rem(self.chip + 8 - t, 8))
+        return self.place.copy(block, block, self.sem.at[7], self.sem.at[8], self.sibling)
+
+    def to_all(self):
+        wait_bytes(self.dp_parts.at[1:8], self.sem.at[5])
+        total = self.dp_parts[0].astype(F32)
+        for n in range(1, 8):
+            total += self.dp_parts[n].astype(F32)
+        self.block(self.chip)[...] = (total * self.scale).astype(BF16)
+        loop(1, 8, lambda t: self.back_copy(t).start())
+        self.pass_copy(0).start()
+
+    def to_sibling(self):
+        def pass_on(t):
+            self.back_copy(t).wait_recv()
+            self.pass_copy(t).start()
+
+        loop(1, 8, pass_on)
+
+    def finish(self):
+        half = self.total.at[pl.ds(self.first, 8 * self.part)]
+        wait_bytes(half, self.sem.at[7])
+        wait_bytes(half, self.sem.at[8])
+        for n in (2, 4, 6):
+            wait_bytes(self.chip_parts.at[1:8], self.sem.at[n])
 
 
 def trunk_kernel(
+    scale,
+    single_ref,
+    single_gain_ref,
+    single_bias_ref,
+    left_weight_ref,
+    right_weight_ref,
     pair_ref,
     cotangent_ref,
-    every_ref,
     cube_ref,
-    mask_ref,
+    residue_ref,
     outer_bias_ref,
     norm_gain_ref,
     norm_bias_ref,
@@ -414,14 +526,16 @@
     back_ref,
     out_ref,
     pair_grad_ref,
+    single_grad_ref,
+    total_ref,
+    every_ref,
+    right_total_ref,
+    right_parts,
+    single_standard,
     front0_sum,
     front1_sum,
     out0_sum,
     out1_sum,
-    small_ref,
-    cube_sum_ref,
-    left_single_ref,
-    right_total_ref,
     first,
     second,
     gate_grad0,
@@ -446,22 +560,56 @@
     sums,
     right_total,
     whole,
+    mask_ref,
     send_sem,
     recv_sem,
     local_sem,
     half_send,
     half_recv,
+    few_sem,
+    total_sem,
+    total_back,
+    *total_refs,
 ):
     place = Place()
     place.greet()
+    me, dp = place.me, place.dp
+    own = own_weights(residue_ref, me)
+    totals = [
+        Total(
+            place,
+            scale,
+            total_ref,
+            first_part,
+            total_refs[5 * n : 5 * n + 5],
+            (total_sem.at[n], total_back.at[n]),
+        )
+        for n, first_part in enumerate((0, 1024, 2816))
+    ]
+    standard, single_inverse = norm(single_ref[...].astype(F32), axis=1)
+    single_standard[...] = standard
+    normed_single = (standard * single_gain_ref[...] + single_bias_ref[...]).astype(BF16)
+    factors = nt(normed_single, factor_weights(left_weight_ref, right_weight_ref))
+    mine = rows_of(me * I)
+    every_ref[mine, :] = (factors * own).astype(BF16)
+    place.met()
+
+    def factor_copy(t):
+        block = every_ref.at[mine]
+        return place.copy(block, block, few_sem.at[0], few_sem.at[1], lax.rem(me + t, 16))
+
+    loop(1, 16, lambda t: factor_copy(t).start())
+    for h in range(2):
+        mask_ref[h] = own * weight_rows(residue_ref)[h : h + 1]
     for t in range(2):
         for n, ref in enumerate((norm_gain_ref, norm_bias_ref, out_gain_ref, out_bias_ref)):
             wides[4 * t + n] = jnp.broadcast_to(ref[t : t + 1, :], (C, C)).T
     wides[8] = jnp.broadcast_to(outer_bias_ref[...], (C, C)).T
     clear(sums, front0_sum, front1_sum, out0_sum, out1_sum, right_total, outer_cells)
+    own_left = every_ref[mine, :][:, :B]
+    mixed_rows(own_left, cube_ref, mixed_cells)
+    wait_bytes(every_ref.at[: 15 * I], few_sem.at[1])
     right_rows = every_ref[...].astype(F32).T[B : 2 * B].astype(BF16)
-    own_left = every_ref[rows_of(place.me * I), :][:, :B]
-    mixed_rows(own_left, cube_ref, mixed_cells)
 
     sems = (send_sem, recv_sem, local_sem)
     swap_sems = (half_send, half_recv)
@@ -497,7 +645,11 @@
     swaps = [Swap(place, swap_sems, n) for n in range(4)]
 
     def over_channels(q, do):
-        loop(q * CQ, (q + 1) * CQ, do)
+        def step(n):
+            for m in range(UNROLL):
+                do(q * CQ + n * UNROLL + m, m)
+
+        loop(0, CQ // UNROLL, step)
 
     def front_first(h, hook=None):
         gain, bias, outer_bias = wide(wides.at[0]), wide(wides.at[1]), wide(wides.at[8])
@@ -518,23 +670,27 @@
         cells_out(cells.at[0], sends.at[0], h)
         send_left0.send(h)
 
-    def forward(travelling, ref, swap, h):
-        travelling.here(h)
-        if h == 0:
-            for q in range(Q):
-                travelling.arrive(h, q)
-                for r in range(2):
-                    swap.rows(ref, h, q, r)
-        else:
-            for q in range(Q):
-                travelling.arrive(h, q)
-                swap.rows(ref, h, q, 0)
-            for q in range(Q):
-                swap.rows(ref, h, q, 1)
+    def forward_right(h):
+        send_right0.here(h)
+        order = ((0, 0, 0), (0, 1, 0), (0, 0, 1)) if h == 0 else (
+            (1, 0, 0), (1, 1, 0), (0, 1, 1), (1, 0, 1), (1, 1, 1)
+        )
+        for half, q, r in order:
+            if half == h and r == 0:
+                send_right0.arrive(h, q)
+            swaps[0].rows(right0, half, q, r)
+
+    def forward_grad(h):
+        send_grad1.here(h)
+        for q in range(Q):
+            send_grad1.arrive(h, q)
+            swaps[2].rows(grad1, h, q, 0)
+        for q in range(Q):
+            swaps[2].rows(grad1, h, q, 1)
 
     front_first(0)
-    front_first(1, lambda: forward(send_right0, right0, swaps[0], 0))
-    forward(send_right0, right0, swaps[0], 1)
+    front_first(1, lambda: forward_right(0))
+    forward_right(1)
     send_left0.arrive_half(0)
     send_left0.arrive_half(1)
     for h in range(2):
@@ -542,7 +698,7 @@
             for n in range(2):
                 swaps[0].arrive(right0, n, q, h)
 
-            def multiply(c):
+            def multiply(c, m):
                 staged[0, c, :, lanes(h)] = nt(left0[c], right0[c, lanes(h), :]).astype(BF16)
 
             over_channels(q, multiply)
@@ -587,32 +743,33 @@
 
     middle(0)
     middle(1)
-    for way in (send_left1, send_right1):
-        way.here(0)
-        way.here(1)
-    for q in range(Q):
+    def incoming_sums(q, h, r):
+        def multiply_sums(c, m):
+            whole[m, :, :C] = tn(left1[c, :, lanes(r)], right1[c, :, lanes(h)])
+            split_rows(
+                place, whole.at[m], kept_sum, sent_sum.at[0], c, r, lanes(h), slice(0, C)
+            )
+
+        over_channels(q, multiply_sums)
+        swaps[1].sums(sent_sum.at[0], received_sum.at[0], h, q, r)
+
+    for n in range(2):
         for way in (send_left1, send_right1):
-            for h in range(2):
-                way.arrive(h, q)
-
-        def multiply_sums(c):
-            for r in range(2):
-                whole[...] = tn(left1[c, :, lanes(r)], right1[c])
-                split_rows(place, whole, kept_sum, sent_sum.at[0], c, r)
-
-        over_channels(q, multiply_sums)
-        for r in range(2):
-            swaps[1].sums(sent_sum.at[0], received_sum.at[0], 0, q, r)
-    for q in range(Q):
-        for r in range(2):
-            swaps[1].sums(sent_sum.at[0], received_sum.at[0], 1, q, r)
+            way.here(n)
+        for q in range(Q):
+            for way in (send_left1, send_right1):
+                way.arrive(n, q)
+            incoming_sums(q, 0, n)
+    for r in range(2):
+        for q in range(Q):
+            incoming_sums(q, 1, r)
 
     def add_halves(swap, received, target, way, h):
         for q in range(Q):
             for r in range(2):
                 swap.arrive(received, h, q, r)
 
-            def add(c):
+            def add(c, m):
                 target[c, :, lanes(h)] = (
                     kept_sum[c, :, lanes(h)] + received[c, :, lanes(h)].astype(F32)
                 ).astype(BF16)
@@ -650,16 +807,16 @@
     add_halves(swaps[1], received_sum.at[0], staged.at[1], send_product1, 0)
     back_second(0)
     add_halves(swaps[1], received_sum.at[0], staged.at[1], send_product1, 1)
-    forward(send_grad1, grad1, swaps[2], 0)
+    forward_grad(0)
     back_second(1)
-    forward(send_grad1, grad1, swaps[2], 1)
+    forward_grad(1)
     for h in range(2):
         for q in range(Q):
             for r in range(2):
                 if h == 0 or r == 1:
                     swaps[2].arrive(grad1, h, q, r)
 
-            def right_back(c):
+            def right_back(c, m):
                 staged[3, c, :, lanes(h)] = nn(left1[c], grad1[c, :, lanes(h)]).astype(BF16)
 
             over_channels(q, right_back)
@@ -669,7 +826,7 @@
             if h == 0:
                 swaps[2].arrive(grad1, 1, q, 0)
 
-            def left_back(c):
+            def left_back(c, m):
                 staged[2, c, :, lanes(h)] = nt(right1[c], grad1[c, lanes(h), :]).astype(BF16)
 
             over_channels(q, left_back)
@@ -724,9 +881,11 @@
         for q in range(Q):
             send_grad0.arrive(r, q)
 
-            def multiply_back(c):
-                whole[...] = tn(grad0[c, :, lanes(r)], left0[c])
-                split_rows(place, whole, kept_sum, sent_sum.at[1], c, r)
+            def multiply_back(c, m):
+                whole[m] = tn(grad0[c, :, lanes(r)], left0[c])
+                split_rows(
+                    place, whole.at[m], kept_sum, sent_sum.at[1], c, r, slice(None), slice(None)
+                )
 
             over_channels(q, multiply_back)
             swaps[3].sums(sent_sum.at[1], received_sum.at[1], 0, q, r)
@@ -738,11 +897,18 @@
 
     back_middle(0)
     back_middle(1, lambda: right_sums(0))
+    for n in range(5):
+        totals[0].put(n * C, front1_sum[:, n * C : (n + 1) * C])
+    totals[0].put(5 * C, out0_sum[...])
+    totals[0].put(6 * C, out1_sum[...])
+    totals[0].put(7 * C, jnp.zeros((C, C), F32))
+    totals[0].start()
     right_sums(1)
+    totals[0].to_chips()
     for h in range(2):
         for q in range(Q):
 
-            def left_back_out(c):
+            def left_back_out(c, m):
                 staged[4, c, :, lanes(h)] = nn(grad0[c], right0[c, :, lanes(h)]).astype(BF16)
 
             over_channels(q, left_back_out)
@@ -785,224 +951,76 @@
         over_pairs(body)
 
     add_halves(swaps[3], received_sum.at[1], staged.at[5], send_right_grad0, 0)
+    totals[0].to_dp()
     back_first(0)
     add_halves(swaps[3], received_sum.at[1], staged.at[5], send_right_grad0, 1)
+    totals[0].to_all()
     back_first(1)
 
-    small_ref[...] = columns(*[sums.at[n] for n in range(9)])
+    right_total_ref[...] = right_total[...].T
+
+    def right_copy(t):
+        target = lax.rem(me + t, 16)
+        return place.copy(
+            right_total_ref.at[rows_of(target * I)],
+            right_parts.at[t],
+            few_sem.at[2],
+            few_sem.at[3],
+            target,
+        )
+
+    loop(1, 16, lambda t: right_copy(t).start())
+    for n in range(5):
+        totals[1].put(n * C, front0_sum[:, n * C : (n + 1) * C])
     left_single = jnp.zeros((I, B), F32)
     for b in range(B):
         rows = outer_cells[b * I : (b + 1) * I, :].astype(BF16)
-        cube_sum_ref[b * B : (b + 1) * B, :] = tn(own_left, rows)
+        totals[1].put(5 * C + b * B, tn(own_left, rows))
         left_single += nt(rows, cube_ref[:, b * C : (b + 1) * C])
-    left_single_ref[...] = side_by_side(left_single, jnp.zeros((I, C - B), F32))
-    right_total_ref[...] = right_total[...].T
+    totals[1].put(13 * C, columns(*[sums.at[n] for n in range(9)]))
+    totals[1].start()
+
+    wait_bytes(right_parts.at[1:16], few_sem.at[3])
+    right_single = right_total_ref[mine, :]
+    for t in range(1, 16):
+        right_single += right_parts[t]
+    both = jnp.concatenate(
+        [left_single, right_single[:, :B], jnp.zeros((I, C - 2 * B), F32)], axis=1
+    )
+    both = (both * own).astype(BF16)
+    single_grad = nn(both, factor_weights(left_weight_ref, right_weight_ref))
+    standard = single_standard[...]
+    normed_single = (standard * single_gain_ref[...] + single_bias_ref[...]).astype(BF16)
+    factor_sums = tn(both, normed_single)
+    totals[1].to_chips()
+    for n in range(8):
+        totals[2].put(n * 64, factor_sums[:64, lanes(n)])
+    gain_sum = jnp.sum(single_grad * standard, axis=0, keepdims=True)
+    bias_sum = jnp.sum(single_grad, axis=0, keepdims=True)
+    tail = [gain_sum[:, lanes(n)] for n in range(8)] + [bias_sum[:, lanes(n)] for n in range(8)]
+    totals[2].put(4 * C, jnp.concatenate(tail + [jnp.zeros((2 * C - 16, C), F32)], axis=0))
+    totals[2].start()
+    single_grad_ref[...] = norm_back(
+        single_grad * single_gain_ref[...], standard, single_inverse, axis=1
+    ).astype(BF16)
+    totals[0].to_sibling()
+    totals[2].to_chips()
+    totals[1].to_dp()
+    totals[2].to_dp()
+    totals[1].to_all()
+    totals[2].to_all()
+    totals[1].to_sibling()
+    totals[2].to_sibling()
+    for batch in totals:
+        batch.finish()
+    wait_bytes(every_ref.at[: 15 * I], few_sem.at[0])
+    wait_bytes(right_parts.at[1:16], few_sem.at[2])
     for way in travel:
         way.sent()
     swaps[0].sent(left0)
     swaps[1].sent(left0)
     swaps[2].sent(left0)
     swaps[3].sent(left0)
-
-
-def total_kernel(
-    scale,
-    right_total_ref,
-    left_single_ref,
-    single_ref,
-    gain_ref,
-    bias_ref,
-    weight_ref,
-    own_ref,
-    front0_sum,
-    front1_sum,
-    out0_sum,
-    out1_sum,
-    cube_sum,
-    small_ref,
-    single_grad_ref,
-    total_ref,
-    packed,
-    right_parts,
-    pair_part,
-    chip_sum,
-    chip_parts,
-    dp_parts,
-    right_send,
-    right_recv,
-    core_sem,
-    chip_send,
-    chip_recv,
-    dp_send,
-    dp_recv,
-    back_send,
-    back_recv,
-    last_send,
-    last_recv,
-):
-    me = lax.axis_index("axial")
-    dp = lax.axis_index("dp")
-    core = lax.rem(me, 2)
-    chip = me // 2
-    sibling = me + 1 - 2 * core
-    barrier = pltpu.get_barrier_semaphore()
-
-    def greet(t, _):
-        pl.semaphore_signal(
-            barrier, inc=1, device_id=(dp, lax.rem(me + t, 16)), device_id_type=MESH
-        )
-        return 0
-
-    def greet_dp(t, _):
-        pl.semaphore_signal(
-            barrier, inc=1, device_id=(lax.rem(dp + t, 8), me), device_id_type=MESH
-        )
-        return 0
-
-    lax.fori_loop(1, 16, greet, 0)
-    lax.fori_loop(1, 8, greet_dp, 0)
-
-    def put(at, value):
-        count = value.shape[0]
-        while count:
-            room = min(count, PART - at % PART)
-            packed[at // PART, at % PART : at % PART + room, :] = value[:room].astype(BF16)
-            at, value, count = at + room, value[room:], count - room
-
-    for n in range(5):
-        put(n * C, front0_sum[:, n * C : (n + 1) * C])
-        put((5 + n) * C, front1_sum[:, n * C : (n + 1) * C])
-    put(10 * C, out0_sum[...])
-    put(11 * C, out1_sum[...])
-    put(12 * C, cube_sum[...])
-    put(24 * C, small_ref[...])
-    standard, inverse = norm(single_ref[...].astype(F32), axis=1)
-    normed = (standard * gain_ref[...] + bias_ref[...]).astype(BF16)
-    pl.semaphore_wait(barrier, 22)
-
-    def right_copy(t):
-        target = lax.rem(me + t, 16)
-        return pltpu.make_async_remote_copy(
-            src_ref=right_total_ref.at[rows_of(target * I)],
-            dst_ref=right_parts.at[t],
-            send_sem=right_send.at[t],
-            recv_sem=right_recv.at[t],
-            device_id=(dp, target),
-            device_id_type=MESH,
-        )
-
-    loop(1, 16, lambda t: right_copy(t).start())
-    loop(1, 16, lambda t: right_copy(t).wait_recv())
-    right_single = right_total_ref[rows_of(me * I), :]
-    for t in range(1, 16):
-        right_single += right_parts[t]
-    both = jnp.concatenate(
-        [left_single_ref[:, :B], right_single[:, :B], jnp.zeros((I, C - 2 * B), F32)], axis=1
-    )
-    both = (both * own_ref[...]).astype(BF16)
-    single_grad = nt(both, weight_ref[...])
-    gain_sum = jnp.sum(single_grad * standard, axis=0, keepdims=True)
-    bias_sum = jnp.sum(single_grad, axis=0, keepdims=True)
-    single_grad_ref[...] = norm_back(
-        single_grad * gain_ref[...], standard, inverse, axis=1
-    ).astype(BF16)
-    factor_sums = tn(both, normed)
-    for n in range(8):
-        put(20 * C + n * 64, factor_sums[:64, n * C : (n + 1) * C])
-    tail = [gain_sum[:, n * C : (n + 1) * C] for n in range(8)]
-    tail += [bias_sum[:, n * C : (n + 1) * C] for n in range(8)]
-    put(25 * C, jnp.concatenate(tail + [jnp.zeros((C - 16, C), F32)], axis=0))
-
-    pair_copy = pltpu.make_async_remote_copy(
-        src_ref=packed.at[pl.ds(8 - 8 * core, 8)],
-        dst_ref=pair_part,
-        send_sem=core_sem.at[0],
-        recv_sem=core_sem.at[1],
-        device_id=(dp, sibling),
-        device_id_type=MESH,
-    )
-    pair_copy.start()
-    pair_copy.wait()
-
-    def chip_copy(t):
-        target = lax.rem(chip + t, 8)
-        return pltpu.make_async_remote_copy(
-            src_ref=chip_sum.at[target],
-            dst_ref=chip_parts.at[t],
-            send_sem=chip_send.at[t],
-            recv_sem=chip_recv.at[t],
-            device_id=(dp, target * 2 + core),
-            device_id_type=MESH,
-        )
-
-    def add_pair(t):
-        n = lax.rem(chip + t, 8)
-        chip_sum[n] = (packed[core * 8 + n].astype(F32) + pair_part[n].astype(F32)).astype(BF16)
-
-    def add_and_send(t):
-        add_pair(t)
-        chip_copy(t).start()
-
-    loop(1, 8, add_and_send)
-    add_pair(0)
-    loop(1, 8, lambda t: chip_copy(t).wait_recv())
-    total = chip_sum[chip].astype(F32)
-    for t in range(1, 8):
-        total += chip_parts[t].astype(F32)
-    dp_parts[dp] = total.astype(BF16)
-
-    def dp_copy(t):
-        return pltpu.make_async_remote_copy(
-            src_ref=dp_parts.at[dp],
-            dst_ref=dp_parts.at[dp],
-            send_sem=dp_send.at[t],
-            recv_sem=dp_recv.at[t],
-            device_id=(lax.rem(dp + t, 8), me),
-            device_id_type=MESH,
-        )
-
-    loop(1, 8, lambda t: dp_copy(t).start())
-    loop(1, 8, lambda t: dp_copy(t).wait_recv())
-    total = dp_parts[0].astype(F32)
-    for n in range(1, 8):
-        total += dp_parts[n].astype(F32)
-    total_ref[core * 8 + chip] = (total * scale).astype(BF16)
-
-    def back_copy(t):
-        block = total_ref.at[core * 8 + chip]
-        return pltpu.make_async_remote_copy(
-            src_ref=block,
-            dst_ref=block,
-            send_sem=back_send.at[t],
-            recv_sem=back_recv.at[t],
-            device_id=(dp, lax.rem(chip + t, 8) * 2 + core),
-            device_id_type=MESH,
-        )
-
-    def last_copy(t):
-        block = total_ref.at[core * 8 + lax.rem(chip + 8 - t, 8)]
-        return pltpu.make_async_remote_copy(
-            src_ref=block,
-            dst_ref=block,
-            send_sem=last_send.at[t],
-            recv_sem=last_recv.at[t],
-            device_id=(dp, sibling),
-            device_id_type=MESH,
-        )
-
-    loop(1, 8, lambda t: back_copy(t).start())
-    last_copy(0).start()
-
-    def pass_on(t):
-        back_copy(t).wait_recv()
-        last_copy(t).start()
-
-    loop(1, 8, pass_on)
-    loop(0, 8, lambda t: last_copy(t).wait())
-    loop(1, 8, lambda t: back_copy(t).wait_send())
-    loop(1, 8, lambda t: dp_copy(t).wait_send())
-    loop(1, 8, lambda t: chip_copy(t).wait_send())
-    loop(1, 16, lambda t: right_copy(t).wait_send())
 
 
 def unpack_kernel(
@@ -1022,29 +1040,27 @@
     out_ref,
 ):
     for t in range(2):
+        front = 8 - 8 * t
         for n in range(4):
-            at = (5 * t + n) * C
+            at = (front + n) * C
             proj_ref[t, :, n * C : (n + 1) * C] = total_ref[at : at + C, :].astype(F32)
-        at = (5 * t + 4) * C
+        at = (front + 4) * C
         gate_ref[t] = total_ref[at : at + C, :].astype(F32)
-        out_ref[t] = total_ref[(10 + t) * C : (11 + t) * C, :].astype(F32)
-    cube = total_ref[12 * C : 20 * C, :].astype(F32).reshape(B, B, C)
+        out_ref[t] = total_ref[(5 + t) * C : (6 + t) * C, :].astype(F32)
+    cube = total_ref[13 * C : 21 * C, :].astype(F32).reshape(B, B, C)
     cube_ref[...] = jnp.swapaxes(cube, 0, 1).reshape(B * B, C)
     for n in range(8):
-        at = 20 * C + n * 64
-        block = jnp.concatenate(
-            [total_ref[at : at + 64, :].astype(F32), jnp.zeros((64, C), F32)], axis=0
-        ).T
-        outer_left_ref[n * C : (n + 1) * C, :] = block[:, :B]
-        outer_right_ref[n * C : (n + 1) * C, :] = block[:, B : 2 * B]
-    small = total_ref[24 * C : 25 * C, :].astype(F32).T
+        at = 22 * C + n * 64
+        outer_left_ref[:, n * C : (n + 1) * C] = total_ref[at : at + B, :].astype(F32)
+        outer_right_ref[:, n * C : (n + 1) * C] = total_ref[at + B : at + 2 * B, :].astype(F32)
+    small = total_ref[21 * C : 22 * C, :].astype(F32).T
     for t in range(2):
         norm_gain_ref[t : t + 1, :] = small[4 * t : 4 * t + 1]
         norm_bias_ref[t : t + 1, :] = small[4 * t + 1 : 4 * t + 2]
         out_gain_ref[t : t + 1, :] = small[4 * t + 2 : 4 * t + 3]
         out_bias_ref[t : t + 1, :] = small[4 * t + 3 : 4 * t + 4]
     pair_bias_ref[...] = small[8:9]
-    rows = total_ref[25 * C : 25 * C + 16, :].astype(F32)
+    rows = total_ref[26 * C : 26 * C + 16, :].astype(F32)
     outer_gain_ref[...] = rows[:8]
     outer_bias_ref[...] = rows[8:16]
 
@@ -1091,52 +1107,29 @@
     triangle_out_bias,
     triangle_out,
 ):
-    me = lax.axis_index("axial")
-    weight = residue_mask[0].astype(F32)
-    own = lax.dynamic_slice_in_dim(weight, me * I, I)[:, None]
-    mask = own[None] * weight.reshape(2, 1, C)
-    own_wide = jnp.broadcast_to(own, (I, C))
-    factor_weight = jnp.concatenate(
-        [outer_left, outer_right, jnp.zeros((outer_left.shape[0], C - 2 * B), BF16)], axis=1
-    )
+    residues = residue_mask.reshape(2, C)
+    left_weight, right_weight = outer_left.T, outer_right.T
     single = single_state[0]
     single_gain, single_bias = outer_norm_gain[None, :], outer_norm_bias[None, :]
     cube = outer_proj.reshape(B, B * C)
     back_weight = jnp.concatenate([triangle_proj, triangle_gate], axis=2)
     front_weight = jnp.swapaxes(back_weight, 1, 2)
 
-    (every,) = call(
-        head_kernel,
-        [((J, C), BF16)],
-        [DMA((16,)), DMA((16,))],
-        (single, single_gain, single_bias, factor_weight, own_wide),
-        "head",
-        collective=0,
-    )
-    (
-        pair_gradient,
-        front0_sum,
-        front1_sum,
-        out0_sum,
-        out1_sum,
-        small,
-        cube_sum,
-        left_single,
-        right_total,
-    ) = call(
-        trunk_kernel,
+    scale = 1.0 / float(lax.axis_size("dp") * J)
+    pair_gradient, single_gradient, total = call(
+        functools.partial(trunk_kernel, scale),
+        [((I, J, C), BF16), ((I, single.shape[1]), BF16), ((28 * C, C), BF16)],
         [
-            ((I, J, C), BF16),
-            ((C, 5 * C), F32),
-            ((C, 5 * C), F32),
-            ((C, C), F32),
-            ((C, C), F32),
-            ((C, C), F32),
-            ((B * B, C), F32),
-            ((I, C), F32),
-            ((J, C), F32),
-        ],
-        [pltpu.VMEM(BY_PAIR, BF16)] * 5
+            pltpu.VMEM((J, C), BF16),
+            pltpu.VMEM((J, C), F32),
+            pltpu.VMEM((16, I, C), F32),
+            pltpu.VMEM((I, single.shape[1]), F32),
+            pltpu.VMEM((C, 5 * C), F32),
+            pltpu.VMEM((C, 5 * C), F32),
+            pltpu.VMEM((C, C), F32),
+            pltpu.VMEM((C, C), F32),
+        ]
+        + [pltpu.VMEM(BY_PAIR, BF16)] * 5
         + [pltpu.VMEM((6,) + BY_CHANNEL, BF16)] * 2
         + [pltpu.VMEM((6,) + HALF, BF16)]
         + [pltpu.VMEM(shape, BF16) for shape in (HALF, EVERY, HALF, HALF, EVERY, HALF)]
@@ -1150,19 +1143,32 @@
             pltpu.VMEM((9, C, C), F32),
             pltpu.VMEM((9, C, J), F32),
             pltpu.VMEM((C, J), F32),
-            pltpu.VMEM((C, J), F32),
+            pltpu.VMEM((UNROLL, C, J), F32),
+            pltpu.VMEM((2, I, C), F32),
             DMA((12,)),
             DMA((12, 2, Q)),
             DMA((12, 2)),
             DMA((4,)),
             DMA((4, 2, Q, 2)),
+            DMA((4,)),
+            DMA((3, 9)),
+            DMA((3, 8)),
+        ]
+        + [
+            pltpu.VMEM((count, part, C), BF16)
+            for part in (64, 112, 48)
+            for count in (16, 8, 8, 8, 8)
         ],
         (
+            single,
+            single_gain,
+            single_bias,
+            left_weight,
+            right_weight,
             pair_state[0],
             pair_cotangent[0],
-            every,
             cube,
-            mask,
+            residues,
             outer_bias[None, :],
             triangle_norm_gain,
             triangle_norm_bias,
@@ -1173,50 +1179,15 @@
             triangle_out,
         ),
         "trunk",
-        collective=1,
-    )
-    scale = 1.0 / float(lax.axis_size("dp") * J)
-    part = (PART, C)
-    single_gradient, total = call(
-        functools.partial(total_kernel, scale),
-        [((I, single.shape[1]), BF16), ((16,) + part, BF16)],
-        [
-            pltpu.VMEM((16,) + part, BF16),
-            pltpu.VMEM((16, I, C), F32),
-            pltpu.VMEM((8,) + part, BF16),
-            pltpu.VMEM((8,) + part, BF16),
-            pltpu.VMEM((8,) + part, BF16),
-            pltpu.VMEM((8,) + part, BF16),
-            DMA((16,)),
-            DMA((16,)),
-            DMA((2,)),
-        ]
-        + [DMA((8,))] * 8,
-        (
-            right_total,
-            left_single,
-            single,
-            single_gain,
-            single_bias,
-            factor_weight,
-            own_wide,
-            front0_sum,
-            front1_sum,
-            out0_sum,
-            out1_sum,
-            cube_sum,
-            small,
-        ),
-        "total",
-        collective=2,
+        collective=0,
     )
     unpacked = call(
         unpack_kernel,
         [
             ((8, C), F32),
             ((8, C), F32),
-            (outer_left.shape, F32),
-            (outer_right.shape, F32),
+            (left_weight.shape, F32),
+            (right_weight.shape, F32),
             (outer_proj.shape, F32),
             ((1, C), F32),
             ((2, C), F32),
@@ -1228,13 +1199,15 @@
             (triangle_out.shape, F32),
         ],
         [],
-        (total.reshape(16 * PART, C),),
+        (total,),
         "unpack",
     )
     unpacked = list(unpacked)
     unpacked[0] = unpacked[0].reshape(-1)
     unpacked[1] = unpacked[1].reshape(-1)
     unpacked[5] = unpacked[5].reshape(-1)
+    unpacked[2] = unpacked[2].T
+    unpacked[3] = unpacked[3].T
     return (single_gradient[None], pair_gradient[None]) + tuple(unpacked)
 
 

time: 285 us -> 248 us (0.87)
  Pallas kernels: 271 us -> 240 us
  local copies, waits for them, and re-layouts: 10.7 us -> 7.24 us
    pallas_call x4 -> x2, Pallas kernels: 271 us -> 240 us  [call(): pl.pallas_call(kernel, out_shape=[jax.ShapeDtypeStruct(shape, dtype) for...]
    unnamed x23 -> x11, local copies, waits for them, and re-layouts: 8.12 us -> 4.51 us
where the time goes in v3:
time: 248 us
  Pallas kernels  240 us (97%)
  local copies, waits for them, and re-layouts  7.24 us (3%)
    pallas_call x2, Pallas kernels, call(): pl.pallas_call(kernel, out_shape=[jax.ShapeDtypeStruct(shape, dtype) for...  240 us

profile of v3, /device:TPU:1, one launch (start us, length us, event | category | flops | bytes accessed | tf_op | source)
XLA Modules:
  0.0 247.8 jit_solution(8387264593767784512)
XLA Ops:
  0.6 0.0 copy-start.1
  0.7 1.8 reshape.45.cube_ref
  2.5 0.0 copy-done.1
  2.5 0.0 copy-start.2
  2.5 0.8 copy-done.2
  3.3 0.0 copy-start
  3.3 0.9 copy.32.front_ref
  4.2 0.0 copy-done
  4.2 237.5 %trunk.1 = (bf16[16,256,128]{2,1,0:T(8,128)(2,1)}, bf16[16,1024]{1,0:T(8,128)(2,1)}, bf16[3584,128]{1,0:T(8,128)(2,1)}) custom-call(bf16[16,1024]{1,0:T(8,128)(2,1)} %bitcast.23, f32[1,1024]{1,0:T(1,128)} %bitcast.25, f32[1,1024]{1,0:T(1,128)} %bitcast.26, bf16[32,1024]{1,0:T(8,128)(2,1)} %bitcast.21, bf16[32,1024]{1,0:T(8,128)(2,1)} %bitcast.22, ...), custom_call_target="tpu_custom_call" | custom-call | tf_op jit(solution)/shard_map/trunk/pallas_call | solution.py:1069
  241.8 2.4 unpack.1
  244.1 0.0 copy-start.3
  244.1 0.8 copy-done.3
  244.9 0.6 copy.36
  245.5 2.3 copy.37
  (2 shorter events, 0.0 us)
Async XLA Ops:
  0.6 1.8 copy-start.1
  2.5 0.8 copy-start.2
  3.3 0.9 copy-start
  244.1 0.8 copy-start.3

commit v4 on v3

--- a/solution.py
+++ b/solution.py
@@ -15,8 +15,8 @@
 I = 16
 J = 256
 B = 32
-Q = 2
-CQ = 8
+Q = 4
+CQ = 4
 UNROLL = 4
 VMEM_LIMIT = 60 * 2**20
 
@@ -137,9 +137,11 @@
     return jnp.concatenate([left_ref[...], right_ref[...], empty], axis=0)
 
 
-def mixed_rows(own_left, cube_ref, mixed_cells):
+def mixed_rows(own_left, outer_proj_ref, rows, cube_ref, mixed_cells):
+    rows[: B * B, :] = outer_proj_ref[...].astype(F32)
     for b in range(B):
-        mixed_cells[b * I : (b + 1) * I, :] = nn(own_left, cube_ref[:, b * C : (b + 1) * C])
+        cube_ref[b] = rows[pl.ds(b, B, stride=B), :].astype(BF16)
+        mixed_cells[b * I : (b + 1) * I, :] = nn(own_left, cube_ref[b])
 
 
 def back_out(cotangent, product, pair_in, gain, bias, front_ref, out_gain, out_bias, out_ref, sums):
@@ -216,7 +218,11 @@
         return (group // 2) * 4 + self.half * 2 + lax.rem(group, 2)
 
     def peer(self, t):
-        return lax.rem(self.group + t, 8)
+        n = t - 1
+        turn = lax.rem(n, 3)
+        step = (2 * turn + 1 - 3 * (turn // 2)) * (1 - n // 6)
+        core = lax.rem(self.me + n // 3 + n // 6, 2)
+        return lax.rem(self.group // 2 + step, 4) * 2 + core
 
     def greet(self):
         barrier = pltpu.get_barrier_semaphore()
@@ -454,6 +460,9 @@
         total = self.chip_sum[self.chip].astype(F32)
         for t in range(1, 8):
             total += self.chip_parts[t].astype(F32)
+        self.send_dp(total)
+
+    def send_dp(self, total):
         dp = self.place.dp
         self.dp_parts[dp] = total.astype(BF16)
         loop(
@@ -482,12 +491,15 @@
         block = self.block(lax.rem(self.chip + 8 - t, 8))
         return self.place.copy(block, block, self.sem.at[7], self.sem.at[8], self.sibling)
 
-    def to_all(self):
+    def dp_total(self):
         wait_bytes(self.dp_parts.at[1:8], self.sem.at[5])
         total = self.dp_parts[0].astype(F32)
         for n in range(1, 8):
             total += self.dp_parts[n].astype(F32)
-        self.block(self.chip)[...] = (total * self.scale).astype(BF16)
+        return (total * self.scale).astype(BF16)
+
+    def to_all(self):
+        self.block(self.chip)[...] = self.dp_total()
         loop(1, 8, lambda t: self.back_copy(t).start())
         self.pass_copy(0).start()
 
@@ -504,6 +516,43 @@
         wait_bytes(half, self.sem.at[8])
         for n in (2, 4, 6):
             wait_bytes(self.chip_parts.at[1:8], self.sem.at[n])
+
+
+class Direct(Total):
+    def start(self):
+        def send(t):
+            n = lax.rem(self.place.me + t, 16)
+            self.place.copy(
+                self.packed.at[n], self.chip_parts.at[t], self.sem.at[2], self.sem.at[3], n
+            ).start()
+
+        loop(1, 16, send)
+
+    def block(self, me):
+        return self.total.at[rows_of(self.first + me * self.part, self.part)]
+
+    def to_dp(self):
+        wait_bytes(self.chip_parts.at[1:16], self.sem.at[3])
+        total = self.packed[self.place.me].astype(F32)
+        for t in range(1, 16):
+            total += self.chip_parts[t].astype(F32)
+        self.send_dp(total)
+
+    def to_all(self):
+        block = self.block(self.place.me)
+        block[...] = self.dp_total()
+
+        def send(t):
+            self.place.copy(
+                block, block, self.sem.at[6], self.sem.at[7], lax.rem(self.place.me + t, 16)
+            ).start()
+
+        loop(1, 16, send)
+
+    def finish(self):
+        for n in (2, 6, 7):
+            wait_bytes(self.chip_parts.at[1:16], self.sem.at[n])
+        wait_bytes(self.dp_parts.at[1:8], self.sem.at[4])
 
 
 def trunk_kernel(
@@ -515,7 +564,7 @@
     right_weight_ref,
     pair_ref,
     cotangent_ref,
-    cube_ref,
+    outer_proj_ref,
     residue_ref,
     outer_bias_ref,
     norm_gain_ref,
@@ -529,6 +578,7 @@
     single_grad_ref,
     total_ref,
     every_ref,
+    cube_ref,
     right_total_ref,
     right_parts,
     single_standard,
@@ -576,7 +626,7 @@
     me, dp = place.me, place.dp
     own = own_weights(residue_ref, me)
     totals = [
-        Total(
+        (Direct if n == 2 else Total)(
             place,
             scale,
             total_ref,
@@ -607,7 +657,7 @@
     wides[8] = jnp.broadcast_to(outer_bias_ref[...], (C, C)).T
     clear(sums, front0_sum, front1_sum, out0_sum, out1_sum, right_total, outer_cells)
     own_left = every_ref[mine, :][:, :B]
-    mixed_rows(own_left, cube_ref, mixed_cells)
+    mixed_rows(own_left, outer_proj_ref, cells.at[0], cube_ref, mixed_cells)
     wait_bytes(every_ref.at[: 15 * I], few_sem.at[1])
     right_rows = every_ref[...].astype(F32).T[B : 2 * B].astype(BF16)
 
@@ -672,9 +722,10 @@
 
     def forward_right(h):
         send_right0.here(h)
-        order = ((0, 0, 0), (0, 1, 0), (0, 0, 1)) if h == 0 else (
-            (1, 0, 0), (1, 1, 0), (0, 1, 1), (1, 0, 1), (1, 1, 1)
-        )
+        pieces = range(Q)
+        order = [(h, q, 0) for q in pieces] + [(0, q, 1) for q in pieces[h * Q // 2 : (h + 1) * Q // 2]]
+        if h == 1:
+            order += [(1, q, 1) for q in pieces]
         for half, q, r in order:
             if half == h and r == 0:
                 send_right0.arrive(h, q)
@@ -682,11 +733,11 @@
 
     def forward_grad(h):
         send_grad1.here(h)
-        for q in range(Q):
-            send_grad1.arrive(h, q)
-            swaps[2].rows(grad1, h, q, 0)
-        for q in range(Q):
-            swaps[2].rows(grad1, h, q, 1)
+        order = [(q, r) for q in range(Q) for r in range(2)]
+        for q, r in order if h == 0 else sorted(order, key=lambda at: at[1]):
+            if r == 0:
+                send_grad1.arrive(h, q)
+            swaps[2].rows(grad1, h, q, r)
 
     front_first(0)
     front_first(1, lambda: forward_right(0))
@@ -809,29 +860,43 @@
     add_halves(swaps[1], received_sum.at[0], staged.at[1], send_product1, 1)
     forward_grad(0)
     back_second(1)
+
+    def send_right_back(h, q):
+        for r in range(2):
+            if h == 0 or r == 1:
+                swaps[2].arrive(grad1, h, q, r)
+
+        def right_back(c, m):
+            staged[3, c, :, lanes(h)] = nn(left1[c], grad1[c, :, lanes(h)]).astype(BF16)
+
+        over_channels(q, right_back)
+        send_right_grad1.send_piece(h, q)
+
+    def send_left_back(h, q):
+        if h == 0:
+            swaps[2].arrive(grad1, 1, q, 0)
+
+        def left_back(c, m):
+            staged[2, c, :, lanes(h)] = nt(right1[c], grad1[c, lanes(h), :]).astype(BF16)
+
+        over_channels(q, left_back)
+        send_left_grad1.send_piece(h, q)
+
+    for q in range(Q // 2):
+        send_right_back(0, q)
     forward_grad(1)
-    for h in range(2):
-        for q in range(Q):
-            for r in range(2):
-                if h == 0 or r == 1:
-                    swaps[2].arrive(grad1, h, q, r)
-
-            def right_back(c, m):
-                staged[3, c, :, lanes(h)] = nn(left1[c], grad1[c, :, lanes(h)]).astype(BF16)
-
-            over_channels(q, right_back)
-            send_right_grad1.send_piece(h, q)
-        send_right_grad1.local(h)
-        for q in range(Q):
-            if h == 0:
-                swaps[2].arrive(grad1, 1, q, 0)
-
-            def left_back(c, m):
-                staged[2, c, :, lanes(h)] = nt(right1[c], grad1[c, lanes(h), :]).astype(BF16)
-
-            over_channels(q, left_back)
-            send_left_grad1.send_piece(h, q)
-        send_left_grad1.local(h)
+    for q in range(Q // 2, Q):
+        send_right_back(0, q)
+    send_right_grad1.local(0)
+    for q in range(Q):
+        send_left_back(0, q)
+    send_left_grad1.local(0)
+    for q in range(Q):
+        send_right_back(1, q)
+    send_right_grad1.local(1)
+    for q in range(Q):
+        send_left_back(1, q)
+    send_left_grad1.local(1)
 
     def back_middle(h, hook=None):
         send_left_grad1.arrive_half(h)
@@ -976,7 +1041,7 @@
     for b in range(B):
         rows = outer_cells[b * I : (b + 1) * I, :].astype(BF16)
         totals[1].put(5 * C + b * B, tn(own_left, rows))
-        left_single += nt(rows, cube_ref[:, b * C : (b + 1) * C])
+        left_single += nt(rows, cube_ref[b])
     totals[1].put(13 * C, columns(*[sums.at[n] for n in range(9)]))
     totals[1].start()
 
@@ -1004,13 +1069,11 @@
         single_grad * single_gain_ref[...], standard, single_inverse, axis=1
     ).astype(BF16)
     totals[0].to_sibling()
-    totals[2].to_chips()
     totals[1].to_dp()
     totals[2].to_dp()
     totals[1].to_all()
     totals[2].to_all()
     totals[1].to_sibling()
-    totals[2].to_sibling()
     for batch in totals:
         batch.finish()
     wait_bytes(every_ref.at[: 15 * I], few_sem.at[0])
@@ -1111,7 +1174,6 @@
     left_weight, right_weight = outer_left.T, outer_right.T
     single = single_state[0]
     single_gain, single_bias = outer_norm_gain[None, :], outer_norm_bias[None, :]
-    cube = outer_proj.reshape(B, B * C)
     back_weight = jnp.concatenate([triangle_proj, triangle_gate], axis=2)
     front_weight = jnp.swapaxes(back_weight, 1, 2)
 
@@ -1121,6 +1183,7 @@
         [((I, J, C), BF16), ((I, single.shape[1]), BF16), ((28 * C, C), BF16)],
         [
             pltpu.VMEM((J, C), BF16),
+            pltpu.VMEM((B, B, C), BF16),
             pltpu.VMEM((J, C), F32),
             pltpu.VMEM((16, I, C), F32),
             pltpu.VMEM((I, single.shape[1]), F32),
@@ -1156,8 +1219,8 @@
         ]
         + [
             pltpu.VMEM((count, part, C), BF16)
-            for part in (64, 112, 48)
-            for count in (16, 8, 8, 8, 8)
+            for part, parts in ((64, 8), (112, 8), (48, 16))
+            for count in (16, 8, 8, parts, 8)
         ],
         (
             single,
@@ -1167,7 +1230,7 @@
             right_weight,
             pair_state[0],
             pair_cotangent[0],
-            cube,
+            outer_proj,
             residues,
             outer_bias[None, :],
             triangle_norm_gain,

time: 248 us -> 244 us (0.984)
  Pallas kernels: 240 us -> 237 us
    pallas_call x2, Pallas kernels: 240 us -> 237 us  [call(): pl.pallas_call(kernel, out_shape=[jax.ShapeDtypeStruct(shape, dtype) for...]
where the time goes in v4:
time: 244 us
  Pallas kernels  237 us (97%)
  local copies, waits for them, and re-layouts  5.6 us (2%)
    pallas_call x2, Pallas kernels, call(): pl.pallas_call(kernel, out_shape=[jax.ShapeDtypeStruct(shape, dtype) for...  237 us

profile of v4, /device:TPU:1, one launch (start us, length us, event | category | flops | bytes accessed | tf_op | source)
XLA Modules:
  0.0 243.6 jit_solution(4288020196388463376)
XLA Ops:
  0.6 0.0 copy-start.1
  0.7 1.0 constant_dynamic-update-slice_fusion.1
  1.7 0.0 copy-done.1
  1.7 0.0 copy-start
  1.7 0.9 copy.32.front_ref
  2.6 0.0 copy-done
  2.6 235.0 %trunk.1 = (bf16[16,256,128]{2,1,0:T(8,128)(2,1)}, bf16[16,1024]{1,0:T(8,128)(2,1)}, bf16[3584,128]{1,0:T(8,128)(2,1)}) custom-call(bf16[16,1024]{1,0:T(8,128)(2,1)} %bitcast.23, f32[1,1024]{1,0:T(1,128)} %bitcast.25, f32[1,1024]{1,0:T(1,128)} %bitcast.26, bf16[32,1024]{1,0:T(8,128)(2,1)} %bitcast.21, bf16[32,1024]{1,0:T(8,128)(2,1)} %bitcast.22, ...), custom_call_target="tpu_custom_call" | custom-call | tf_op jit(solution)/shard_map/trunk/pallas_call | solution.py:1132
  237.6 2.4 unpack.1
  239.9 0.0 copy-start.2
  239.9 0.8 copy-done.2
  240.7 0.6 copy.36
  241.3 2.3 copy.37
  (1 shorter events, 0.0 us)
Async XLA Ops:
  0.6 1.0 copy-start.1
  1.7 0.9 copy-start
  239.9 0.8 copy-start.2

commit v5 on v4

--- a/solution.py
+++ b/solution.py
@@ -124,12 +124,12 @@
 def over_pairs(body, hook=None, at=4):
     def step(n, _):
         if hook is not None:
-            pl.when(2 * n == at)(hook)
-        body(2 * n)
-        body(2 * n + 1)
+            pl.when(4 * n == at)(hook)
+        for m in range(4):
+            body(4 * n + m)
         return 0
 
-    lax.fori_loop(0, I // 4, step, 0)
+    lax.fori_loop(0, I // 8, step, 0)
 
 
 def factor_weights(left_ref, right_ref):
@@ -788,9 +788,9 @@
         for n, way in ((0, send_left1), (1, send_right1)):
             cells_out(cells.at[n], sends.at[2 + n], h)
             way.local(h)
-        for q in range(Q):
-            send_left1.send_piece(h, q)
-            send_right1.send_piece(h, q)
+        for way in (send_left1, send_right1):
+            for q in range(Q):
+                way.send_piece(h, q)
 
     middle(0)
     middle(1)
@@ -808,11 +808,13 @@
         for way in (send_left1, send_right1):
             way.here(n)
         for q in range(Q):
-            for way in (send_left1, send_right1):
-                way.arrive(n, q)
+            send_left1.arrive(n, q)
+            if n == 0:
+                send_right1.arrive(0, q)
             incoming_sums(q, 0, n)
-    for r in range(2):
-        for q in range(Q):
+    for q in range(Q):
+        send_right1.arrive(1, q)
+        for r in range(2):
             incoming_sums(q, 1, r)
 
     def add_halves(swap, received, target, way, h):
@@ -1088,6 +1090,10 @@
 
 def unpack_kernel(
     total_ref,
+    single_from,
+    pair_from,
+    single_to,
+    pair_to,
     outer_gain_ref,
     outer_bias_ref,
     outer_left_ref,
@@ -1102,6 +1108,8 @@
     out_bias_ref,
     out_ref,
 ):
+    pair_to[...] = pair_from[...]
+    single_to[...] = single_from[...]
     for t in range(2):
         front = 8 - 8 * t
         for n in range(4):
@@ -1128,7 +1136,7 @@
     outer_bias_ref[...] = rows[8:16]
 
 
-def call(kernel, outs, scratch, args, name, collective=None, flops=0):
+def call(kernel, outs, scratch, args, name, collective=None):
     return pl.pallas_call(
         kernel,
         out_shape=[jax.ShapeDtypeStruct(shape, dtype) for shape, dtype in outs],
@@ -1247,6 +1255,8 @@
     unpacked = call(
         unpack_kernel,
         [
+            (single_gradient.shape, BF16),
+            (pair_gradient.shape, BF16),
             ((8, C), F32),
             ((8, C), F32),
             (left_weight.shape, F32),
@@ -1262,10 +1272,10 @@
             (triangle_out.shape, F32),
         ],
         [],
-        (total,),
+        (total, single_gradient, pair_gradient),
         "unpack",
     )
-    unpacked = list(unpacked)
+    single_gradient, pair_gradient, *unpacked = unpacked
     unpacked[0] = unpacked[0].reshape(-1)
     unpacked[1] = unpacked[1].reshape(-1)
     unpacked[5] = unpacked[5].reshape(-1)

time: 244 us -> 235 us (0.963)
  Pallas kernels: 237 us -> 233 us
  local copies, waits for them, and re-layouts: 5.6 us -> 1.93 us
    pallas_call x2, Pallas kernels: 237 us -> 233 us  [call(): pl.pallas_call(kernel, out_shape=[jax.ShapeDtypeStruct(shape, dtype) for...]
    unnamed x9 -> x5, local copies, waits for them, and re-layouts: 4.68 us -> 1.01 us
where the time goes in v5:
time: 235 us
  Pallas kernels  233 us (99%)
    pallas_call x2, Pallas kernels, call(): pl.pallas_call(kernel, out_shape=[jax.ShapeDtypeStruct(shape, dtype) for...  233 us

profile of v5, /device:TPU:1, one launch (start us, length us, event | category | flops | bytes accessed | tf_op | source)
XLA Modules:
  0.0 235.3 jit_solution(13567544817542409156)
XLA Ops:
  0.6 0.0 copy-start.1
  0.7 1.0 constant_dynamic-update-slice_fusion.1
  1.7 0.0 copy-done.1
  1.7 0.0 copy-start
  1.7 0.9 copy.32.front_ref
  2.6 0.0 copy-done
  2.6 229.5 %trunk.1 = (bf16[16,256,128]{2,1,0:T(8,128)(2,1)}, bf16[16,1024]{1,0:T(8,128)(2,1)}, bf16[3584,128]{1,0:T(8,128)(2,1)}) custom-call(bf16[16,1024]{1,0:T(8,128)(2,1)} %bitcast.22, f32[1,1024]{1,0:T(1,128)} %bitcast.23, f32[1,1024]{1,0:T(1,128)} %bitcast.24, bf16[32,1024]{1,0:T(8,128)(2,1)} %bitcast.20, bf16[32,1024]{1,0:T(8,128)(2,1)} %bitcast.21, ...), custom_call_target="tpu_custom_call" | custom-call | tf_op jit(solution)/shard_map/trunk/pallas_call | solution.py:1140
  232.1 3.1 %unpack.1 = (bf16[16,1024]{1,0:T(8,128)(2,1)}, bf16[16,256,128]{2,1,0:T(8,128)(2,1)}, f32[8,128]{1,0:T(8,128)}, f32[8,128]{1,0:T(8,128)}, f32[32,1024]{1,0:T(8,1...) custom-call(bf16[3584,128]{1,0:T(8,128)(2,1)} %get-tuple-element.33., ...), custom_call_target="tpu_custom_call" | custom-call | tf_op jit(solution)/shard_map/unpack/pallas_call | solution.py:1140
  (1 shorter events, 0.0 us)
Async XLA Ops:
  0.6 1.0 copy-start.1
  1.7 0.9 copy-start
